TPU v7x, 32 devices: a whole 2x2x4 slice. The times are simulated.
32 devices in a mesh: dp: 8 (over z, core), ctx: 4 (over y, x).
Axes of the slice: x: 2, y: 2, z: 4, core: 2. Of those that a mesh axis runs over, the one named last changes fastest.
Arguments:
- inputs: bfloat16 [8, 4, 256, 2048], P('dp', 'ctx'), may hold values from -6 to 6
- positions: int32 [8, 4, 256], P('dp', 'ctx'), may hold values from 0 to 3071, as said below
- block_order: int32 [4, 2], replicated, may hold values from 0 to 7, as said below
- norm_attn: bfloat16 [2048], P(('dp', 'ctx')), may hold values from 0.099609375 to 1.8984375
- w_query: bfloat16 [2048, 2048], P(('dp', 'ctx')), may hold values from -0.125 to 0.125
- w_key: bfloat16 [2048, 256], P(('dp', 'ctx')), may hold values from -0.125 to 0.125
- w_value: bfloat16 [2048, 256], P(('dp', 'ctx')), may hold values from -0.125 to 0.125
- w_out: bfloat16 [2048, 2048], P(('dp', 'ctx')), may hold values from -1 to 1
- norm_mlp: bfloat16 [2048], P(('dp', 'ctx')), may hold values from 0.099609375 to 1.8984375
- w_gate: bfloat16 [2048, 5632], P(('dp', 'ctx')), may hold values from -0.125 to 0.125
- w_up: bfloat16 [2048, 5632], P(('dp', 'ctx')), may hold values from -0.125 to 0.125
- w_down: bfloat16 [5632, 2048], P(('dp', 'ctx')), may hold values from -0.078125 to 0.078125
- cotangent: bfloat16 [8, 4, 256, 2048], P('dp', 'ctx'), may hold values from -6 to 6
Outputs:
- outputs: bfloat16 [8, 4, 256, 2048], P('dp', 'ctx')
- grad_inputs: float32 [8, 4, 256, 2048], P('dp', 'ctx')
- grad_norm_attn: float32 [2048], P(('dp', 'ctx'))
- grad_w_query: float32 [2048, 2048], P(('dp', 'ctx'))
- grad_w_key: float32 [2048, 256], P(('dp', 'ctx'))
- grad_w_value: float32 [2048, 256], P(('dp', 'ctx'))
- grad_w_out: float32 [2048, 2048], P(('dp', 'ctx'))
- grad_norm_mlp: float32 [2048], P(('dp', 'ctx'))
- grad_w_gate: float32 [2048, 5632], P(('dp', 'ctx'))
- grad_w_up: float32 [2048, 5632], P(('dp', 'ctx'))
- grad_w_down: float32 [5632, 2048], P(('dp', 'ctx'))
Inputs may be any that keep to these rules, and one draw needn't show every extreme that they name: `block_order`: each row of the table is one context rank's two logical blocks of 128 tokens, in the order its rows hold them; every block number appears exactly once. Within a sequence the positions rise strictly along the logical token order; its logical first token has position 0 and its last 3071.
All inputs are finite; a program needn't handle non-finite values.
Results may differ from a plain program's by a relative error of at most 0.029.
Values may be sent and summed in bfloat16 or wider, within the bound.
No kernel may reach another device: no remote copies, remote signals or barrier semaphores. Data moves between devices by JAX's collectives and lax.ppermute only.
A program may use at most 384 MiB of HBM per device.

v0:
```python
import jax
import jax.numpy as jnp
from jax import lax
from jax.sharding import PartitionSpec as P

HEADS = 32
KV_HEADS = 4
HEAD_DIM = 64


NORM_EPS = 1e-05
ROPE_BASE = 10000.0
MASKED_SCORE = -1e30


def passed_along(block, axis, distance):
    devices = range(lax.axis_size(axis))
    route = [((i - distance) % len(devices), i) for i in devices]
    return lax.ppermute(block, axis, route)


def multiply(left, right):
    return jnp.dot(left, right, preferred_element_type=jnp.float32)


def against(left, right):
    return lax.dot_general(
        left, right, (((1,), (1,)), ((), ())), preferred_element_type=jnp.float32
    )


def outer_sum(left, right):
    return lax.dot_general(
        left, right, (((0,), (0,)), ((), ())), preferred_element_type=jnp.float32
    )


def rotate(values, angles):
    cosine = jnp.cos(angles)
    sine = jnp.sin(angles)
    cosine = jnp.concatenate([cosine, cosine], -1)[:, None, :]
    sine = jnp.concatenate([sine, sine], -1)[:, None, :]
    half_dim = values.shape[-1] // 2
    turned = jnp.concatenate([-values[..., half_dim:], values[..., :half_dim]], -1)
    return values * cosine + turned * sine


def norm_scale(values):
    return lax.rsqrt(jnp.mean(values * values, -1, keepdims=True) + NORM_EPS)


def norm_back(grad_hidden, normed, scale_rows, gain):
    gain_grad = jnp.sum(grad_hidden * normed, 0)
    scaled = grad_hidden * gain
    return (
        gain_grad,
        scale_rows * (scaled - normed * jnp.mean(scaled * normed, -1, keepdims=True)),
    )


def logical_rows(order, first_row, row_count, block_rows):
    global_rows = first_row + jnp.arange(row_count, dtype=jnp.int32)
    flat_order = order.reshape(-1)
    slots = global_rows // block_rows
    matches = slots[:, None] == jnp.arange(flat_order.shape[0], dtype=jnp.int32)[None, :]
    picked = jnp.sum(jnp.where(matches, flat_order[None, :], 0), 1)
    return picked * block_rows + global_rows % block_rows


def attend_block(running, queries, key_rows, value_rows, query_index, key_index):
    maxima, totals, mixture = running
    kv_heads = queries.shape[1]
    head_dim = queries.shape[3]
    key_heads = key_rows.reshape(key_rows.shape[0], kv_heads, head_dim)
    value_heads = value_rows.reshape(value_rows.shape[0], kv_heads, head_dim)
    scores = jnp.einsum(
        "qgjd,kgd->gjqk", queries, key_heads, preferred_element_type=jnp.float32
    ) * head_dim ** (-0.5)
    visible = key_index[None, :] <= query_index[:, None]
    scores = jnp.where(visible, scores, MASKED_SCORE)
    new_peak = jnp.maximum(maxima, jnp.max(scores, -1))
    weights = jnp.where(visible, jnp.exp(scores - new_peak[..., None]), 0.0)
    factor = jnp.exp(maxima - new_peak)
    totals = totals * factor + jnp.sum(weights, -1)
    mixture = mixture * factor[..., None] + jnp.einsum(
        "gjqk,kgd->gjqd",
        weights.astype(jnp.bfloat16),
        value_heads,
        preferred_element_type=jnp.float32,
    )
    return (new_peak, totals, mixture)


def attend_back(
    queries, key_rows, value_rows, grad_heads, log_total, delta_rows, query_index, key_index
):
    kv_heads = queries.shape[1]
    head_dim = queries.shape[3]
    key_count = key_rows.shape[0]
    key_heads = key_rows.reshape(key_count, kv_heads, head_dim)
    value_heads = value_rows.reshape(key_count, kv_heads, head_dim)
    score_scale = head_dim ** (-0.5)
    scores = (
        jnp.einsum("qgjd,kgd->gjqk", queries, key_heads, preferred_element_type=jnp.float32)
        * score_scale
    )
    visible = key_index[None, :] <= query_index[:, None]
    probabilities = jnp.where(visible, jnp.exp(scores - log_total[..., None]), 0.0)
    grad_value = jnp.einsum(
        "gjqk,gjqd->kgd",
        probabilities.astype(jnp.bfloat16),
        grad_heads,
        preferred_element_type=jnp.float32,
    )
    grad_probs = jnp.einsum(
        "gjqd,kgd->gjqk", grad_heads, value_heads, preferred_element_type=jnp.float32
    )
    grad_scores = (probabilities * (grad_probs - delta_rows[..., None])).astype(jnp.bfloat16)
    grad_query = (
        jnp.einsum("gjqk,kgd->gjqd", grad_scores, key_heads, preferred_element_type=jnp.float32)
        * score_scale
    )
    grad_key = (
        jnp.einsum("gjqk,qgjd->kgd", grad_scores, queries, preferred_element_type=jnp.float32)
        * score_scale
    )
    return (grad_query, grad_key.reshape(key_count, -1), grad_value.reshape(key_count, -1))


def local(
    inputs,
    positions,
    block_order,
    norm_attn,
    w_query,
    w_key,
    w_value,
    w_out,
    norm_mlp,
    w_gate,
    w_up,
    w_down,
    cotangent,
):
    row_count = inputs.shape[2]
    model_width = inputs.shape[3]
    block_rows = row_count // 2
    ctx_size = lax.axis_size("ctx")
    ctx_rank = lax.axis_index("ctx")
    head_dim = HEAD_DIM
    kv_heads = KV_HEADS
    heads = HEADS
    group_size = heads // kv_heads
    x_rows = inputs.reshape(row_count, model_width).astype(jnp.float32)
    gain_attn, full_query, full_key, full_value, full_out = (
        lax.all_gather(norm_attn, ("dp", "ctx"), axis=0, tiled=True),
        lax.all_gather(w_query, ("dp", "ctx"), axis=0, tiled=True),
        lax.all_gather(w_key, ("dp", "ctx"), axis=0, tiled=True),
        lax.all_gather(w_value, ("dp", "ctx"), axis=0, tiled=True),
        lax.all_gather(w_out, ("dp", "ctx"), axis=0, tiled=True),
    )
    frequency = ROPE_BASE ** (-jnp.arange(head_dim // 2, dtype=jnp.float32) * 2.0 / head_dim)
    angles = positions.reshape(row_count).astype(jnp.float32)[:, None] * frequency[None, :]
    my_index = logical_rows(block_order, ctx_rank * row_count, row_count, block_rows)
    scale_attn = norm_scale(x_rows)
    normed_attn = x_rows * scale_attn
    hidden_attn = (normed_attn * gain_attn.astype(jnp.float32)).astype(jnp.bfloat16)
    query_full = multiply(hidden_attn, full_query).reshape(row_count, heads, head_dim)
    queries = (
        rotate(query_full, angles)
        .astype(jnp.bfloat16)
        .reshape(row_count, kv_heads, group_size, head_dim)
    )
    key_full = multiply(hidden_attn, full_key).reshape(row_count, kv_heads, head_dim)
    key_rows = rotate(key_full, angles).astype(jnp.bfloat16).reshape(row_count, kv_heads * head_dim)
    value_rows = multiply(hidden_attn, full_value).astype(jnp.bfloat16)
    start_state = (
        jnp.full((kv_heads, group_size, row_count), MASKED_SCORE, jnp.float32),
        jnp.zeros((kv_heads, group_size, row_count), jnp.float32),
        jnp.zeros((kv_heads, group_size, row_count, head_dim), jnp.float32),
    )

    def forward_turn(cycle_step, carried):
        running, moving_keys, moving_values = carried
        source = (ctx_rank - cycle_step) % ctx_size
        key_index = logical_rows(block_order, source * row_count, row_count, block_rows)
        running = attend_block(running, queries, moving_keys, moving_values, my_index, key_index)
        moving_keys, moving_values = passed_along((moving_keys, moving_values), "ctx", 1)
        return (running, moving_keys, moving_values)

    running, last_keys, last_values = lax.fori_loop(
        0, ctx_size - 1, forward_turn, (start_state, key_rows, value_rows)
    )
    last_source = (ctx_rank + 1) % ctx_size
    running = attend_block(
        running,
        queries,
        last_keys,
        last_values,
        my_index,
        logical_rows(block_order, last_source * row_count, row_count, block_rows),
    )
    maxima, totals, mixture = running
    attended = mixture / totals[..., None]
    log_total = maxima + jnp.log(totals)
    attn_low = (
        attended.transpose(2, 0, 1, 3).reshape(row_count, heads * head_dim).astype(jnp.bfloat16)
    )
    middle = x_rows + multiply(attn_low, full_out)
    gain_mlp, full_gate, full_up, full_down = (
        lax.all_gather(norm_mlp, ("dp", "ctx"), axis=0, tiled=True),
        lax.all_gather(w_gate, ("dp", "ctx"), axis=0, tiled=True),
        lax.all_gather(w_up, ("dp", "ctx"), axis=0, tiled=True),
        lax.all_gather(w_down, ("dp", "ctx"), axis=0, tiled=True),
    )
    scale_mlp = norm_scale(middle)
    normed_mlp = middle * scale_mlp
    hidden_mlp = (normed_mlp * gain_mlp.astype(jnp.float32)).astype(jnp.bfloat16)
    gate_rows = multiply(hidden_mlp, full_gate)
    up_rows = multiply(hidden_mlp, full_up)
    sigmoid_gate = jax.nn.sigmoid(gate_rows)
    swished = gate_rows * sigmoid_gate
    activated = (swished * up_rows).astype(jnp.bfloat16)
    result = middle + multiply(activated, full_down)
    outputs = result.astype(jnp.bfloat16).reshape(inputs.shape)
    grad_top = cotangent.reshape(row_count, model_width)
    grad_activated = against(grad_top, full_down)
    grad_down = outer_sum(activated, grad_top)
    grad_gate = (
        grad_activated * up_rows * sigmoid_gate * (1.0 + gate_rows * (1.0 - sigmoid_gate))
    ).astype(jnp.bfloat16)
    grad_up = (grad_activated * swished).astype(jnp.bfloat16)
    grad_gate_w = outer_sum(hidden_mlp, grad_gate)
    grad_up_w = outer_sum(hidden_mlp, grad_up)
    grad_hidden_mlp = against(grad_gate, full_gate) + against(grad_up, full_up)
    gain_mlp_grad, grad_mid_norm = norm_back(
        grad_hidden_mlp, normed_mlp, scale_mlp, gain_mlp.astype(jnp.float32)
    )
    grad_middle = grad_top.astype(jnp.float32) + grad_mid_norm
    out_gain_mlp, out_gate, out_up, out_down = (
        lax.psum_scatter(gain_mlp_grad, ("dp", "ctx"), scatter_dimension=0, tiled=True),
        lax.psum_scatter(grad_gate_w, ("dp", "ctx"), scatter_dimension=0, tiled=True),
        lax.psum_scatter(grad_up_w, ("dp", "ctx"), scatter_dimension=0, tiled=True),
        lax.psum_scatter(grad_down, ("dp", "ctx"), scatter_dimension=0, tiled=True),
    )
    grad_branch = grad_middle.astype(jnp.bfloat16)
    grad_out_w = outer_sum(attn_low, grad_branch)
    grad_attn = against(grad_branch, full_out).astype(jnp.bfloat16)
    grad_heads = grad_attn.reshape(row_count, kv_heads, group_size, head_dim).transpose(1, 2, 0, 3)
    delta_rows = jnp.sum(grad_heads.astype(jnp.float32) * attended, -1)
    zero_query = jnp.zeros((kv_heads, group_size, row_count, head_dim), jnp.float32)
    zero_kv = jnp.zeros((row_count, kv_heads * head_dim), jnp.float32)

    def backward_turn(cycle_step, carried):
        grad_query, moving_keys, moving_values, moving_gkey, moving_gvalue = carried
        source = (ctx_rank - cycle_step) % ctx_size
        key_index = logical_rows(block_order, source * row_count, row_count, block_rows)
        part_query, part_key, part_value = attend_back(
            queries,
            moving_keys,
            moving_values,
            grad_heads,
            log_total,
            delta_rows,
            my_index,
            key_index,
        )
        moving_keys, moving_values = passed_along((moving_keys, moving_values), "ctx", 1)
        moving_gkey, moving_gvalue = (
            passed_along((moving_gkey + part_key).astype(jnp.bfloat16), "ctx", 1).astype(
                jnp.float32
            ),
            passed_along((moving_gvalue + part_value).astype(jnp.bfloat16), "ctx", 1).astype(
                jnp.float32
            ),
        )
        return (grad_query + part_query, moving_keys, moving_values, moving_gkey, moving_gvalue)

    grad_query, last_keys, last_values, held_gkey, held_gvalue = lax.fori_loop(
        0, ctx_size - 1, backward_turn, (zero_query, key_rows, value_rows, zero_kv, zero_kv)
    )
    last_source = (ctx_rank + 1) % ctx_size
    part_query, part_key, part_value = attend_back(
        queries,
        last_keys,
        last_values,
        grad_heads,
        log_total,
        delta_rows,
        my_index,
        logical_rows(block_order, last_source * row_count, row_count, block_rows),
    )
    grad_query = grad_query + part_query
    grad_key_rows, grad_value_rows = (
        passed_along((held_gkey + part_key).astype(jnp.bfloat16), "ctx", 1).astype(jnp.float32),
        passed_along((held_gvalue + part_value).astype(jnp.bfloat16), "ctx", 1).astype(jnp.float32),
    )
    query_heads_grad = grad_query.transpose(2, 0, 1, 3).reshape(row_count, heads, head_dim)
    grad_query_low = (
        rotate(query_heads_grad, -angles).astype(jnp.bfloat16).reshape(row_count, heads * head_dim)
    )
    grad_key_low = (
        rotate(grad_key_rows.reshape(row_count, kv_heads, head_dim), -angles)
        .astype(jnp.bfloat16)
        .reshape(row_count, kv_heads * head_dim)
    )
    grad_value_low = grad_value_rows.astype(jnp.bfloat16)
    grad_query_w = outer_sum(hidden_attn, grad_query_low)
    grad_key_w = outer_sum(hidden_attn, grad_key_low)
    grad_value_w = outer_sum(hidden_attn, grad_value_low)
    grad_hidden_attn = (
        against(grad_query_low, full_query)
        + against(grad_key_low, full_key)
        + against(grad_value_low, full_value)
    )
    gain_attn_grad, grad_in_norm = norm_back(
        grad_hidden_attn, normed_attn, scale_attn, gain_attn.astype(jnp.float32)
    )
    grad_inputs = (grad_middle + grad_in_norm).reshape(inputs.shape)
    out_gain_attn, out_query, out_key, out_value, out_out = (
        lax.psum_scatter(gain_attn_grad, ("dp", "ctx"), scatter_dimension=0, tiled=True),
        lax.psum_scatter(grad_query_w, ("dp", "ctx"), scatter_dimension=0, tiled=True),
        lax.psum_scatter(grad_key_w, ("dp", "ctx"), scatter_dimension=0, tiled=True),
        lax.psum_scatter(grad_value_w, ("dp", "ctx"), scatter_dimension=0, tiled=True),
        lax.psum_scatter(grad_out_w, ("dp", "ctx"), scatter_dimension=0, tiled=True),
    )
    return (
        outputs,
        grad_inputs,
        out_gain_attn,
        out_query,
        out_key,
        out_value,
        out_out,
        out_gain_mlp,
        out_gate,
        out_up,
        out_down,
    )


def solution(mesh):
    placed = (
        P("dp", "ctx", None, None),
        P("dp", "ctx", None),
        P(),
        P(("dp", "ctx")),
        P(("dp", "ctx"), None),
        P(("dp", "ctx"), None),
        P(("dp", "ctx"), None),
        P(("dp", "ctx"), None),
        P(("dp", "ctx")),
        P(("dp", "ctx"), None),
        P(("dp", "ctx"), None),
        P(("dp", "ctx"), None),
        P("dp", "ctx", None, None),
    )
    return jax.shard_map(
        local,
        mesh=mesh,
        in_specs=placed,
        out_specs=(
            P("dp", "ctx", None, None),
            P("dp", "ctx", None, None),
            P(("dp", "ctx")),
            P(("dp", "ctx"), None),
            P(("dp", "ctx"), None),
            P(("dp", "ctx"), None),
            P(("dp", "ctx"), None),
            P(("dp", "ctx")),
            P(("dp", "ctx"), None),
            P(("dp", "ctx"), None),
            P(("dp", "ctx"), None),
        ),
        check_vma=False,
    )
```

profile of v0, /device:TPU:0, one launch (start us, length us, event | category | flops | bytes accessed | tf_op | source)
XLA Modules:
  0.0 4788.5 jit_solution(5000349643607924360)
XLA Ops:
  15.2 42.1 all-reduce.5
  70.3 53.1 %all-gather.10.cloned.1.call-done = bf16[2048,256]{1,0:T(8,128)(2,1)} async-done(((bf16[64,256]{1,0:T(8,128)(2,1)}), bf16[2048,256]{1,0:T(8,128)(2,1)}) %all-gather.10.cloned.1.call-update) | async-done | bytes 1048592 | tf_op jit(solution)/shard_map/all_gather | solution.py:159
  125.2 77.6 %all-gather.12.cloned.1.call-done = bf16[2048,2048]{1,0:T(8,128)(2,1)} async-done(((bf16[64,2048]{1,0:T(8,128)(2,1)}), bf16[2048,2048]{1,0:T(8,128)(2,1)}) %all-gather.12.cloned.1.call-update) | async-done | bytes 8388624 | tf_op jit(solution)/shard_map/all_gather | solution.py:157
  222.2 34.2 while.52
  264.0 23.1 all-gather.14.cloned.1.call-done
  294.5 138.6 %all-gather.16.cloned.1.call-done = bf16[2048,5632]{1,0:T(8,128)(2,1)} async-done(((bf16[64,5632]{1,0:T(8,128)(2,1)}), bf16[2048,5632]{1,0:T(8,128)(2,1)}) %all-gather.16.cloned.1.call-update) | async-done | bytes 23068688 | tf_op jit(solution)/shard_map/all_gather | solution.py:212
  433.1 13.2 fusion.108
  446.3 132.4 %all-gather.18.cloned.1.call-done = bf16[2048,5632]{1,0:T(8,128)(2,1)} async-done(((bf16[64,5632]{1,0:T(8,128)(2,1)}), bf16[2048,5632]{1,0:T(8,128)(2,1)}) %all-gather.18.cloned.1.call-update) | async-done | bytes 23068688 | tf_op jit(solution)/shard_map/all_gather | solution.py:213
  578.7 13.3 fusion.109
  592.0 132.4 %all-gather.20.cloned.1.call-done = bf16[5632,2048]{1,0:T(8,128)(2,1)} async-done(((bf16[176,2048]{1,0:T(8,128)(2,1)}), bf16[5632,2048]{1,0:T(8,128)(2,1)}) %all-gather.20.cloned.1.call-update) | async-done | bytes 23068688 | tf_op jit(solution)/shard_map/all_gather | solution.py:214
  724.4 26.1 multiply_convert_fusion.2
  750.5 12.7 fusion.110
  763.2 13.9 multiply_reduce_fusion
  792.9 65.0 %while.53 = (s32[]{:T(128)}, f32[4,8,256,64]{2,3,1,0:T(8,128)S(1)}, bf16[256,256]{0,1:T(8,128)(2,1)S(1)}, bf16[256,256]{0,1:T(8,128)(2,1)S(1)}, f32[256,256]{0,1...) while((s32[]{:T(128)}, f32[4,8,256,64]{2,3,1,0:T(8,128)S(1)}, ...), condition=%wide.wide.region_15.16_spmd.clone, body=%wide.wide.region_13.15_spmd.clone.sunk | while | flops 1365390592 | bytes 58629772 | solution.py:279
  913.6 19.7 fusion.113
  933.3 19.7 fusion.114
  954.3 19.7 fusion.69
  999.4 39.3 all-reduce.4
  1043.4 99.9 %reduce-scatter.12.cloned.1.call-done = f32[64,256]{1,0:T(8,128)} async-done(((f32[2048,256]{1,0:T(8,128)}), f32[64,256]{1,0:T(8,128)}) %reduce-scatter.12.cloned.1.call-update) | async-done | bytes 65552 | tf_op jit(solution)/shard_map/reduce_scatter | solution.py:324
  1143.3 356.5 %reduce-scatter.8.cloned.1.call-done = f32[64,2048]{1,0:T(8,128)} async-done(((f32[2048,2048]{1,0:T(8,128)}), f32[64,2048]{1,0:T(8,128)}) %reduce-scatter.8.cloned.1.call-update) | async-done | bytes 524304 | tf_op jit(solution)/shard_map/reduce_scatter | solution.py:322
  1499.8 362.0 %reduce-scatter.14.cloned.1.call-done = f32[64,2048]{1,0:T(8,128)} async-done(((f32[2048,2048]{1,0:T(8,128)}), f32[64,2048]{1,0:T(8,128)}) %reduce-scatter.14.cloned.1.call-update) | async-done | bytes 524304 | tf_op jit(solution)/shard_map/reduce_scatter | solution.py:325
  1861.8 972.8 %reduce-scatter.16.cloned.1.call-done = f32[64,5632]{1,0:T(8,128)} async-done(((f32[2048,5632]{1,0:T(8,128)}), f32[64,5632]{1,0:T(8,128)}) %reduce-scatter.16.cloned.1.call-update) | async-done | bytes 1441808 | tf_op jit(solution)/shard_map/reduce_scatter | solution.py:242
  2834.6 973.7 %reduce-scatter.18.cloned.1.call-done = f32[64,5632]{1,0:T(8,128)} async-done(((f32[2048,5632]{1,0:T(8,128)}), f32[64,5632]{1,0:T(8,128)}) %reduce-scatter.18.cloned.1.call-update) | async-done | bytes 1441808 | tf_op jit(solution)/shard_map/reduce_scatter | solution.py:243
  3808.3 973.5 %reduce-scatter.20.cloned.1.call-done = f32[176,2048]{1,0:T(8,128)} async-done(((f32[5632,2048]{1,0:T(8,128)}), f32[176,2048]{1,0:T(8,128)}) %reduce-scatter.20.cloned.1.call-update) | async-done | bytes 1441808 | tf_op jit(solution)/shard_map/reduce_scatter | solution.py:244
  (378 shorter events, 257.6 us)
Async XLA Ops:
  7.2 60.3 %all-gather.8.cloned.1.call-start = ((), (), s32[]{:S(2)}) async-start(), calls=%async_computation.7 | async-start | bytes 1081344 | tf_op jit(solution)/shard_map/all_gather | solution.py:158
  7.9 115.4 %all-gather.10.cloned.1.call-start = ((), (), s32[]{:S(2)}) async-start(), calls=%async_computation.8 | async-start | bytes 1081344 | tf_op jit(solution)/shard_map/all_gather | solution.py:159
  8.7 194.1 %all-gather.12.cloned.1.call-start = ((), (), s32[]{:S(2)}) async-start(), calls=%async_computation.9 | async-start | bytes 8650752 | tf_op jit(solution)/shard_map/all_gather | solution.py:157
  9.4 277.7 %all-gather.14.cloned.1.call-start = ((), (), s32[]{:S(2)}) async-start(), calls=%async_computation.10 | async-start | bytes 8650752 | tf_op jit(solution)/shard_map/all_gather | solution.py:160
  10.0 423.1 %all-gather.16.cloned.1.call-start = ((), (), s32[]{:S(2)}) async-start(), calls=%async_computation.11 | async-start | bytes 23789568 | tf_op jit(solution)/shard_map/all_gather | solution.py:212
  10.6 568.1 %all-gather.18.cloned.1.call-start = ((), (), s32[]{:S(2)}) async-start(), calls=%async_computation.12 | async-start | bytes 23789568 | tf_op jit(solution)/shard_map/all_gather | solution.py:213
  11.1 713.2 %all-gather.20.cloned.1.call-start = ((), (), s32[]{:S(2)}) async-start(), calls=%async_computation.13 | async-start | bytes 23789568 | tf_op jit(solution)/shard_map/all_gather | solution.py:214
  11.9 1031.5 %reduce-scatter.10.cloned.1.call-start = ((), (), s32[]{:S(2)}) async-start(), calls=%async_computation.15 | async-start | bytes 2162688 | tf_op jit(solution)/shard_map/reduce_scatter | solution.py:323
  222.2 10.5 collective-permute-start
  232.7 10.1 collective-permute-start
  233.3 13.5 collective-permute-start.1
  246.8 9.6 collective-permute-start
  793.1 21.7 collective-permute-start.2
  795.0 19.8 collective-permute-start.3
  814.8 21.6 collective-permute-start.2
  816.0 20.4 collective-permute-start.3
  836.4 21.4 collective-permute-start.2
  837.8 20.1 collective-permute-start.3
  872.2 271.1 %reduce-scatter.12.cloned.1.call-start = ((), (), s32[]{:S(2)}) async-start(), calls=%async_computation.16 | async-start | bytes 2162688 | tf_op jit(solution)/shard_map/reduce_scatter | solution.py:324
  886.6 613.2 %reduce-scatter.8.cloned.1.call-start = ((), (), s32[]{:S(2)}) async-start(), calls=%async_computation.14 | async-start | bytes 17301504 | tf_op jit(solution)/shard_map/reduce_scatter | solution.py:322
  901.4 960.4 %reduce-scatter.14.cloned.1.call-start = ((), (), s32[]{:S(2)}) async-start(), calls=%async_computation.17 | async-start | bytes 17301504 | tf_op jit(solution)/shard_map/reduce_scatter | solution.py:325
  912.4 1922.2 %reduce-scatter.16.cloned.1.call-start = ((), (), s32[]{:S(2)}) async-start(), calls=%async_computation.18 | async-start | bytes 47579136 | tf_op jit(solution)/shard_map/reduce_scatter | solution.py:242
  933.2 2875.0 %reduce-scatter.18.cloned.1.call-start = ((), (), s32[]{:S(2)}) async-start(), calls=%async_computation.19 | async-start | bytes 47579136 | tf_op jit(solution)/shard_map/reduce_scatter | solution.py:243
  953.1 3828.8 %reduce-scatter.20.cloned.1.call-start = ((), (), s32[]{:S(2)}) async-start(), calls=%async_computation.20 | async-start | bytes 47579136 | tf_op jit(solution)/shard_map/reduce_scatter | solution.py:244
  (83 other events, 1614.5 us)
Sparse Core Ops, SparseCore 0:
  11.0 56.4 all-gather.7
  70.5 52.8 all-gather.9
  126.2 76.5 all-gather.11
  205.5 81.5 all-gather.13
  289.8 143.2 all-gather.15
  435.9 142.7 all-gather.17
  581.6 142.7 all-gather.19
  872.3 134.4 reduce-scatter.9
  1009.7 133.5 reduce-scatter.11
  1146.0 353.7 reduce-scatter.7
  1502.7 359.0 reduce-scatter.13
  1864.5 970.0 reduce-scatter.15
  2837.4 970.7 reduce-scatter.17
  3811.0 970.7 reduce-scatter.19
where the time goes:
time: 4800 us; the launch traced here: 4790 us
  waiting for transfers between devices  4330 us (90%)
  matrix products  258 us (5%)
  blocking collectives  81.4 us (2%)
    reduce_scatter x1, waiting for transfers between devices, local(): lax.psum_scatter(grad_up_w, ('dp', 'ctx'), scatter_dimension=0, tiled=True)  974 us
    reduce_scatter x1, waiting for transfers between devices, local(): lax.psum_scatter(grad_down, ('dp', 'ctx'), scatter_dimension=0, tiled=True)  974 us
    reduce_scatter x1, waiting for transfers between devices, local(): lax.psum_scatter(grad_gate_w, ('dp', 'ctx'), scatter_dimension=0, tiled=T...  973 us
    reduce_scatter x1, waiting for transfers between devices, local(): lax.psum_scatter(grad_out_w, ('dp', 'ctx'), scatter_dimension=0, tiled=True)  362 us
    reduce_scatter x1, waiting for transfers between devices, local(): lax.psum_scatter(grad_query_w, ('dp', 'ctx'), scatter_dimension=0, tiled=...  356 us
    all_gather x1, waiting for transfers between devices, local(): lax.all_gather(w_gate, ('dp', 'ctx'), axis=0, tiled=True)  139 us
    all_gather x1, waiting for transfers between devices, local(): lax.all_gather(w_down, ('dp', 'ctx'), axis=0, tiled=True)  132 us
    all_gather x1, waiting for transfers between devices, local(): lax.all_gather(w_up, ('dp', 'ctx'), axis=0, tiled=True)  132 us
  transfers between devices with their start and end apart: 34, of which 22 were waited for; matrix products, arithmetic and copies ran while one was open for 5% of the time, Pallas kernels for 0%

commit v1 on v0

v1 whole, which is shorter than its diff:
```python
import jax
import jax.numpy as jnp
from jax import lax
from jax.sharding import PartitionSpec as P

HEADS = 32
KV_HEADS = 4
HEAD_DIM = 64


NORM_EPS = 1e-05
ROPE_BASE = 10000.0
MASKED_SCORE = -1e30
LOW = jnp.bfloat16
WIDE = jnp.float32


def multiply(left, right):
    return jnp.dot(left, right, preferred_element_type=WIDE)


def against(left, right):
    return lax.dot_general(left, right, (((1,), (1,)), ((), ())), preferred_element_type=WIDE)


def outer_sum(left, right):
    return lax.dot_general(left, right, (((0,), (0,)), ((), ())), preferred_element_type=WIDE)


def swapped(block, distance, axis="ctx"):
    route = [(i, i ^ distance) for i in range(lax.axis_size(axis))]
    return lax.ppermute(block, axis, route)


def ctx_gather(block):
    size = lax.axis_size("ctx")
    if size != 4:
        return [block] + [swapped(block, k) for k in range(1, size)]
    half = block.shape[0] // 2
    from_x = swapped(block, 1)
    from_y = swapped(block, 2)
    far_top = swapped(from_x[:half], 2)
    far_low = swapped(from_y[half:], 1)
    return [block, from_x, from_y, jnp.concatenate([far_top, far_low], 0)]


def ctx_scatter_sum(parts):
    size = lax.axis_size("ctx")
    if size != 4:
        total = parts[0].astype(WIDE)
        for k in range(1, size):
            total = total + swapped(parts[k].astype(LOW), k).astype(WIDE)
        return total
    half = parts[0].shape[-1] // 2
    left = [part[:, :half] for part in parts]
    right = [part[:, half:] for part in parts]
    got_left = swapped(jnp.stack([left[1], left[3]]).astype(LOW), 1).astype(WIDE)
    got_right = swapped(jnp.stack([right[2], right[3]]).astype(LOW), 2).astype(WIDE)
    far_left = swapped((left[2].astype(WIDE) + got_left[1]).astype(LOW), 2).astype(WIDE)
    far_right = swapped((right[1].astype(WIDE) + got_right[1]).astype(LOW), 1).astype(WIDE)
    return jnp.concatenate(
        [
            left[0].astype(WIDE) + got_left[0] + far_left,
            right[0].astype(WIDE) + got_right[0] + far_right,
        ],
        -1,
    )


def in_rank_order(parts):
    me = lax.axis_index("ctx")
    stacked = jnp.stack(parts)
    return [
        lax.dynamic_index_in_dim(stacked, me ^ r, 0, keepdims=False) for r in range(len(parts))
    ]


def rows_to_columns(pick):
    me = lax.axis_index("ctx")
    size = lax.axis_size("ctx")
    parts = [pick(me)] + [swapped(pick(me ^ k), k) for k in range(1, size)]
    return jnp.concatenate(in_rank_order(parts), 0)


def columns_to_rows(block):
    me = lax.axis_index("ctx")
    size = lax.axis_size("ctx")
    rows = block.shape[0] // size
    pieces = [lax.dynamic_slice_in_dim(block, (me ^ k) * rows, rows, 0) for k in range(size)]
    return in_rank_order([pieces[0]] + [swapped(pieces[k], k) for k in range(1, size)])


def regrouped(block, back=False):
    dp_size, ctx_size = lax.axis_size("dp"), lax.axis_size("ctx")
    route = [(b, (b % dp_size) * ctx_size + b // dp_size) for b in range(dp_size * ctx_size)]
    if back:
        route = [(there, here) for here, there in route]
    return lax.ppermute(block, ("dp", "ctx"), route)


def dp_gather(block):
    return lax.all_gather(block, "dp", axis=0, tiled=True)


def dp_scatter_sum(block):
    return lax.psum_scatter(block, "dp", scatter_dimension=0, tiled=True)


def rotate(values, angles):
    cosine = jnp.cos(angles)
    sine = jnp.sin(angles)
    cosine = jnp.concatenate([cosine, cosine], -1)[:, None, :]
    sine = jnp.concatenate([sine, sine], -1)[:, None, :]
    half_dim = values.shape[-1] // 2
    turned = jnp.concatenate([-values[..., half_dim:], values[..., :half_dim]], -1)
    return values * cosine + turned * sine


def norm_scale(values):
    return lax.rsqrt(jnp.mean(values * values, -1, keepdims=True) + NORM_EPS)


def norm_back(grad_hidden, normed, scale_rows, gain):
    gain_grad = jnp.sum(grad_hidden * normed, 0)
    scaled = grad_hidden * gain
    return (
        gain_grad,
        scale_rows * (scaled - normed * jnp.mean(scaled * normed, -1, keepdims=True)),
    )


def split_rows(values, count):
    rows = values.shape[0] // count
    return [values[k * rows : (k + 1) * rows] for k in range(count)]


def local(
    inputs,
    positions,
    block_order,
    norm_attn,
    w_query,
    w_key,
    w_value,
    w_out,
    norm_mlp,
    w_gate,
    w_up,
    w_down,
    cotangent,
):
    row_count = inputs.shape[2]
    model_width = inputs.shape[3]
    block_rows = row_count // 2
    ctx_size = lax.axis_size("ctx")
    ctx_rank = lax.axis_index("ctx")
    head_dim = HEAD_DIM
    heads = HEADS // ctx_size
    sharers = ctx_size // KV_HEADS
    query_width = heads * head_dim
    ff_width = w_gate.shape[1] // ctx_size
    score_scale = head_dim ** (-0.5)
    both = ("dp", "ctx")

    x_low = inputs.reshape(row_count, model_width)
    grad_top = cotangent.reshape(row_count, model_width)
    x_parts = ctx_gather(x_low)
    gains = lax.all_gather(jnp.stack([norm_attn, norm_mlp]), both, axis=1, tiled=True).astype(WIDE)
    gain_attn, gain_mlp = gains[0], gains[1]

    def pick_attn(rank):
        kv_start = rank // sharers * head_dim
        return jnp.concatenate(
            [
                lax.dynamic_slice_in_dim(w_query, rank * query_width, query_width, 1),
                lax.dynamic_slice_in_dim(w_key, kv_start, head_dim, 1),
                lax.dynamic_slice_in_dim(w_value, kv_start, head_dim, 1),
            ],
            1,
        )

    def pick_mlp(rank):
        return jnp.concatenate(
            [
                lax.dynamic_slice_in_dim(w_gate, rank * ff_width, ff_width, 1),
                lax.dynamic_slice_in_dim(w_up, rank * ff_width, ff_width, 1),
            ],
            1,
        )

    part_qkv = dp_gather(rows_to_columns(pick_attn))
    part_out = dp_gather(regrouped(w_out))
    part_gate_up = dp_gather(rows_to_columns(pick_mlp))
    part_down = dp_gather(regrouped(w_down))
    part_gate, part_up = part_gate_up[:, :ff_width], part_gate_up[:, ff_width:]

    frequency = ROPE_BASE ** (-jnp.arange(head_dim // 2, dtype=WIDE) * 2.0 / head_dim)
    position_rows = positions.reshape(row_count)
    all_positions = jnp.concatenate(
        [position_rows] + [swapped(position_rows, k) for k in range(1, ctx_size)]
    )
    angles = all_positions.astype(WIDE)[:, None] * frequency[None, :]
    offsets = jnp.arange(block_rows, dtype=jnp.int32)
    index = jnp.concatenate(
        [
            (
                lax.dynamic_index_in_dim(block_order, ctx_rank ^ k, 0, keepdims=False)[:, None]
                * block_rows
                + offsets[None, :]
            ).reshape(row_count)
            for k in range(ctx_size)
        ]
    )
    visible = index[None, :] <= index[:, None]
    seq_rows = row_count * ctx_size

    x_all = jnp.concatenate(x_parts, 0).astype(WIDE)
    hidden_attn = (x_all * norm_scale(x_all) * gain_attn).astype(LOW)
    qkv = multiply(hidden_attn, part_qkv)
    queries = rotate(qkv[:, :query_width].reshape(seq_rows, heads, head_dim), angles).astype(LOW)
    keys = rotate(qkv[:, None, query_width : query_width + head_dim], angles)[:, 0].astype(LOW)
    values = qkv[:, query_width + head_dim :].astype(LOW)
    scores = jnp.einsum("qhd,kd->hqk", queries, keys, preferred_element_type=WIDE) * score_scale
    scores = jnp.where(visible, scores, MASKED_SCORE)
    maxima = jnp.max(scores, -1, keepdims=True)
    weights = jnp.exp(scores - maxima)
    totals = jnp.sum(weights, -1, keepdims=True)
    log_total = maxima + jnp.log(totals)
    probabilities = (weights / totals).astype(LOW)
    attended = jnp.einsum("hqk,kd->qhd", probabilities, values, preferred_element_type=WIDE)
    attn_low = attended.reshape(seq_rows, query_width).astype(LOW)

    x_rows = x_low.astype(WIDE)
    middle = x_rows + ctx_scatter_sum(split_rows(multiply(attn_low, part_out), ctx_size))
    scale_mlp = norm_scale(middle)
    normed_mlp = middle * scale_mlp
    hidden_mlp = jnp.concatenate(ctx_gather((normed_mlp * gain_mlp).astype(LOW)), 0)
    gate_rows = multiply(hidden_mlp, part_gate)
    up_rows = multiply(hidden_mlp, part_up)
    sigmoid_gate = jax.nn.sigmoid(gate_rows)
    swished = gate_rows * sigmoid_gate
    activated = (swished * up_rows).astype(LOW)

    top_all = jnp.concatenate(ctx_gather(grad_top), 0)
    grad_down = dp_scatter_sum(outer_sum(activated, top_all).astype(LOW))
    grad_activated = against(top_all, part_down)
    grad_gate = (
        grad_activated * up_rows * sigmoid_gate * (1.0 + gate_rows * (1.0 - sigmoid_gate))
    ).astype(LOW)
    grad_up = (grad_activated * swished).astype(LOW)
    grad_gate_up = jnp.concatenate([grad_gate, grad_up], 1)
    grad_hidden_mlp = ctx_scatter_sum(split_rows(against(grad_gate_up, part_gate_up), ctx_size))
    grad_gate_up_w = dp_scatter_sum(outer_sum(hidden_mlp, grad_gate_up).astype(LOW))
    gain_mlp_grad, grad_mid_norm = norm_back(grad_hidden_mlp, normed_mlp, scale_mlp, gain_mlp)
    grad_middle = grad_top.astype(WIDE) + grad_mid_norm
    result = middle + ctx_scatter_sum(split_rows(multiply(activated, part_down), ctx_size))
    outputs = result.astype(LOW).reshape(inputs.shape)

    grad_branch = jnp.concatenate(ctx_gather(grad_middle.astype(LOW)), 0)
    grad_out_w = dp_scatter_sum(outer_sum(attn_low, grad_branch).astype(LOW))
    grad_attn = against(grad_branch, part_out).astype(LOW)
    grad_heads = grad_attn.reshape(seq_rows, heads, head_dim)
    delta_rows = jnp.sum(grad_heads.astype(WIDE) * attended, -1).T[..., None]
    scores = jnp.einsum("qhd,kd->hqk", queries, keys, preferred_element_type=WIDE) * score_scale
    weights = jnp.where(visible, jnp.exp(scores - log_total), 0.0)
    grad_values = jnp.einsum(
        "hqk,qhd->kd", weights.astype(LOW), grad_heads, preferred_element_type=WIDE
    )
    grad_probs = jnp.einsum("qhd,kd->hqk", grad_heads, values, preferred_element_type=WIDE)
    grad_scores = (weights * (grad_probs - delta_rows)).astype(LOW)
    grad_queries = jnp.einsum("hqk,kd->qhd", grad_scores, keys, preferred_element_type=WIDE)
    grad_keys = jnp.einsum("hqk,qhd->kd", grad_scores, queries, preferred_element_type=WIDE)
    grad_queries = rotate(grad_queries * score_scale, -angles).reshape(seq_rows, query_width)
    grad_keys = rotate(grad_keys[:, None, :] * score_scale, -angles)[:, 0]
    grad_qkv = jnp.concatenate([grad_queries, grad_keys, grad_values], 1).astype(LOW)
    grad_hidden_attn = ctx_scatter_sum(split_rows(against(grad_qkv, part_qkv), ctx_size))
    grad_qkv_w = dp_scatter_sum(outer_sum(hidden_attn, grad_qkv).astype(LOW))
    scale_attn = norm_scale(x_rows)
    gain_attn_grad, grad_in_norm = norm_back(
        grad_hidden_attn, x_rows * scale_attn, scale_attn, gain_attn
    )
    grad_inputs = (grad_middle + grad_in_norm).reshape(inputs.shape)

    out_gains = lax.psum_scatter(
        jnp.stack([gain_attn_grad, gain_mlp_grad]), both, scatter_dimension=1, tiled=True
    )
    qkv_rows = columns_to_rows(grad_qkv_w)
    out_query = jnp.concatenate([part[:, :query_width] for part in qkv_rows], 1).astype(WIDE)
    kv_parts = [part[:, query_width:].astype(WIDE) for part in qkv_rows]
    kv_parts = [sum(kv_parts[g * sharers : (g + 1) * sharers]) for g in range(KV_HEADS)]
    out_key = jnp.concatenate([part[:, :head_dim] for part in kv_parts], 1)
    out_value = jnp.concatenate([part[:, head_dim:] for part in kv_parts], 1)
    mlp_rows = columns_to_rows(grad_gate_up_w)
    out_gate = jnp.concatenate([part[:, :ff_width] for part in mlp_rows], 1).astype(WIDE)
    out_up = jnp.concatenate([part[:, ff_width:] for part in mlp_rows], 1).astype(WIDE)
    out_out = regrouped(grad_out_w, back=True).astype(WIDE)
    out_down = regrouped(grad_down, back=True).astype(WIDE)
    return (
        outputs,
        grad_inputs,
        out_gains[0],
        out_query,
        out_key,
        out_value,
        out_out,
        out_gains[1],
        out_gate,
        out_up,
        out_down,
    )


def solution(mesh):
    placed = (
        P("dp", "ctx", None, None),
        P("dp", "ctx", None),
        P(),
        P(("dp", "ctx")),
        P(("dp", "ctx"), None),
        P(("dp", "ctx"), None),
        P(("dp", "ctx"), None),
        P(("dp", "ctx"), None),
        P(("dp", "ctx")),
        P(("dp", "ctx"), None),
        P(("dp", "ctx"), None),
        P(("dp", "ctx"), None),
        P("dp", "ctx", None, None),
    )
    return jax.shard_map(
        local,
        mesh=mesh,
        in_specs=placed,
        out_specs=(
            P("dp", "ctx", None, None),
            P("dp", "ctx", None, None),
            P(("dp", "ctx")),
            P(("dp", "ctx"), None),
            P(("dp", "ctx"), None),
            P(("dp", "ctx"), None),
            P(("dp", "ctx"), None),
            P(("dp", "ctx")),
            P(("dp", "ctx"), None),
            P(("dp", "ctx"), None),
            P(("dp", "ctx"), None),
        ),
        check_vma=False,
    )
```

time: 4800 us -> 1030 us (0.21)
  waiting for transfers between devices: 4330 us -> 514 us
  starting transfers between devices: 24.3 us -> 140 us
  matrix products: 258 us -> 203 us
    reduce_scatter x7 -> x4, waiting for transfers between devices: 3740 us -> 213 us  [dp_scatter_sum(): return lax.psum_scatter(block, 'dp', scatter_dimension=0, tiled=True)]
    all_gather x7 -> x4, waiting for transfers between devices: 565 us -> 0.05 us  [dp_gather(): return lax.all_gather(block, 'dp', axis=0, tiled=True)]
    ppermute x20 -> x51, waiting for transfers between devices: 22.3 us -> 265 us  [the longest x47 265 us: swapped(): return lax.ppermute(block, axis, route)]
    ppermute x20 -> x51, starting transfers between devices: 23.1 us -> 139 us  [the longest x47 134 us: swapped(): return lax.ppermute(block, axis, route)]
    unnamed x2 -> x0, blocking collectives: 81.4 us -> none
    all_gather x0 -> x1, blocking collectives: none -> 64.4 us  [local(): lax.all_gather(jnp.stack([norm_attn, norm_mlp]), both, axis=1, tiled=True)]
    dot_general x35 -> x11, matrix products: 109 us -> 121 us  [the longest x5 47.2 us: multiply(): return jnp.dot(left, right, preferred_element_type=WIDE)]
  transfers between devices with their start and end apart: 34 -> 60, of which waited for: 22 -> 38; matrix products, arithmetic and copies ran while one was open for 5% -> 21% of each run, Pallas kernels for 0% -> 0%
where the time goes in v1:
time: 1030 us; the launch traced here: 1020 us
  waiting for transfers between devices  514 us (50%)
  matrix products  203 us (20%)
  starting transfers between devices  140 us (14%)
  blocking collectives  64.4 us (6%)
  other arithmetic  49 us (5%)
  local copies, waits for them, and re-layouts  33.3 us (3%)
  between operations  15.5 us (2%)
    ppermute x47, waiting for transfers between devices, swapped(): return lax.ppermute(block, axis, route)  265 us
    reduce_scatter x4, waiting for transfers between devices, dp_scatter_sum(): return lax.psum_scatter(block, 'dp', scatter_dimension=0, tiled=True)  213 us
    ppermute x47, starting transfers between devices, swapped(): return lax.ppermute(block, axis, route)  134 us
    all_gather x1, blocking collectives, local(): lax.all_gather(jnp.stack([norm_attn, norm_mlp]), both, axis=1, tiled=True)  64.4 us
    dot_general x5, matrix products, multiply(): return jnp.dot(left, right, preferred_element_type=WIDE)  47.2 us
    dot_general x4, matrix products, against(): lax.dot_general(left, right, (((1,), (1,)), ((), ())), preferred_element_...  43.5 us
    dot_general x4, matrix products, outer_sum(): lax.dot_general(left, right, (((0,), (0,)), ((), ())), preferred_element_...  38.2 us
    unnamed x10, waiting for transfers between devices  35.4 us
  transfers between devices with their start and end apart: 60, of which 38 were waited for; matrix products, arithmetic and copies ran while one was open for 21% of the time, Pallas kernels for 0%

profile of v1, /device:TPU:0, one launch (start us, length us, event | category | flops | bytes accessed | tf_op | source)
XLA Modules:
  0.0 1018.2 jit_solution(7093261290336201782)
XLA Ops:
  22.6 58.4 %collective-permute-start.7 = (s32[256]{0:T(256)S(1)}, s32[256]{0:T(256)S(1)}, u32[]{:S(2)}, u32[]{:S(2)}) collective-permute-start(s32[256]{0:T(256)S(1)} %bitcast.393), channel_id=1, source_target_pairs={{0,1},{1,0},{2,3},{3,2},{4,5},{5,4},{6,7},{7,6},{8,9},{9,8},{10,11... | collective-permute-start | bytes 3080 | tf_op jit(solution)/shard_map/ppermute | solution.py:32
  86.2 64.4 %all-gather = bf16[32,64,2]{1,2,0:T(2,128)(2,1)S(1)} all-gather(bf16[1,64,2]{1,2,0:T(2,128)(2,1)S(1)} %maximum_bitcast_fusion.2), channel_id=1, replica_groups=mesh['dp'=8,'ctx'=4] {'dp','ctx'}, dimensions={0}, use_global_device_ids=true | all-gather | bytes 8448 | tf_op jit(solution)/shard_map/all_gather | solution.py:168
  166.7 13.8 %collective-permute-done = bf16[256,2048]{1,0:T(8,128)(2,1)S(1)} collective-permute-done((bf16[256,2048]{1,0:T(8,128)(2,1)S(1)}, bf16[256,2048]{1,0:T(8,128)(2,1)S(1)}, u32[]{:S(2)}, u32[]{:S(2)}) %collective-permute-start) | collective-permute-done | bytes 1048608 | tf_op jit(solution)/shard_map/ppermute | solution.py:32
  209.3 13.9 %fusion.4 = (f32[8,1024]{1,0:T(8,128)S(1)}, f32[1024,1024,8]{1,0,2:T(8,128)}) fusion(pred[1024,1024]{0,1:T(8,128)(4,1)S(1)} %broadcast_compare_fusion, bf16[1024,64,1]{0,1,2:T(8,128)(2,1)S(1)} %get-tuple-element.109, bf16[1024,8,64]{0,2,1:T(8,128)(2,1)S(1)} %bitcast.364), kind=kOutput, calls=%fused_computation.9 | convolution fusion | flops 1098899456 | bytes 35815424 | tf_op jit(solution)/shard_map/qhd,kd->hqk/dot_general | solution.py:223
  223.2 14.4 %fusion.5 = f32[8,1024]{1,0:T(8,128)S(1)} fusion(f32[1024,1024,8]{1,0,2:T(8,128)} %get-tuple-element.136, f32[8,1024]{1,0:T(8,128)S(1)} %get-tuple-element.135, pred[1024,1024]{0,1:T(8,128)(4,1)S(1)} %broadcast_compare_fusion), kind=kLoop, calls=%fused_computation.10 | loop fusion | flops 33546240 | bytes 34668544 | tf_op jit(solution)/shard_map/reduce_sum | solution.py:227
  237.6 16.2 %bitcast_convert_fusion = (bf16[1024,8,64]{0,2,1:T(8,128)(2,1)S(1)}, f32[64,8,1024]{2,0,1:T(8,128)}) fusion(f32[1024,1024,8]{1,0,2:T(8,128)} %get-tuple-element.136, f32[8,1024]{1,0:T(8,128)S(1)} %fusion.5, f32[8,1024]{1,0:T(8,128)S(1)} %get-tuple-element.135, pred[1024,1024]{0,1:T(8,128)(4,1)S(1)} %broadcast_compare_fusion, f32[1024,640]{0,1:T(8,128)S(1)} %fusion.38), kind=kOutput, calls=%fused_computation.65 | convolution fusion | flops 1116209152 | bytes 37945344 | tf_op jit(solution)/shard_map/hqk,kd->qhd/dot_general | solution.py:230
  260.0 21.2 %collective-permute-done.11 = bf16[2,256,1024]{2,1,0:T(8,128)(2,1)S(1)} collective-permute-done((bf16[2,256,1024]{2,1,0:T(8,128)(2,1)S(1)}, bf16[2,256,1024]{2,1,0:T(8,128)(2,1)S(1)}, u32[]{:S(2)}, u32[]{:S(2)}) %collective-permute-start.11) | collective-permute-done | bytes 1048608 | tf_op jit(solution)/shard_map/ppermute | solution.py:32
  295.0 12.8 %collective-permute-done.27 = bf16[256,2048]{1,0:T(8,128)(2,1)S(1)} collective-permute-done((bf16[256,2048]{1,0:T(8,128)(2,1)S(1)}, bf16[256,2048]{1,0:T(8,128)(2,1)S(1)}, u32[]{:S(2)}, u32[]{:S(2)}) %collective-permute-start.27) | collective-permute-done | bytes 1048608 | tf_op jit(solution)/shard_map/ppermute | solution.py:32
  332.1 10.6 %collective-permute-done.15 = bf16[256,2048]{1,0:T(8,128)(2,1)S(1)} collective-permute-done((bf16[256,2048]{1,0:T(8,128)(2,1)S(1)}, bf16[256,2048]{1,0:T(8,128)(2,1)S(1)}, u32[]{:S(2)}, u32[]{:S(2)}) %collective-permute-start.15) | collective-permute-done | bytes 1048608 | tf_op jit(solution)/shard_map/ppermute | solution.py:32
  364.7 11.7 %fusion.127 = f32[1024,1408]{1,0:T(8,128)} fusion(bf16[1024,2048]{1,0:T(8,128)(2,1)} %copy-done.31, bf16[1408,2048]{1,0:T(8,128)(2,1)} %all-gather.12.cloned.1.call-done), kind=kOutput, calls=%fused_computation.326 | convolution fusion | flops 5905580032 | bytes 15728640 | tf_op jit(solution)/shard_map/dot_general | solution.py:23
  376.4 11.9 %fusion.14 = f32[1024,1408]{1,0:T(8,128)} fusion(bf16[1024,2048]{1,0:T(8,128)(2,1)} %constant_dynamic-update-slice_fusion.5, bf16[2048,2816]{1,0:T(8,128)(2,1)} %all-gather.10.cloned.1.call-done), kind=kOutput, calls=%fused_computation.22 | convolution fusion | flops 5905580032 | bytes 15728640 | tf_op jit(solution)/shard_map/dot_general | solution.py:19
  388.4 15.4 %multiply_convert_fusion.1 = (bf16[1024,1408]{1,0:T(8,128)(2,1)}, bf16[1024,1408]{1,0:T(8,128)(2,1)}, bf16[1024,1408]{1,0:T(8,128)(2,1)}) fusion(f32[1024,1408]{1,0:T(8,128)} %fusion.127, f32[1024,1408]{1,0:T(8,128)} %fusion.14, bf16[1024,2048]{1,0:T(8,128)(2,1)} %constant_dynamic-update-slice_fusion.5, bf16[2048,2816]{1,0:T(8,128)(2,1)S(1)} %copy-done.40), kind=kOutput, calls=%fused_computation.28 | convolution fusion | flops 5927206912 | bytes 30146560 | tf_op jit(solution)/shard_map/dot_general | solution.py:19
  403.7 19.4 %fusion.124 = (bf16[1024,2048]{1,0:T(8,128)(2,1)}, f32[1024,2048]{1,0:T(8,128)}) fusion(bf16[2048,2816]{1,0:T(8,128)(2,1)} %all-gather.10.cloned.1.call-done, bf16[1024,1408]{1,0:T(8,128)(2,1)} %get-tuple-element.25, bf16[1024,1408]{1,0:T(8,128)(2,1)} %get-tuple-element.24), kind=kOutput, calls=%fused_computation.323 | convolution fusion | flops 11824791552 | bytes 29884416 | tf_op jit(solution)/shard_map/dot_general | solution.py:23
  427.0 17.0 %collective-permute-done.31 = bf16[2,256,1024]{2,1,0:T(8,128)(2,1)S(1)} collective-permute-done((bf16[2,256,1024]{2,1,0:T(8,128)(2,1)S(1)}, bf16[2,256,1024]{2,1,0:T(8,128)(2,1)S(1)}, u32[]{:S(2)}, u32[]{:S(2)}) %collective-permute-start.31) | collective-permute-done | bytes 1048608 | tf_op jit(solution)/shard_map/ppermute | solution.py:32
  471.5 19.4 %collective-permute-done.35 = bf16[256,2048]{1,0:T(8,128)(2,1)S(1)} collective-permute-done((bf16[256,2048]{1,0:T(8,128)(2,1)S(1)}, bf16[256,2048]{1,0:T(8,128)(2,1)S(1)}, u32[]{:S(2)}, u32[]{:S(2)}) %collective-permute-start.35) | collective-permute-done | bytes 1048608 | tf_op jit(solution)/shard_map/ppermute | solution.py:32
  517.7 17.8 %fusion.1 = bf16[8,1024,1024]{1,2,0:T(8,128)(2,1)S(1)} fusion(f32[1024,1024,8]{1,0,2:T(8,128)} %get-tuple-element.136, f32[8,1024]{1,0:T(8,128)S(1)} %bitcast.403, f32[8,1024]{1,0:T(8,128)S(1)} %log_add_fusion, pred[1024,1024]{0,1:T(8,128)(4,1)} %copy-done.3, bf16[1024,8,64]{0,2,1:T(8,128)(2,1)} %bitcast.401, f32[1024,640]{0,1:T(8,128)} %copy-done.16), kind=kOutput, calls=%fused_computation.2 | convolution fusion | flops 1124073472 | bytes 52625408 | tf_op jit(solution)/shard_map/qhd,kd->hqk/dot_general | solution.py:269
  548.1 15.3 %fusion.44 = bf16[1024,64]{0,1:T(8,128)(2,1)S(1)} fusion(bf16[1024,8,64]{0,2,1:T(8,128)(2,1)} %bitcast.402, f32[1024,1024,8]{1,0,2:T(8,128)} %get-tuple-element.136, f32[8,1024]{1,0:T(8,128)S(1)} %log_add_fusion, pred[1024,1024]{0,1:T(8,128)(4,1)S(1)} %copy-done.4), kind=kOutput, calls=%fused_computation.86 | convolution fusion | flops 1107361792 | bytes 35815424 | tf_op jit(solution)/shard_map/hqk,qhd->kd/dot_general | solution.py:266
  575.8 16.5 %collective-permute-done.39 = bf16[2,256,1024]{2,1,0:T(8,128)(2,1)S(1)} collective-permute-done((bf16[2,256,1024]{2,1,0:T(8,128)(2,1)S(1)}, bf16[2,256,1024]{2,1,0:T(8,128)(2,1)S(1)}, u32[]{:S(2)}, u32[]{:S(2)}) %collective-permute-start.39) | collective-permute-done | bytes 1048608 | tf_op jit(solution)/shard_map/ppermute | solution.py:32
  627.5 18.5 %convolution_convert_fusion = bf16[2048,2816]{1,0:T(8,128)(2,1)} fusion(bf16[1024,2048]{1,0:T(8,128)(2,1)} %constant_dynamic-update-slice_fusion.5, bf16[1024,1408]{1,0:T(8,128)(2,1)} %get-tuple-element.25, bf16[1024,1408]{1,0:T(8,128)(2,1)} %get-tuple-element.24), kind=kOutput, calls=%fused_computation.15 | convolution fusion | flops 11828461568 | bytes 21495808 | tf_op jit(solution)/shard_map/dot_general | solution.py:27
  658.7 21.0 %collective-permute-done.23 = bf16[2,256,1024]{2,1,0:T(8,128)(2,1)S(1)} collective-permute-done((bf16[2,256,1024]{2,1,0:T(8,128)(2,1)S(1)}, bf16[2,256,1024]{2,1,0:T(8,128)(2,1)S(1)}, u32[]{:S(2)}, u32[]{:S(2)}) %collective-permute-start.23) | collective-permute-done | bytes 1048608 | tf_op jit(solution)/shard_map/ppermute | solution.py:32
  708.9 28.1 %collective-permute-start.44 = (bf16[64,640]{1,0:T(8,128)(2,1)S(1)}, bf16[64,640]{1,0:T(8,128)(2,1)S(1)}, u32[]{:S(2)}, u32[]{:S(2)}) collective-permute-start(bf16[64,640]{1,0:T(8,128)(2,1)S(1)} %get-tuple-element.91), channel_id=1, source_target_pairs={{0,2},{1,3},{2,0},{3,1},{4,6},{5,7},{6,4},{7,5},{8,10},{9,11},{10,... | collective-permute-start | bytes 245768 | tf_op jit(solution)/shard_map/ppermute | solution.py:32
  737.0 35.2 %reduce-scatter.16.cloned.1.call-done = f32[64,2]{1,0:T(8,128)} async-done(((f32[2048,2]{1,0:T(8,128)}), f32[64,2]{1,0:T(8,128)}) %reduce-scatter.16.cloned.1.call-update) | async-done | bytes 528
  775.6 60.3 %reduce-scatter.14.cloned.1.call-done = bf16[176,2048]{1,0:T(8,128)(2,1)} async-done(((bf16[1408,2048]{1,0:T(8,128)(2,1)}), bf16[176,2048]{1,0:T(8,128)(2,1)}) %reduce-scatter.14.cloned.1.call-update) | async-done | bytes 720912 | tf_op jit(solution)/shard_map/reduce_scatter | solution.py:106
  837.6 153.1 %reduce-scatter.12.cloned.1.call-done = bf16[256,2816]{1,0:T(8,128)(2,1)} async-done(((bf16[2048,2816]{1,0:T(8,128)(2,1)}), bf16[256,2816]{1,0:T(8,128)(2,1)}) %reduce-scatter.12.cloned.1.call-update) | async-done | bytes 1441808 | tf_op jit(solution)/shard_map/reduce_scatter | solution.py:106
  (361 shorter events, 316.3 us)
Async XLA Ops:
  7.2 192.1 %all-gather.6.cloned.1.call-start = ((), (), s32[]{:S(2)}) async-start(), calls=%async_computation.5 | async-start | bytes 2949120 | tf_op jit(solution)/shard_map/all_gather | solution.py:102
  19.4 234.4 %all-gather.8.cloned.1.call-start = ((), (), s32[]{:S(2)}) async-start(), calls=%async_computation.6 | async-start | bytes 2359296 | tf_op jit(solution)/shard_map/all_gather | solution.py:102
  20.9 343.8 %all-gather.12.cloned.1.call-start = ((), (), s32[]{:S(2)}) async-start(), calls=%async_computation.8 | async-start | bytes 6488064 | tf_op jit(solution)/shard_map/all_gather | solution.py:102
  22.6 353.9 %all-gather.10.cloned.1.call-start = ((), (), s32[]{:S(2)}) async-start(), calls=%async_computation.7 | async-start | bytes 12976128 | tf_op jit(solution)/shard_map/all_gather | solution.py:102
  22.6 130.3 %collective-permute-start.7 = (s32[256]{0:T(256)S(1)}, s32[256]{0:T(256)S(1)}, u32[]{:S(2)}, u32[]{:S(2)}) collective-permute-start(s32[256]{0:T(256)S(1)} %bitcast.393), channel_id=1, source_target_pairs={{0,1},{1,0},{2,3},{3,2},{4,5},{5,4},{6,7},{7,6},{8,9},{9,8},{10,11... | collective-permute-start | bytes 3080 | tf_op jit(solution)/shard_map/ppermute | solution.py:32
  81.0 72.1 %collective-permute-start.8 = (s32[256]{0:T(256)S(1)}, s32[256]{0:T(256)S(1)}, u32[]{:S(2)}, u32[]{:S(2)}) collective-permute-start(s32[256]{0:T(256)S(1)} %bitcast.394), channel_id=1, source_target_pairs={{0,2},{1,3},{2,0},{3,1},{4,6},{5,7},{6,4},{7,5},{8,10},{9,11},{10,... | collective-permute-start | bytes 3080 | tf_op jit(solution)/shard_map/ppermute | solution.py:32
  81.0 73.7 %collective-permute-start.9 = (s32[256]{0:T(256)S(1)}, s32[256]{0:T(256)S(1)}, u32[]{:S(2)}, u32[]{:S(2)}) collective-permute-start(s32[256]{0:T(256)S(1)} %bitcast.395), channel_id=1, source_target_pairs={{0,3},{1,2},{2,1},{3,0},{4,7},{5,6},{6,5},{7,4},{8,11},{9,10},{10,... | collective-permute-start | bytes 3080 | tf_op jit(solution)/shard_map/ppermute | solution.py:32
  83.4 74.9 %collective-permute-start.19 = (bf16[64,2816]{1,0:T(8,128)(2,1)}, bf16[64,2816]{1,0:T(8,128)(2,1)}, u32[]{:S(2)}, u32[]{:S(2)}) collective-permute-start(bf16[64,2816]{1,0:T(8,128)(2,1)} %pad_maximum_fusion.19), channel_id=1, source_target_pairs={{0,1},{1,0},{2,3},{3,2},{4,5},{5,4},{6,7},{7,6},{8,9},{9,8},{10,11... | collective-permute-start | bytes 1081352 | tf_op jit(solution)/shard_map/ppermute | solution.py:32
  86.1 72.2 %collective-permute-start.20 = (bf16[64,2816]{1,0:T(8,128)(2,1)}, bf16[64,2816]{1,0:T(8,128)(2,1)}, u32[]{:S(2)}, u32[]{:S(2)}) collective-permute-start(bf16[64,2816]{1,0:T(8,128)(2,1)} %pad_maximum_fusion.20), channel_id=1, source_target_pairs={{0,2},{1,3},{2,0},{3,1},{4,6},{5,7},{6,4},{7,5},{8,10},{9,11},{10,... | collective-permute-start | bytes 1081352 | tf_op jit(solution)/shard_map/ppermute | solution.py:32
  153.1 27.4 %collective-permute-start = (bf16[256,2048]{1,0:T(8,128)(2,1)S(1)}, bf16[256,2048]{1,0:T(8,128)(2,1)S(1)}, u32[]{:S(2)}, u32[]{:S(2)}) collective-permute-start(bf16[256,2048]{1,0:T(8,128)(2,1)S(1)} %bitcast.352), channel_id=1, source_target_pairs={{0,1},{1,0},{2,3},{3,2},{4,5},{5,4},{6,7},{7,6},{8,9},{9,8},{10,11... | collective-permute-start | bytes 3145736 | tf_op jit(solution)/shard_map/ppermute | solution.py:32
  154.6 30.4 %collective-permute-start.1 = (bf16[256,2048]{1,0:T(8,128)(2,1)S(1)}, bf16[256,2048]{1,0:T(8,128)(2,1)}, u32[]{:S(2)}, u32[]{:S(2)}) collective-permute-start(bf16[256,2048]{1,0:T(8,128)(2,1)S(1)} %bitcast.353), channel_id=1, source_target_pairs={{0,2},{1,3},{2,0},{3,1},{4,6},{5,7},{6,4},{7,5},{8,10},{9,11},{10,... | collective-permute-start | bytes 3145736 | tf_op jit(solution)/shard_map/ppermute | solution.py:32
  184.8 519.6 %reduce-scatter.10.cloned.1.call-start = ((), (), s32[]{:S(2)}) async-start(), calls=%async_computation.10 | async-start | bytes 2359296 | tf_op jit(solution)/shard_map/reduce_scatter | solution.py:106
  281.7 26.1 %collective-permute-start.27 = (bf16[256,2048]{1,0:T(8,128)(2,1)S(1)}, bf16[256,2048]{1,0:T(8,128)(2,1)S(1)}, u32[]{:S(2)}, u32[]{:S(2)}) collective-permute-start(bf16[256,2048]{1,0:T(8,128)(2,1)S(1)} %bitcast.362), channel_id=1, source_target_pairs={{0,1},{1,0},{2,3},{3,2},{4,5},{5,4},{6,7},{7,6},{8,9},{9,8},{10,11... | collective-permute-start | bytes 3145736 | tf_op jit(solution)/shard_map/ppermute | solution.py:32
  317.9 36.7 %collective-permute-start.16 = (bf16[256,2048]{1,0:T(8,128)(2,1)S(1)}, bf16[256,2048]{1,0:T(8,128)(2,1)S(1)}, u32[]{:S(2)}, u32[]{:S(2)}) collective-permute-start(bf16[256,2048]{1,0:T(8,128)(2,1)S(1)} %get-tuple-element.23), channel_id=1, source_target_pairs={{0,2},{1,3},{2,0},{3,1},{4,6},{5,7},{6,4},{7,5},{8,10},{9,11},{10,... | collective-permute-start | bytes 3145736 | tf_op jit(solution)/shard_map/ppermute | solution.py:32
  320.9 28.3 %collective-permute-start.30 = (bf16[128,2048]{1,0:T(8,128)(2,1)S(1)}, bf16[128,2048]{1,0:T(8,128)(2,1)S(1)}, u32[]{:S(2)}, u32[]{:S(2)}) collective-permute-start(bf16[128,2048]{1,0:T(8,128)(2,1)S(1)} %slice.493), channel_id=1, source_target_pairs={{0,1},{1,0},{2,3},{3,2},{4,5},{5,4},{6,7},{7,6},{8,9},{9,8},{10,11... | collective-permute-start | bytes 1572872 | tf_op jit(solution)/shard_map/ppermute | solution.py:32
  510.8 195.2 %reduce-scatter.8.cloned.1.call-start = ((), (), s32[]{:S(2)}) async-start(), calls=%async_computation.9 | async-start | bytes 2949120 | tf_op jit(solution)/shard_map/reduce_scatter | solution.py:106
  568.8 203.4 %reduce-scatter.16.cloned.1.call-start = ((), (), s32[]{:S(2)}) async-start(), calls=%async_computation.13 | async-start | bytes 1081344
  616.9 219.0 %reduce-scatter.14.cloned.1.call-start = ((), (), s32[]{:S(2)}) async-start(), calls=%async_computation.12 | async-start | bytes 6488064 | tf_op jit(solution)/shard_map/reduce_scatter | solution.py:106
  627.5 363.3 %reduce-scatter.12.cloned.1.call-start = ((), (), s32[]{:S(2)}) async-start(), calls=%async_computation.11 | async-start | bytes 12976128 | tf_op jit(solution)/shard_map/reduce_scatter | solution.py:106
  704.4 69.9 %collective-permute-start.46 = (bf16[64,2048]{1,0:T(8,128)(2,1)}, bf16[64,2048]{1,0:T(8,128)(2,1)S(1)}, u32[]{:S(2)}, u32[]{:S(2)}) collective-permute-start(bf16[64,2048]{1,0:T(8,128)(2,1)} %reduce-scatter.10.cloned.1.call-done), channel_id=1, source_target_pairs={{0,0},{4,1},{8,2},{12,3},{16,4},{20,5},{24,6},{28,7},{1,8},{5,9},{... | collective-permute-start | bytes 786440 | tf_op jit(solution)/shard_map/ppermute | solution.py:98
  707.0 68.1 %collective-permute-start.43 = (bf16[64,640]{1,0:T(8,128)(2,1)S(1)}, bf16[64,640]{1,0:T(8,128)(2,1)S(1)}, u32[]{:S(2)}, u32[]{:S(2)}) collective-permute-start(bf16[64,640]{1,0:T(8,128)(2,1)S(1)} %get-tuple-element.92), channel_id=1, source_target_pairs={{0,1},{1,0},{2,3},{3,2},{4,5},{5,4},{6,7},{7,6},{8,9},{9,8},{10,11... | collective-permute-start | bytes 245768 | tf_op jit(solution)/shard_map/ppermute | solution.py:32
  708.9 66.2 %collective-permute-start.44 = (bf16[64,640]{1,0:T(8,128)(2,1)S(1)}, bf16[64,640]{1,0:T(8,128)(2,1)S(1)}, u32[]{:S(2)}, u32[]{:S(2)}) collective-permute-start(bf16[64,640]{1,0:T(8,128)(2,1)S(1)} %get-tuple-element.91), channel_id=1, source_target_pairs={{0,2},{1,3},{2,0},{3,1},{4,6},{5,7},{6,4},{7,5},{8,10},{9,11},{10,... | collective-permute-start | bytes 245768 | tf_op jit(solution)/shard_map/ppermute | solution.py:32
  737.0 38.1 %collective-permute-start.45 = (bf16[64,640]{1,0:T(8,128)(2,1)S(1)}, bf16[64,640]{1,0:T(8,128)(2,1)S(1)}, u32[]{:S(2)}, u32[]{:S(2)}) collective-permute-start(bf16[64,640]{1,0:T(8,128)(2,1)S(1)} %get-tuple-element.90), channel_id=1, source_target_pairs={{0,3},{1,2},{2,1},{3,0},{4,7},{5,6},{6,5},{7,4},{8,11},{9,10},{10,... | collective-permute-start | bytes 245768 | tf_op jit(solution)/shard_map/ppermute | solution.py:32
  835.9 162.2 %collective-permute-start.50 = (bf16[176,2048]{1,0:T(8,128)(2,1)}, bf16[176,2048]{1,0:T(8,128)(2,1)S(1)}, u32[]{:S(2)}, u32[]{:S(2)}) collective-permute-start(bf16[176,2048]{1,0:T(8,128)(2,1)} %reduce-scatter.14.cloned.1.call-done), channel_id=1, source_target_pairs={{0,0},{4,1},{8,2},{12,3},{16,4},{20,5},{24,6},{28,7},{1,8},{5,9},{... | collective-permute-start | bytes 2162696 | tf_op jit(solution)/shard_map/ppermute | solution.py:98
  (81 other events, 1501.1 us)
Sparse Core Ops, SparseCore 0:
  19.5 55.1 all-gather.5
  76.3 28.9 all-gather.7
  107.5 59.8 all-gather.11
  184.9 104.8 all-gather.9
  510.9 47.6 reduce-scatter.9
  569.0 48.9 reduce-scatter.7
  620.2 151.9 reduce-scatter.15
  774.6 61.2 reduce-scatter.13
  838.3 152.4 reduce-scatter.11

commit v2 on v1

v2 whole, which is shorter than its diff:
```python
import functools

import jax
import jax.numpy as jnp
from jax import lax
from jax.experimental import pallas as pl
from jax.experimental.pallas import tpu as pltpu
from jax.sharding import PartitionSpec as P

HEADS = 32
KV_HEADS = 4
HEAD_DIM = 64
LANES = 2 * HEAD_DIM


NORM_EPS = 1e-05
ROPE_BASE = 10000.0
MASKED_SCORE = -1e30
LOW = jnp.bfloat16
WIDE = jnp.float32


def multiply(left, right):
    return jnp.dot(left, right, preferred_element_type=WIDE)


def against(left, right):
    return lax.dot_general(left, right, (((1,), (1,)), ((), ())), preferred_element_type=WIDE)


def outer_sum(left, right):
    return lax.dot_general(left, right, (((0,), (0,)), ((), ())), preferred_element_type=WIDE)


def swapped(block, distance, axis="ctx"):
    route = [(i, i ^ distance) for i in range(lax.axis_size(axis))]
    return lax.ppermute(block, axis, route)


def tied(*values):
    return lax.optimization_barrier(values)


def tied_lists(received, others):
    values = tied(*received, *others)
    return list(values[: len(received)]), list(values[len(received) :])


def ctx_gather(block, first=(), second=()):
    size = lax.axis_size("ctx")
    if size != 4:
        got = [swapped(block, k) for k in range(1, size)]
        got, others = tied_lists(got, [*first, *second])
        return [block] + got, others
    half = block.shape[0] // 2
    got = [swapped(block, 1), swapped(block, 2)]
    (from_x, from_y), first = tied_lists(got, first)
    got = [swapped(from_x[:half], 2), swapped(from_y[half:], 1)]
    far, second = tied_lists(got, second)
    return [block, from_x, from_y, jnp.concatenate(far, 0)], first + second


def ctx_scatter_sum(values, first=(), second=()):
    size = lax.axis_size("ctx")
    parts = split_rows(values, size)
    if size != 4:
        got = [swapped(parts[k].astype(LOW), k) for k in range(1, size)]
        got, others = tied_lists(got, [*first, *second])
        return sum([part.astype(WIDE) for part in got], parts[0].astype(WIDE)), others
    half = parts[0].shape[-1] // 2
    left = [part[:, :half] for part in parts]
    right = [part[:, half:] for part in parts]
    got = [
        swapped(jnp.stack([left[1], left[3]]).astype(LOW), 1),
        swapped(jnp.stack([right[2], right[3]]).astype(LOW), 2),
    ]
    (got_left, got_right), first = tied_lists(got, first)
    got_left, got_right = got_left.astype(WIDE), got_right.astype(WIDE)
    got = [
        swapped((left[2].astype(WIDE) + got_left[1]).astype(LOW), 2),
        swapped((right[1].astype(WIDE) + got_right[1]).astype(LOW), 1),
    ]
    (far_left, far_right), second = tied_lists(got, second)
    total = jnp.concatenate(
        [
            left[0].astype(WIDE) + got_left[0] + far_left.astype(WIDE),
            right[0].astype(WIDE) + got_right[0] + far_right.astype(WIDE),
        ],
        -1,
    )
    return total, first + second


def in_rank_order(parts):
    me = lax.axis_index("ctx")
    stacked = jnp.stack(parts)
    return [
        lax.dynamic_index_in_dim(stacked, me ^ r, 0, keepdims=False) for r in range(len(parts))
    ]


def exchanged(pick):
    me = lax.axis_index("ctx")
    return [pick(me)] + [swapped(pick(me ^ k), k) for k in range(1, lax.axis_size("ctx"))]


def columns_to_rows(block):
    me = lax.axis_index("ctx")
    size = lax.axis_size("ctx")
    rows = block.shape[0] // size
    pieces = [lax.dynamic_slice_in_dim(block, (me ^ k) * rows, rows, 0) for k in range(size)]
    return in_rank_order([pieces[0]] + [swapped(pieces[k], k) for k in range(1, size)])


def regrouped(block, back=False):
    dp_size, ctx_size = lax.axis_size("dp"), lax.axis_size("ctx")
    route = [(b, (b % dp_size) * ctx_size + b // dp_size) for b in range(dp_size * ctx_size)]
    if back:
        route = [(there, here) for here, there in route]
    return lax.ppermute(block, ("dp", "ctx"), route)


def dp_gather(block):
    return lax.all_gather(block, "dp", axis=0, tiled=True)


def dp_scatter_sum(block):
    return lax.psum_scatter(block, "dp", scatter_dimension=0, tiled=True)


def lane_of(shape):
    return lax.broadcasted_iota(jnp.int32, shape, 1)


def turned(values):
    first = lane_of(values.shape) % HEAD_DIM < HEAD_DIM // 2
    return jnp.where(
        first,
        pltpu.roll(values, LANES - HEAD_DIM // 2, 1),
        pltpu.roll(values, HEAD_DIM // 2, 1),
    )


def both_heads(pair):
    even = lane_of(pair.shape) < HEAD_DIM
    zero = jnp.zeros_like(pair)
    return jnp.concatenate([jnp.where(even, pair, zero), jnp.where(even, zero, pair)], 0)


def one_pair(stacked):
    rows = stacked.shape[0] // 2
    even = lane_of((rows, LANES)) < HEAD_DIM
    return jnp.where(even, stacked[:rows], stacked[rows:])


def seen(rows, chunk, last_key):
    query = lax.broadcasted_iota(jnp.int32, (rows, chunk), 0) % (chunk // 2)
    key = lax.broadcasted_iota(jnp.int32, (rows, chunk), 1)
    return key <= query + last_key


def attend_kernel(pairs, chunk, order, q_ref, kv_ref, cos_ref, sin_ref, cosb_ref, sinb_ref,
                  out_ref, rot_ref, keys_ref, values_ref, lse_ref):
    rows = chunk // 2
    step = pl.program_id(0)
    chunks = keys_ref.shape[0] // chunk

    @pl.when(step == 0)
    def _():
        for b in range(keys_ref.shape[0] // rows):
            here = slice(b * rows, (b + 1) * rows)
            there = pl.ds(pl.multiple_of(order[b] * rows, rows), rows)
            own = kv_ref[here, :]
            other = pltpu.roll(own, HEAD_DIM, 1)
            low = lane_of(own.shape) < HEAD_DIM
            keys = jnp.where(low, own, other)
            keys = keys * cos_ref[here, :] + turned(keys) * sin_ref[here, :]
            keys_ref[there, :] = keys.astype(LOW)
            values_ref[there, :] = jnp.where(low, other, own).astype(LOW)

    cosine, sine = cosb_ref[...], sinb_ref[...]
    place = order[step]
    last_key = (place % 2) * rows
    for p in range(pairs):
        lanes = slice(p * LANES, (p + 1) * LANES)
        pair = q_ref[:, lanes]
        pair = pair * cosine + turned(pair) * sine
        rot_ref[:, lanes] = (pair.astype(LOW).astype(WIDE) * HEAD_DIM**-0.5).astype(LOW)

    for count in range(1, chunks + 1):

        @pl.when(place // 2 == count - 1)
        def _(count=count):
            visible = seen(2 * rows, chunk, last_key)
            all_lse = jnp.zeros((rows, LANES), WIDE)
            lane = lane_of((rows, LANES))
            for p in range(pairs):
                lanes = slice(p * LANES, (p + 1) * LANES)
                queries = both_heads(rot_ref[:, lanes])
                scores = [
                    against(queries, keys_ref[c * chunk : (c + 1) * chunk, :]) for c in range(count)
                ]
                scores[-1] = jnp.where(visible, scores[-1], MASKED_SCORE)
                top = jnp.max(functools.reduce(jnp.maximum, scores), 1, keepdims=True)
                weights = [jnp.exp(s - top) for s in scores]
                total = jnp.sum(functools.reduce(jnp.add, weights), 1, keepdims=True)
                mixture = sum(
                    multiply(w.astype(LOW), values_ref[c * chunk : (c + 1) * chunk, :])
                    for c, w in enumerate(weights)
                )
                out_ref[:, lanes] = one_pair(mixture / total).astype(LOW)
                lse = top + jnp.log(total)
                all_lse = jnp.where(lane == 2 * p, lse[:rows], all_lse)
                all_lse = jnp.where(lane == 2 * p + 1, lse[rows:], all_lse)
            lse_ref[...] = all_lse


def attend_back_kernel(pairs, chunk, order, rot_ref, grad_ref, out_ref, lse_ref, cosb_ref, sinb_ref,
                       keys_ref, values_ref, cos_ref, sin_ref, dqkv_ref, dkeys, dvalues, flat):
    rows = chunk // 2
    step = pl.program_id(0)
    steps = pl.num_programs(0)
    chunks = keys_ref.shape[0] // chunk
    scale = HEAD_DIM**-0.5

    @pl.when(step == 0)
    def _():
        dkeys[...] = jnp.zeros_like(dkeys)
        dvalues[...] = jnp.zeros_like(dvalues)

    place = order[step]
    last_chunk = place // 2
    last_key = (place % 2) * rows
    here = pl.ds(pl.multiple_of(step * rows, rows), rows)
    queries, grads, lses, deltas = [], [], [], []
    for p in range(pairs):
        lanes = slice(p * LANES, (p + 1) * LANES)
        queries.append(both_heads(rot_ref[:, lanes]))
        grads.append(both_heads(grad_ref[:, lanes]))
        product = grad_ref[:, lanes].astype(WIDE) * out_ref[:, lanes].astype(WIDE)
        low = lane_of(product.shape) < HEAD_DIM
        deltas.append(
            jnp.concatenate(
                [
                    jnp.sum(jnp.where(low, product, 0.0), 1, keepdims=True),
                    jnp.sum(jnp.where(low, 0.0, product), 1, keepdims=True),
                ],
                0,
            )
        )
        lses.append(
            jnp.concatenate(
                [lse_ref[:, 2 * p : 2 * p + 1], lse_ref[:, 2 * p + 1 : 2 * p + 2]], 0
            )
        )
    queries_t = [q.T for q in queries]
    grads_t = [g.T for g in grads]

    def one_chunk(c, dq, masked):
        place_c = pl.ds(pl.multiple_of(c * chunk, chunk), chunk)
        keys = keys_ref[place_c, :]
        values = values_ref[place_c, :]
        dk = dkeys[c]
        dv = dvalues[c]
        new = []
        for p in range(pairs):
            weights = jnp.exp(against(queries[p], keys) - lses[p])
            if masked:
                weights = jnp.where(seen(2 * rows, chunk, last_key), weights, 0.0)
            slopes = against(grads[p], values)
            ds = (weights * (slopes - deltas[p])).astype(LOW)
            new.append(dq[p] + multiply(ds, keys))
            dk = dk + multiply(queries_t[p], ds)
            dv = dv + multiply(grads_t[p], weights.astype(LOW))
        dkeys[c] = dk
        dvalues[c] = dv
        return tuple(new)

    start = tuple(jnp.zeros((2 * rows, LANES), WIDE) for _ in range(pairs))
    dq = lax.fori_loop(0, last_chunk, lambda c, d: one_chunk(c, d, False), start)
    dq = one_chunk(last_chunk, dq, True)
    cosine, sine = cosb_ref[...], sinb_ref[...]
    for p in range(pairs):
        pair = one_pair(dq[p]) * scale
        pair = pair * cosine - turned(pair) * sine
        dqkv_ref[here, p * LANES : (p + 1) * LANES] = pair.astype(LOW)

    @pl.when(step == steps - 1)
    def _():
        for c in range(chunks):
            dk, dv = dkeys[c], dvalues[c]
            side = jnp.concatenate(
                [dk[:HEAD_DIM] + dk[HEAD_DIM:], dv[:HEAD_DIM] + dv[HEAD_DIM:]], 0
            )
            flat[c * chunk : (c + 1) * chunk, :] = side.T
        for b in range(keys_ref.shape[0] // rows):
            mine = slice(b * rows, (b + 1) * rows)
            there = pl.ds(pl.multiple_of(order[b] * rows, rows), rows)
            own = flat[there, :]
            back = own * cos_ref[mine, :] - turned(own) * sin_ref[mine, :]
            low = lane_of(own.shape) < HEAD_DIM
            dqkv_ref[mine, pairs * LANES :] = jnp.where(low, back, own).astype(LOW)


def attend(order, qkv, cosine, sine, rows):
    seq, width = qkv.shape[0], qkv.shape[1] - LANES
    pairs = width // LANES
    blocks = seq // rows
    block = lambda w: pl.BlockSpec((rows, w), lambda i, _: (i, 0))
    whole = lambda w, at=0: pl.BlockSpec((seq, w), lambda i, _: (0, at))
    return pl.pallas_call(
        functools.partial(attend_kernel, pairs, 2 * rows),
        grid_spec=pltpu.PrefetchScalarGridSpec(
            num_scalar_prefetch=1,
            grid=(blocks,),
            in_specs=[block(width), whole(LANES, pairs), whole(LANES), whole(LANES), block(LANES), block(LANES)],
            out_specs=[block(width), block(width), whole(LANES), whole(LANES), block(LANES)],
        ),
        out_shape=[
            jax.ShapeDtypeStruct((seq, width), LOW),
            jax.ShapeDtypeStruct((seq, width), LOW),
            jax.ShapeDtypeStruct((seq, LANES), LOW),
            jax.ShapeDtypeStruct((seq, LANES), LOW),
            jax.ShapeDtypeStruct((seq, LANES), WIDE),
        ],
        compiler_params=pltpu.CompilerParams(vmem_limit_bytes=48 << 20),
        cost_estimate=pl.CostEstimate(flops=2 * 2 * seq * seq * width, bytes_accessed=8 << 20, transcendentals=seq * seq * width // HEAD_DIM // 2),
        name="attend",
    )(order, qkv, qkv, cosine, sine, cosine, sine)


def attend_back(order, rotated, grad, out, lse, keys, values, cosine, sine, rows):
    seq, width = rotated.shape
    pairs = width // LANES
    blocks = seq // rows
    block = lambda w: pl.BlockSpec((rows, w), lambda i, _: (i, 0))
    whole = lambda w: pl.BlockSpec((seq, w), lambda i, _: (0, 0))
    chunks = seq // (2 * rows)
    return pl.pallas_call(
        functools.partial(attend_back_kernel, pairs, 2 * rows),
        grid_spec=pltpu.PrefetchScalarGridSpec(
            num_scalar_prefetch=1,
            grid=(blocks,),
            in_specs=[block(width), block(width), block(width), block(LANES), block(LANES), block(LANES),
                      whole(LANES), whole(LANES), whole(LANES), whole(LANES)],
            out_specs=whole(width + LANES),
            scratch_shapes=[
                pltpu.VMEM((chunks, LANES, 2 * rows), WIDE),
                pltpu.VMEM((chunks, LANES, 2 * rows), WIDE),
                pltpu.VMEM((seq, LANES), WIDE),
            ],
        ),
        out_shape=jax.ShapeDtypeStruct((seq, width + LANES), LOW),
        compiler_params=pltpu.CompilerParams(vmem_limit_bytes=48 << 20),
        cost_estimate=pl.CostEstimate(flops=5 * 2 * seq * seq * width, bytes_accessed=8 << 20, transcendentals=seq * seq * width // HEAD_DIM // 2),
        name="attend_back",
    )(order, rotated, grad, out, lse, cosine, sine, keys, values, cosine, sine)


def fold_kernel(count, cuts, qkv_ref, out_ref, joined_ref):
    rows, cut = out_ref.shape[0] // count, out_ref.shape[1] // cuts
    width = qkv_ref.shape[1]
    joined_ref[:, :width] = qkv_ref[...]
    for d in range(count):
        for j in range(cuts):
            there = (d * cuts + j) * rows
            joined_ref[there : there + rows, width:] = out_ref[
                d * rows : (d + 1) * rows, j * cut : (j + 1) * cut
            ]


def fold(qkv, out, count):
    cuts = qkv.shape[0] // out.shape[0]
    width = qkv.shape[1] + out.shape[1] // cuts
    return pl.pallas_call(
        functools.partial(fold_kernel, count, cuts),
        out_shape=jax.ShapeDtypeStruct((qkv.shape[0], width), qkv.dtype),
        compiler_params=pltpu.CompilerParams(vmem_limit_bytes=40 << 20),
        name="fold",
    )(qkv, out)


def unfold_kernel(count, cuts, joined_ref, qkv_ref, out_ref):
    rows, cut = out_ref.shape[0] // count, out_ref.shape[1] // cuts
    width = qkv_ref.shape[1]
    qkv_ref[...] = joined_ref[:, :width]
    for d in range(count):
        for j in range(cuts):
            there = (d * cuts + j) * rows
            out_ref[d * rows : (d + 1) * rows, j * cut : (j + 1) * cut] = joined_ref[
                there : there + rows, width:
            ]


def unfold(joined, cut, cuts, count):
    rows, width = joined.shape
    return pl.pallas_call(
        functools.partial(unfold_kernel, count, cuts),
        out_shape=[
            jax.ShapeDtypeStruct((rows, width - cut), joined.dtype),
            jax.ShapeDtypeStruct((rows // cuts, cut * cuts), joined.dtype),
        ],
        compiler_params=pltpu.CompilerParams(vmem_limit_bytes=40 << 20),
        name="unfold",
    )(joined)


def spread_kernel(dp_size, chunk, gate_ref, up_ref, out_ref):
    ranks, _, width = out_ref.shape
    for side, ref in enumerate((gate_ref, up_ref)):
        for r in range(ranks):
            for d in range(dp_size):
                here = side * width // 2 + d * chunk
                there = (d * ranks + r) * chunk
                out_ref[r, :, here : here + chunk] = ref[:, there : there + chunk]


def merge_kernel(dp_size, chunk, parts_ref, gate_ref, up_ref):
    ranks, _, width = parts_ref.shape
    for side, ref in enumerate((gate_ref, up_ref)):
        for r in range(ranks):
            for d in range(dp_size):
                here = side * width // 2 + d * chunk
                there = (d * ranks + r) * chunk
                ref[:, there : there + chunk] = parts_ref[r, :, here : here + chunk].astype(WIDE)


def spread(gate, up, dp_size, ctx_size, chunk):
    shape = (ctx_size, gate.shape[0], 2 * dp_size * chunk)
    return pl.pallas_call(
        functools.partial(spread_kernel, dp_size, chunk),
        out_shape=jax.ShapeDtypeStruct(shape, gate.dtype),
        name="spread",
    )(gate, up)


def merge(parts, dp_size, chunk):
    shape = jax.ShapeDtypeStruct((parts.shape[1], parts.shape[0] * dp_size * chunk), WIDE)
    return pl.pallas_call(
        functools.partial(merge_kernel, dp_size, chunk), out_shape=[shape, shape], name="merge"
    )(parts)


def norm_scale(values):
    return lax.rsqrt(jnp.mean(values * values, -1, keepdims=True) + NORM_EPS)


def norm_back(grad_hidden, normed, scale_rows, gain):
    gain_grad = jnp.sum(grad_hidden * normed, 0)
    scaled = grad_hidden * gain
    return (
        gain_grad,
        scale_rows * (scaled - normed * jnp.mean(scaled * normed, -1, keepdims=True)),
    )


def split_rows(values, count):
    rows = values.shape[0] // count
    return [values[k * rows : (k + 1) * rows] for k in range(count)]


def local(
    inputs,
    positions,
    block_order,
    norm_attn,
    w_query,
    w_key,
    w_value,
    w_out,
    norm_mlp,
    w_gate,
    w_up,
    w_down,
    cotangent,
):
    row_count = inputs.shape[2]
    model_width = inputs.shape[3]
    block_rows = row_count // 2
    dp_size, ctx_size = lax.axis_size("dp"), lax.axis_size("ctx")
    ctx_rank = lax.axis_index("ctx")
    head_dim = HEAD_DIM
    sharers = ctx_size // KV_HEADS
    query_width = HEADS // ctx_size * head_dim
    qkv_width = query_width + 2 * head_dim
    ff_width = w_gate.shape[1] // ctx_size
    ff_chunk = w_down.shape[0]

    x_low = inputs.reshape(row_count, model_width)
    grad_top = cotangent.reshape(row_count, model_width)
    gain_rows = norm_attn.shape[0]
    own_positions = positions.reshape(gain_rows, -1)
    position_width = own_positions.shape[1]
    own_extras = jnp.concatenate(
        [
            jnp.stack([norm_attn, norm_mlp], 1),
            (own_positions // LANES).astype(LOW),
            (own_positions % LANES).astype(LOW),
        ],
        1,
    )
    own_extras = jnp.pad(own_extras, ((0, 0), (0, LANES - own_extras.shape[1])))

    def pick_attn(rank):
        kv_start = rank // sharers * head_dim
        return jnp.concatenate(
            [
                lax.dynamic_slice_in_dim(w_query, rank * query_width, query_width, 1),
                lax.dynamic_slice_in_dim(w_key, kv_start, head_dim, 1),
                lax.dynamic_slice_in_dim(w_value, kv_start, head_dim, 1),
                own_extras,
            ],
            1,
        )

    cuts = model_width // query_width
    parts_qkv = exchanged(pick_attn)
    parts_qkv, (block_out, x_low, columns) = tied_lists(
        parts_qkv,
        [regrouped(w_out), x_low, spread(w_gate, w_up, dp_size, ctx_size, ff_chunk)],
    )
    block_qkv = jnp.concatenate(in_rank_order(parts_qkv), 0)
    gathered_attn = dp_gather(fold(block_qkv, block_out, 1))
    x_parts, _ = ctx_gather(x_low)
    x_parts, (columns,) = tied_lists(x_parts, [columns])
    x_all = jnp.concatenate(x_parts, 0)
    parts_gate_up = exchanged(
        lambda rank: lax.dynamic_index_in_dim(columns, rank, 0, keepdims=False)
    )
    gathered_qkv, part_out = unfold(gathered_attn, query_width, cuts, dp_size)
    part_qkv = gathered_qkv[:, :qkv_width]
    gains = gathered_qkv[:, qkv_width:].astype(WIDE).T
    gain_attn, gain_mlp = gains[0], gains[1]

    sent = block_qkv.reshape(ctx_size, gain_rows, -1)[:, :, qkv_width + 2 :].astype(WIDE)
    sent = LANES * sent[..., :position_width] + sent[..., position_width : 2 * position_width]
    sent = sent.reshape(ctx_size, row_count)
    ranks = [ctx_rank ^ k for k in range(ctx_size)]
    all_positions = jnp.concatenate(
        [lax.dynamic_index_in_dim(sent, r, 0, keepdims=False) for r in ranks]
    )
    frequency = ROPE_BASE ** (-jnp.arange(head_dim // 2, dtype=WIDE) * 2.0 / head_dim)
    angles = all_positions[:, None] * frequency[None, :]
    cosine = jnp.tile(jnp.cos(angles), (1, 4))
    sine = jnp.sin(angles)
    sine = jnp.concatenate([-sine, sine, -sine, sine], 1)
    order = jnp.concatenate([block_order[r] for r in ranks])

    x_wide = x_all.astype(WIDE)
    normed_attn = x_wide * norm_scale(x_wide)
    hidden_attn = (normed_attn * gain_attn).astype(LOW)
    (qkv,), parts_gate_up = tied_lists([multiply(hidden_attn, part_qkv)], parts_gate_up)
    part_gate_up = dp_gather(jnp.concatenate(in_rank_order(parts_gate_up), 0))
    attn_low, rotated, keys, values, log_total = attend(order, qkv, cosine, sine, block_rows)
    part_mixed = multiply(attn_low, part_out).astype(LOW)

    x_rows = x_low.astype(WIDE)
    mixed, _ = ctx_scatter_sum(part_mixed)
    middle, w_down = tied(x_rows + mixed, w_down)
    part_down = dp_gather(w_down)
    scale_mlp = norm_scale(middle)
    normed_mlp = middle * scale_mlp
    hidden_parts, _ = ctx_gather((normed_mlp * gain_mlp).astype(LOW))
    hidden_parts, (grad_top,) = tied_lists(hidden_parts, [grad_top])
    hidden_mlp = jnp.concatenate(hidden_parts, 0)
    gate_rows = multiply(hidden_mlp, part_gate_up[:, :ff_width])
    up_rows = multiply(hidden_mlp, part_gate_up[:, ff_width:])
    sigmoid_gate = jax.nn.sigmoid(gate_rows)
    swished = gate_rows * sigmoid_gate
    top_parts, (gate_rows, activated) = ctx_gather(
        grad_top, [gate_rows], [(swished * up_rows).astype(LOW)]
    )
    top_all = jnp.concatenate(top_parts, 0)
    part_down_w, part_down = tied(outer_sum(activated, top_all).astype(LOW), part_down)
    grad_down = dp_scatter_sum(part_down_w)

    grad_activated = against(top_all, part_down)
    grad_gate = (
        grad_activated * up_rows * sigmoid_gate * (1.0 + gate_rows * (1.0 - sigmoid_gate))
    ).astype(LOW)
    grad_up = (grad_activated * swished).astype(LOW)
    grad_gate_up = jnp.concatenate([grad_gate, grad_up], 1)
    part_hidden_mlp, grad_gate_up = tied(
        against(grad_gate_up, part_gate_up).astype(LOW), grad_gate_up
    )
    grad_hidden_mlp, (part_gate_up_w,) = ctx_scatter_sum(
        part_hidden_mlp, [outer_sum(hidden_mlp, grad_gate_up).astype(LOW)]
    )
    grad_gate_up_w = dp_scatter_sum(part_gate_up_w)
    gain_mlp_grad, grad_mid_norm = norm_back(grad_hidden_mlp, normed_mlp, scale_mlp, gain_mlp)
    grad_middle = grad_top.astype(WIDE) + grad_mid_norm

    branch_parts, (part_result, grad_down) = ctx_gather(
        grad_middle.astype(LOW), [multiply(activated, part_down).astype(LOW)], [grad_down]
    )
    grad_branch = jnp.concatenate(branch_parts, 0)
    grad_attn, part_result = tied(against(grad_branch, part_out).astype(LOW), part_result)
    grad_qkv = attend_back(
        order, rotated, grad_attn, attn_low, log_total, keys, values, cosine, sine, block_rows
    )
    part_result, (grad_qkv,) = ctx_scatter_sum(part_result, [grad_qkv])
    outputs = (middle + part_result).astype(LOW).reshape(inputs.shape)
    part_hidden_attn = against(grad_qkv, part_qkv)
    gain_attn_grad = jnp.sum(part_hidden_attn * normed_attn, 0)
    gain_grads = jnp.pad(
        jnp.stack([gain_attn_grad, gain_mlp_grad], 1).astype(LOW), ((0, 0), (0, LANES - 2))
    )
    part_hidden_attn, grad_qkv, outputs = tied(part_hidden_attn.astype(LOW), grad_qkv, outputs)
    part_qkv_w = jnp.concatenate([outer_sum(hidden_attn, grad_qkv).astype(LOW), gain_grads], 1)
    part_out_w = outer_sum(attn_low, grad_branch).astype(LOW)
    grad_hidden_attn, (part_attn_w,) = ctx_scatter_sum(
        part_hidden_attn, [fold(part_qkv_w, part_out_w, dp_size)]
    )
    grad_attn_w = dp_scatter_sum(part_attn_w)
    scale_attn = norm_scale(x_rows)
    _, grad_in_norm = norm_back(grad_hidden_attn, x_rows * scale_attn, scale_attn, gain_attn)
    grad_inputs = (grad_middle + grad_in_norm).reshape(inputs.shape)

    gate_up_rows = jnp.stack(columns_to_rows(grad_gate_up_w))
    out_gate, out_up = merge(gate_up_rows, dp_size, ff_chunk)
    out_down = grad_down.astype(WIDE)
    grad_attn_w, out_gate, out_up, grad_inputs = tied(grad_attn_w, out_gate, out_up, grad_inputs)
    grad_qkv_w, grad_out_w = unfold(grad_attn_w, query_width, cuts, 1)
    out_out = regrouped(grad_out_w, back=True).astype(WIDE)
    qkv_rows = columns_to_rows(grad_qkv_w)
    out_query = jnp.concatenate([part[:, :query_width] for part in qkv_rows], 1).astype(WIDE)
    rests = [part[:, query_width:].astype(WIDE) for part in qkv_rows]
    kv_parts = [sum(rests[g * sharers : (g + 1) * sharers]) for g in range(KV_HEADS)]
    out_key = jnp.concatenate([part[:, :head_dim] for part in kv_parts], 1)
    out_value = jnp.concatenate([part[:, head_dim : 2 * head_dim] for part in kv_parts], 1)
    out_gains = sum(rests)[:, 2 * head_dim : 2 * head_dim + 2].T
    return (
        outputs,
        grad_inputs,
        out_gains[0],
        out_query,
        out_key,
        out_value,
        out_out,
        out_gains[1],
        out_gate,
        out_up,
        out_down,
    )


def solution(mesh):
    placed = (
        P("dp", "ctx", None, None),
        P("dp", "ctx", None),
        P(),
        P(("dp", "ctx")),
        P(("dp", "ctx"), None),
        P(("dp", "ctx"), None),
        P(("dp", "ctx"), None),
        P(("dp", "ctx"), None),
        P(("dp", "ctx")),
        P(("dp", "ctx"), None),
        P(("dp", "ctx"), None),
        P(("dp", "ctx"), None),
        P("dp", "ctx", None, None),
    )
    return jax.shard_map(
        local,
        mesh=mesh,
        in_specs=placed,
        out_specs=(
            P("dp", "ctx", None, None),
            P("dp", "ctx", None, None),
            P(("dp", "ctx")),
            P(("dp", "ctx"), None),
            P(("dp", "ctx"), None),
            P(("dp", "ctx"), None),
            P(("dp", "ctx"), None),
            P(("dp", "ctx")),
            P(("dp", "ctx"), None),
            P(("dp", "ctx"), None),
            P(("dp", "ctx"), None),
        ),
        check_vma=False,
    )
```

time: 1030 us -> 576 us (0.56)
  the two profiles are of different devices: /device:TPU:0 before, /device:TPU:6 now
where the time goes in v2:
time: 576 us; the launch traced here: 569 us
  waiting for transfers between devices  231 us (40%)
  matrix products  110 us (19%)
  Pallas kernels  55.7 us (10%)
  other arithmetic  55.4 us (10%)
  local copies, waits for them, and re-layouts  53.2 us (9%)
  starting transfers between devices  47.9 us (8%)
  between operations  15.7 us (3%)
    ppermute x44, waiting for transfers between devices, swapped(): return lax.ppermute(block, axis, route)  186 us
    ppermute x44, starting transfers between devices, swapped(): return lax.ppermute(block, axis, route)  41.6 us
    dot_general x5, matrix products, multiply(): return jnp.dot(left, right, preferred_element_type=WIDE)  38.4 us
    dot_general x4, matrix products, against(): lax.dot_general(left, right, (((1,), (1,)), ((), ())), preferred_element_...  37.1 us
    dot_general x4, matrix products, outer_sum(): lax.dot_general(left, right, (((0,), (0,)), ((), ())), preferred_element_...  34.7 us
    pallas_call x1, Pallas kernels, attend_back(): pl.pallas_call(functools.partial(attend_back_kernel, pairs, 2 * rows), gr...  30.9 us
    unnamed x128, local copies, waits for them, and re-layouts  29.7 us
    reduce_scatter x3, waiting for transfers between devices, dp_scatter_sum(): return lax.psum_scatter(block, 'dp', scatter_dimension=0, tiled=True)  19.2 us
  transfers between devices with their start and end apart: 52, of which 33 were waited for; matrix products, arithmetic and copies ran while one was open for 35% of the time, Pallas kernels for 10%

profile of v2, /device:TPU:6, one launch (start us, length us, event | category | flops | bytes accessed | tf_op | source)
XLA Modules:
  0.0 568.8 jit_solution(12952210051205874265)
XLA Ops:
  28.0 24.2 %collective-permute-done.5 = bf16[256,2048]{1,0:T(8,128)(2,1)S(1)} collective-permute-done((bf16[256,2048]{1,0:T(8,128)(2,1)S(1)}, bf16[256,2048]{1,0:T(8,128)(2,1)S(1)}, u32[]{:S(2)}, u32[]{:S(2)}) %collective-permute-start.5) | collective-permute-done | bytes 1048608 | tf_op jit(solution)/shard_map/ppermute | solution.py:37
  54.4 11.6 %collective-permute-done.7 = bf16[128,2048]{1,0:T(8,128)(2,1)S(1)} collective-permute-done((bf16[128,2048]{1,0:T(8,128)(2,1)S(1)}, bf16[128,2048]{1,0:T(8,128)(2,1)S(1)}, u32[]{:S(2)}, u32[]{:S(2)}) %collective-permute-start.7) | collective-permute-done | bytes 524320 | tf_op jit(solution)/shard_map/ppermute | solution.py:37
  73.7 9.4 %all-gather.4.cloned.1.call-done.joined_ref = bf16[2048,1280]{1,0:T(8,128)(2,1)} async-done(((bf16[256,1280]{1,0:T(8,128)(2,1)}), bf16[2048,1280]{1,0:T(8,128)(2,1)}) %all-gather.4.cloned.1.call-update) | async-done | bytes 5242896 | tf_op jit(solution)/shard_map/all_gather | solution.py:124
  104.3 16.8 %attend.1 = (bf16[1024,512]{1,0:T(8,128)(2,1)S(1)}, bf16[1024,512]{1,0:T(8,128)(2,1)S(1)}, bf16[1024,128]{1,0:T(8,128)(2,1)S(1)}, bf16[1024,128]{1,0:T(8,128)(2,1)S(1)}, f32[1024,128]{1,0:T(8,128)S(1)}) custom-call(s32[8]{0:T(128)S(1)} %pad_add_fusion.order, f32[1024,640]{1,0:T(8,128)} %fusion.16.q_ref.kv_ref, f32[1024,640]{1,0:T(8,128)} %fusion.16.q_ref.kv_ref, ...), custom_call_target="tpu_custom_call" | custom-call | flops 2147483648 | bytes 8388608 | tf_op jit(solution)/shard_map/attend/pallas_call | solution.py:311
  125.4 24.0 %collective-permute-done.11 = bf16[2,256,1024]{2,1,0:T(8,128)(2,1)S(1)} collective-permute-done((bf16[2,256,1024]{2,1,0:T(8,128)(2,1)S(1)}, bf16[2,256,1024]{2,1,0:T(8,128)(2,1)S(1)}, u32[]{:S(2)}, u32[]{:S(2)}) %collective-permute-start.11) | collective-permute-done | bytes 1048608 | tf_op jit(solution)/shard_map/ppermute | solution.py:37
  152.8 11.1 %collective-permute-done.14 = bf16[256,1024]{1,0:T(8,128)(2,1)S(1)} collective-permute-done((bf16[256,1024]{1,0:T(8,128)(2,1)S(1)}, bf16[256,1024]{1,0:T(8,128)(2,1)S(1)}, u32[]{:S(2)}, u32[]{:S(2)}) %collective-permute-start.14) | collective-permute-done | bytes 524320 | tf_op jit(solution)/shard_map/ppermute | solution.py:37
  170.7 21.9 %collective-permute-done.16 = bf16[256,2048]{1,0:T(8,128)(2,1)} collective-permute-done((bf16[256,2048]{1,0:T(8,128)(2,1)}, bf16[256,2048]{1,0:T(8,128)(2,1)}, u32[]{:S(2)}, u32[]{:S(2)}) %collective-permute-start.16) | collective-permute-done | bytes 1048608 | tf_op jit(solution)/shard_map/ppermute | solution.py:37
  197.2 8.8 %collective-permute-done.18 = bf16[128,2048]{1,0:T(8,128)(2,1)S(1)} collective-permute-done((bf16[128,2048]{1,0:T(8,128)(2,1)S(1)}, bf16[128,2048]{1,0:T(8,128)(2,1)S(1)}, u32[]{:S(2)}, u32[]{:S(2)}) %collective-permute-start.18) | collective-permute-done | bytes 524320 | tf_op jit(solution)/shard_map/ppermute | solution.py:37
  221.0 10.5 %fusion.8 = f32[1024,1408]{1,0:T(8,128)S(1)} fusion(bf16[1024,2048]{1,0:T(8,128)(2,1)} %constant_dynamic-update-slice_fusion, bf16[2048,2816]{1,0:T(8,128)(2,1)} %all-gather.6.cloned.1.call-done), kind=kOutput, calls=%fused_computation.13 | convolution fusion | flops 5905580032 | bytes 15728640 | tf_op jit(solution)/shard_map/dot_general | solution.py:24
  235.6 12.1 %multiply_convert_fusion.2 = (bf16[1024,1408]{1,0:T(8,128)(2,1)S(1)}, f32[1024,1408]{1,0:T(8,128)}) fusion(f32[1024,1408]{1,0:T(8,128)S(1)} %fusion.8, bf16[1024,2048]{1,0:T(8,128)(2,1)} %constant_dynamic-update-slice_fusion, bf16[2048,2816]{1,0:T(8,128)(2,1)} %all-gather.6.cloned.1.call-done), kind=kOutput, calls=%fused_computation.18 | convolution fusion | flops 5914230784 | bytes 24379392 | tf_op jit(solution)/shard_map/dot_general | solution.py:24
  253.2 8.0 %convolution_convert_fusion.1 = bf16[1408,2048]{1,0:T(8,128)(2,1)} fusion(bf16[1024,1408]{1,0:T(8,128)(2,1)S(1)} %get-tuple-element.140, bf16[1024,2048]{1,0:T(8,128)(2,1)S(1)} %constant_dynamic-update-slice_fusion.4), kind=kOutput, calls=%fused_computation.8 | convolution fusion | flops 5908463616 | bytes 12845056 | tf_op jit(solution)/shard_map/dot_general | solution.py:32
  263.9 10.6 %fusion.77 = f32[1024,1408]{1,0:T(8,128)S(1)} fusion(bf16[1024,2048]{1,0:T(8,128)(2,1)} %copy-done.45, bf16[1408,2048]{1,0:T(8,128)(2,1)} %all-gather.8.cloned.1.call-done), kind=kOutput, calls=%fused_computation.252 | convolution fusion | flops 5905580032 | bytes 15728640 | tf_op jit(solution)/shard_map/dot_general | solution.py:28
  283.5 16.4 %convolution_convert_fusion.2 = bf16[1024,2048]{1,0:T(8,128)(2,1)} fusion(bf16[2048,2816]{1,0:T(8,128)(2,1)} %all-gather.6.cloned.1.call-done, bf16[1024,1408]{1,0:T(8,128)(2,1)S(1)} %get-tuple-element.199, bf16[1024,1408]{1,0:T(8,128)(2,1)S(1)} %get-tuple-element.198), kind=kOutput, calls=%fused_computation.22 | convolution fusion | flops 11824791552 | bytes 21495808 | tf_op jit(solution)/shard_map/dot_general | solution.py:28
  305.0 17.9 %convolution_convert_fusion = bf16[2048,2816]{1,0:T(8,128)(2,1)} fusion(bf16[1024,2048]{1,0:T(8,128)(2,1)} %constant_dynamic-update-slice_fusion, bf16[1024,2816]{1,0:T(8,128)(2,1)S(1)} %copy-done.23), kind=kOutput, calls=%fused_computation | convolution fusion | flops 11816927232 | bytes 21495808 | tf_op jit(solution)/shard_map/dot_general | solution.py:32
  335.4 10.9 %collective-permute-done.26 = bf16[256,1024]{1,0:T(8,128)(2,1)S(1)} collective-permute-done((bf16[256,1024]{1,0:T(8,128)(2,1)S(1)}, bf16[256,1024]{1,0:T(8,128)(2,1)S(1)}, u32[]{:S(2)}, u32[]{:S(2)}) %collective-permute-start.26) | collective-permute-done | bytes 524320 | tf_op jit(solution)/shard_map/ppermute | solution.py:37
  353.6 8.6 %convolution_convert_fusion.3 = bf16[1024,2048]{1,0:T(8,128)(2,1)} fusion(bf16[1024,1408]{1,0:T(8,128)(2,1)S(1)} %copy-done.53, bf16[1408,2048]{1,0:T(8,128)(2,1)S(1)} %bitcast.244), kind=kOutput, calls=%fused_computation.23 | convolution fusion | flops 5907677184 | bytes 12845056 | tf_op jit(solution)/shard_map/dot_general | solution.py:24
  362.2 13.3 %collective-permute-done.28 = bf16[256,2048]{1,0:T(8,128)(2,1)S(1)} collective-permute-done((bf16[256,2048]{1,0:T(8,128)(2,1)S(1)}, bf16[256,2048]{1,0:T(8,128)(2,1)S(1)}, u32[]{:S(2)}, u32[]{:S(2)}) %collective-permute-start.28) | collective-permute-done | bytes 1048608 | tf_op jit(solution)/shard_map/ppermute | solution.py:37
  378.5 8.6 %collective-permute-done.30 = bf16[128,2048]{1,0:T(8,128)(2,1)} collective-permute-done((bf16[128,2048]{1,0:T(8,128)(2,1)S(1)}, bf16[128,2048]{1,0:T(8,128)(2,1)}, u32[]{:S(2)}, u32[]{:S(2)}) %collective-permute-start.30) | collective-permute-done | bytes 524320 | tf_op jit(solution)/shard_map/ppermute | solution.py:37
  399.0 30.9 %attend_back.1 = bf16[1024,640]{1,0:T(8,128)(2,1)} custom-call(s32[8]{0:T(128)S(1)} %pad_add_fusion.order, bf16[1024,512]{1,0:T(8,128)(2,1)S(1)} %copy-done.10, bf16[1024,512]{1,0:T(8,128)(2,1)S(1)} %convolution_convert_fusion.7.grad_ref, bf16[1024,512]{1,0:T(8,128)(2,1)S(1)} %copy-done.8, f32[1024,128]{1,0:T(8,128)S(1)} %get-tuple-element.159.lse_ref, ...), custom_call_target="tpu_custom_call" | custom-call | flops 5368709120 | bytes 8388608 | tf_op jit(solution)/shard_map/attend_back/pallas_call | solution.py:339
  464.8 9.7 %collective-permute-done.35 = bf16[2,256,1024]{2,1,0:T(8,128)(2,1)} collective-permute-done((bf16[2,256,1024]{2,1,0:T(8,128)(2,1)}, bf16[2,256,1024]{2,1,0:T(8,128)(2,1)}, u32[]{:S(2)}, u32[]{:S(2)}) %collective-permute-start.35) | collective-permute-done | bytes 1048608 | tf_op jit(solution)/shard_map/ppermute | solution.py:37
  481.5 9.2 %collective-permute-done.41 = bf16[256,1024]{1,0:T(8,128)(2,1)S(1)} collective-permute-done((bf16[256,1024]{1,0:T(8,128)(2,1)S(1)}, bf16[256,1024]{1,0:T(8,128)(2,1)S(1)}, u32[]{:S(2)}, u32[]{:S(2)}) %collective-permute-start.41) | collective-permute-done | bytes 524320 | tf_op jit(solution)/shard_map/ppermute | solution.py:37
  490.7 6.1 %collective-permute-done.40 = bf16[256,1024]{1,0:T(8,128)(2,1)S(1)} collective-permute-done((bf16[256,1024]{1,0:T(8,128)(2,1)S(1)}, bf16[256,1024]{1,0:T(8,128)(2,1)S(1)}, u32[]{:S(2)}, u32[]{:S(2)}) %collective-permute-start.40) | collective-permute-done | bytes 524320 | tf_op jit(solution)/shard_map/ppermute | solution.py:37
  515.7 19.2 %reduce-scatter.6.cloned.1.call-done.joined_ref = bf16[256,1280]{1,0:T(8,128)(2,1)} async-done(((bf16[2048,1280]{1,0:T(8,128)(2,1)}), bf16[256,1280]{1,0:T(8,128)(2,1)}) %reduce-scatter.6.cloned.1.call-update) | async-done | bytes 655376 | tf_op jit(solution)/shard_map/reduce_scatter | solution.py:128
  547.2 13.7 %collective-permute-done.45 = bf16[64,2048]{1,0:T(8,128)(2,1)S(1)} collective-permute-done((bf16[64,2048]{1,0:T(8,128)(2,1)S(1)}, bf16[64,2048]{1,0:T(8,128)(2,1)S(1)}, u32[]{:S(2)}, u32[]{:S(2)}) %collective-permute-start.45) | collective-permute-done | bytes 262176 | tf_op jit(solution)/shard_map/ppermute | solution.py:120
  (357 shorter events, 219.6 us)
Async XLA Ops:
  7.2 75.9 %all-gather.4.cloned.1.call-start = ((), (), s32[]{:S(2)}) async-start(), calls=%async_computation.3 | async-start | bytes 5898240 | tf_op jit(solution)/shard_map/all_gather | solution.py:124
  26.9 194.1 %all-gather.6.cloned.1.call-start = ((), (), s32[]{:S(2)}) async-start(), calls=%async_computation.4 | async-start | bytes 12976128 | tf_op jit(solution)/shard_map/all_gather | solution.py:124
  26.9 25.2 %collective-permute-start.5 = (bf16[256,2048]{1,0:T(8,128)(2,1)S(1)}, bf16[256,2048]{1,0:T(8,128)(2,1)S(1)}, u32[]{:S(2)}, u32[]{:S(2)}) collective-permute-start(bf16[256,2048]{1,0:T(8,128)(2,1)S(1)} %bitcast.216), channel_id=1, source_target_pairs={{0,2},{1,3},{2,0},{3,1},{4,6},{5,7},{6,4},{7,5},{8,10},{9,11},{10,... | collective-permute-start | bytes 3145736 | tf_op jit(solution)/shard_map/ppermute | solution.py:37
  28.0 24.9 %collective-permute-start.4 = (bf16[256,2048]{1,0:T(8,128)(2,1)S(1)}, bf16[256,2048]{1,0:T(8,128)(2,1)S(1)}, u32[]{:S(2)}, u32[]{:S(2)}) collective-permute-start(bf16[256,2048]{1,0:T(8,128)(2,1)S(1)} %bitcast.217), channel_id=1, source_target_pairs={{0,1},{1,0},{2,3},{3,2},{4,5},{5,4},{6,7},{7,6},{8,9},{9,8},{10,11... | collective-permute-start | bytes 3145736 | tf_op jit(solution)/shard_map/ppermute | solution.py:37
  69.2 24.3 %collective-permute-start.10 = (bf16[64,2816]{1,0:T(8,128)(2,1)}, bf16[64,2816]{1,0:T(8,128)(2,1)}, u32[]{:S(2)}, u32[]{:S(2)}) collective-permute-start(bf16[64,2816]{1,0:T(8,128)(2,1)} %get-tuple-element.246), channel_id=1, source_target_pairs={{0,3},{1,2},{2,1},{3,0},{4,7},{5,6},{6,5},{7,4},{8,11},{9,10},{10,... | collective-permute-start | bytes 1081352 | tf_op jit(solution)/shard_map/ppermute | solution.py:37
  71.1 22.5 %collective-permute-start.9 = (bf16[64,2816]{1,0:T(8,128)(2,1)}, bf16[64,2816]{1,0:T(8,128)(2,1)}, u32[]{:S(2)}, u32[]{:S(2)}) collective-permute-start(bf16[64,2816]{1,0:T(8,128)(2,1)} %get-tuple-element.247), channel_id=1, source_target_pairs={{0,2},{1,3},{2,0},{3,1},{4,6},{5,7},{6,4},{7,5},{8,10},{9,11},{10,... | collective-permute-start | bytes 1081352 | tf_op jit(solution)/shard_map/ppermute | solution.py:37
  72.1 21.5 %collective-permute-start.8 = (bf16[64,2816]{1,0:T(8,128)(2,1)}, bf16[64,2816]{1,0:T(8,128)(2,1)}, u32[]{:S(2)}, u32[]{:S(2)}) collective-permute-start(bf16[64,2816]{1,0:T(8,128)(2,1)} %get-tuple-element.248), channel_id=1, source_target_pairs={{0,1},{1,0},{2,3},{3,2},{4,5},{5,4},{6,7},{7,6},{8,9},{9,8},{10,11... | collective-permute-start | bytes 1081352 | tf_op jit(solution)/shard_map/ppermute | solution.py:37
  96.3 167.4 %all-gather.8.cloned.1.call-start = ((), (), s32[]{:S(2)}) async-start(), calls=%async_computation.5 | async-start | bytes 6488064 | tf_op jit(solution)/shard_map/all_gather | solution.py:124
  123.9 25.4 %collective-permute-start.11 = (bf16[2,256,1024]{2,1,0:T(8,128)(2,1)S(1)}, bf16[2,256,1024]{2,1,0:T(8,128)(2,1)S(1)}, u32[]{:S(2)}, u32[]{:S(2)}) collective-permute-start(bf16[2,256,1024]{2,1,0:T(8,128)(2,1)S(1)} %pad_maximum_fusion.8), channel_id=1, source_target_pairs={{0,1},{1,0},{2,3},{3,2},{4,5},{5,4},{6,7},{7,6},{8,9},{9,8},{10,11... | collective-permute-start | bytes 3145736 | tf_op jit(solution)/shard_map/ppermute | solution.py:37
  124.6 25.1 %collective-permute-start.12 = (bf16[2,256,1024]{2,1,0:T(8,128)(2,1)S(1)}, bf16[2,256,1024]{2,1,0:T(8,128)(2,1)S(1)}, u32[]{:S(2)}, u32[]{:S(2)}) collective-permute-start(bf16[2,256,1024]{2,1,0:T(8,128)(2,1)S(1)} %pad_maximum_fusion.9), channel_id=1, source_target_pairs={{0,2},{1,3},{2,0},{3,1},{4,6},{5,7},{6,4},{7,5},{8,10},{9,11},{10,... | collective-permute-start | bytes 3145736 | tf_op jit(solution)/shard_map/ppermute | solution.py:37
  169.1 23.5 %collective-permute-start.16 = (bf16[256,2048]{1,0:T(8,128)(2,1)}, bf16[256,2048]{1,0:T(8,128)(2,1)}, u32[]{:S(2)}, u32[]{:S(2)}) collective-permute-start(bf16[256,2048]{1,0:T(8,128)(2,1)} %multiply_convert_fusion.3), channel_id=1, source_target_pairs={{0,2},{1,3},{2,0},{3,1},{4,6},{5,7},{6,4},{7,5},{8,10},{9,11},{10,... | collective-permute-start | bytes 3145736 | tf_op jit(solution)/shard_map/ppermute | solution.py:37
  169.6 23.3 %collective-permute-start.15 = (bf16[256,2048]{1,0:T(8,128)(2,1)}, bf16[256,2048]{1,0:T(8,128)(2,1)}, u32[]{:S(2)}, u32[]{:S(2)}) collective-permute-start(bf16[256,2048]{1,0:T(8,128)(2,1)} %multiply_convert_fusion.3), channel_id=1, source_target_pairs={{0,1},{1,0},{2,3},{3,2},{4,5},{5,4},{6,7},{7,6},{8,9},{9,8},{10,11... | collective-permute-start | bytes 3145736 | tf_op jit(solution)/shard_map/ppermute | solution.py:37
  170.2 216.9 %reduce-scatter.4.cloned.1.call-start = ((), (), s32[]{:S(2)}) async-start(), calls=%async_computation.6 | async-start | bytes 6488064 | tf_op jit(solution)/shard_map/reduce_scatter | solution.py:128
  207.5 24.0 %collective-permute-start.20 = (bf16[256,2048]{1,0:T(8,128)(2,1)}, bf16[256,2048]{1,0:T(8,128)(2,1)}, u32[]{:S(2)}, u32[]{:S(2)}) collective-permute-start(bf16[256,2048]{1,0:T(8,128)(2,1)} %bitcast.30), channel_id=1, source_target_pairs={{0,2},{1,3},{2,0},{3,1},{4,6},{5,7},{6,4},{7,5},{8,10},{9,11},{10,... | collective-permute-start | bytes 3145736 | tf_op jit(solution)/shard_map/ppermute | solution.py:37
  209.0 22.5 %collective-permute-start.19 = (bf16[256,2048]{1,0:T(8,128)(2,1)}, bf16[256,2048]{1,0:T(8,128)(2,1)}, u32[]{:S(2)}, u32[]{:S(2)}) collective-permute-start(bf16[256,2048]{1,0:T(8,128)(2,1)} %bitcast.30), channel_id=1, source_target_pairs={{0,1},{1,0},{2,3},{3,2},{4,5},{5,4},{6,7},{7,6},{8,9},{9,8},{10,11... | collective-permute-start | bytes 3145736 | tf_op jit(solution)/shard_map/ppermute | solution.py:37
  263.7 234.1 %reduce-scatter.8.cloned.1.call-start = ((), (), s32[]{:S(2)}) async-start(), calls=%async_computation.8 | async-start | bytes 12976128 | tf_op jit(solution)/shard_map/reduce_scatter | solution.py:128
  302.8 25.6 %collective-permute-start.23 = (bf16[2,256,1024]{2,1,0:T(8,128)(2,1)}, bf16[2,256,1024]{2,1,0:T(8,128)(2,1)}, u32[]{:S(2)}, u32[]{:S(2)}) collective-permute-start(bf16[2,256,1024]{2,1,0:T(8,128)(2,1)} %pad_maximum_fusion.11), channel_id=1, source_target_pairs={{0,1},{1,0},{2,3},{3,2},{4,5},{5,4},{6,7},{7,6},{8,9},{9,8},{10,11... | collective-permute-start | bytes 3145736 | tf_op jit(solution)/shard_map/ppermute | solution.py:37
  304.5 25.3 %collective-permute-start.24 = (bf16[2,256,1024]{2,1,0:T(8,128)(2,1)}, bf16[2,256,1024]{2,1,0:T(8,128)(2,1)}, u32[]{:S(2)}, u32[]{:S(2)}) collective-permute-start(bf16[2,256,1024]{2,1,0:T(8,128)(2,1)} %pad_maximum_fusion.12), channel_id=1, source_target_pairs={{0,2},{1,3},{2,0},{3,1},{4,6},{5,7},{6,4},{7,5},{8,10},{9,11},{10,... | collective-permute-start | bytes 3145736 | tf_op jit(solution)/shard_map/ppermute | solution.py:37
  329.8 205.1 %reduce-scatter.6.cloned.1.call-start = ((), (), s32[]{:S(2)}) async-start(), calls=%async_computation.7 | async-start | bytes 5898240 | tf_op jit(solution)/shard_map/reduce_scatter | solution.py:128
  352.4 23.0 %collective-permute-start.28 = (bf16[256,2048]{1,0:T(8,128)(2,1)S(1)}, bf16[256,2048]{1,0:T(8,128)(2,1)S(1)}, u32[]{:S(2)}, u32[]{:S(2)}) collective-permute-start(bf16[256,2048]{1,0:T(8,128)(2,1)S(1)} %get-tuple-element.196), channel_id=1, source_target_pairs={{0,2},{1,3},{2,0},{3,1},{4,6},{5,7},{6,4},{7,5},{8,10},{9,11},{10,... | collective-permute-start | bytes 3145736 | tf_op jit(solution)/shard_map/ppermute | solution.py:37
  353.0 23.1 %collective-permute-start.27 = (bf16[256,2048]{1,0:T(8,128)(2,1)S(1)}, bf16[256,2048]{1,0:T(8,128)(2,1)S(1)}, u32[]{:S(2)}, u32[]{:S(2)}) collective-permute-start(bf16[256,2048]{1,0:T(8,128)(2,1)S(1)} %get-tuple-element.196), channel_id=1, source_target_pairs={{0,1},{1,0},{2,3},{3,2},{4,5},{5,4},{6,7},{7,6},{8,9},{9,8},{10,11... | collective-permute-start | bytes 3145736 | tf_op jit(solution)/shard_map/ppermute | solution.py:37
  396.0 38.5 %collective-permute-start.31 = (bf16[2,256,1024]{2,1,0:T(8,128)(2,1)S(1)}, bf16[2,256,1024]{2,1,0:T(8,128)(2,1)S(1)}, u32[]{:S(2)}, u32[]{:S(2)}) collective-permute-start(bf16[2,256,1024]{2,1,0:T(8,128)(2,1)S(1)} %pad_maximum_fusion.13), channel_id=1, source_target_pairs={{0,1},{1,0},{2,3},{3,2},{4,5},{5,4},{6,7},{7,6},{8,9},{9,8},{10,11... | collective-permute-start | bytes 3145736 | tf_op jit(solution)/shard_map/ppermute | solution.py:37
  397.5 37.0 %collective-permute-start.32 = (bf16[2,256,1024]{2,1,0:T(8,128)(2,1)S(1)}, bf16[2,256,1024]{2,1,0:T(8,128)(2,1)S(1)}, u32[]{:S(2)}, u32[]{:S(2)}) collective-permute-start(bf16[2,256,1024]{2,1,0:T(8,128)(2,1)S(1)} %pad_maximum_fusion.14), channel_id=1, source_target_pairs={{0,2},{1,3},{2,0},{3,1},{4,6},{5,7},{6,4},{7,5},{8,10},{9,11},{10,... | collective-permute-start | bytes 3145736 | tf_op jit(solution)/shard_map/ppermute | solution.py:37
  540.9 20.0 %collective-permute-start.45 = (bf16[64,2048]{1,0:T(8,128)(2,1)S(1)}, bf16[64,2048]{1,0:T(8,128)(2,1)S(1)}, u32[]{:S(2)}, u32[]{:S(2)}) collective-permute-start(bf16[64,2048]{1,0:T(8,128)(2,1)S(1)} %get-tuple-element.181), channel_id=1, source_target_pairs={{0,0},{4,1},{8,2},{12,3},{16,4},{20,5},{24,6},{28,7},{1,8},{5,9},{... | collective-permute-start | bytes 786440 | tf_op jit(solution)/shard_map/ppermute | solution.py:120
  (86 other events, 707.8 us)
Sparse Core Ops, SparseCore 0:
  27.0 56.0 all-gather.3
  96.4 106.8 all-gather.5
  204.9 58.7 all-gather.7
  265.8 63.5 reduce-scatter.3
  331.6 117.6 reduce-scatter.7
  476.3 58.5 reduce-scatter.5

commit v3 on v2

--- a/solution.py
+++ b/solution.py
@@ -50,14 +50,17 @@
     size = lax.axis_size("ctx")
     if size != 4:
         got = [swapped(block, k) for k in range(1, size)]
+        second = second(*first) if callable(second) else second
         got, others = tied_lists(got, [*first, *second])
         return [block] + got, others
-    half = block.shape[0] // 2
-    got = [swapped(block, 1), swapped(block, 2)]
-    (from_x, from_y), first = tied_lists(got, first)
-    got = [swapped(from_x[:half], 2), swapped(from_y[half:], 1)]
-    far, second = tied_lists(got, second)
-    return [block, from_x, from_y, jnp.concatenate(far, 0)], first + second
+    top, low = split_rows(block, 2)
+    near = [swapped(top, 1), swapped(low, 2)]
+    late = [swapped(low, 1), swapped(top, 2)]
+    near, first = tied_lists(near, first)
+    far = [swapped(near[0], 2), swapped(near[1], 1)]
+    second = second(*first) if callable(second) else second
+    got, second = tied_lists(late + far, second)
+    return [block, near[0], *got[:2], near[1], *got[2:]], first + second
 
 
 def ctx_scatter_sum(values, first=(), second=()):
@@ -110,14 +113,6 @@
     rows = block.shape[0] // size
     pieces = [lax.dynamic_slice_in_dim(block, (me ^ k) * rows, rows, 0) for k in range(size)]
     return in_rank_order([pieces[0]] + [swapped(pieces[k], k) for k in range(1, size)])
-
-
-def regrouped(block, back=False):
-    dp_size, ctx_size = lax.axis_size("dp"), lax.axis_size("ctx")
-    route = [(b, (b % dp_size) * ctx_size + b // dp_size) for b in range(dp_size * ctx_size)]
-    if back:
-        route = [(there, here) for here, there in route]
-    return lax.ppermute(block, ("dp", "ctx"), route)
 
 
 def dp_gather(block):
@@ -405,6 +400,28 @@
     )(joined)
 
 
+def place_kernel(outer, me_ref, *refs):
+    *part_refs, out_ref = refs
+    rows = out_ref.shape[2]
+    for k, ref in enumerate(part_refs):
+        for i in range(outer):
+            out_ref[i, me_ref[0] ^ k] = ref[i * rows : (i + 1) * rows, :]
+
+
+def placed_by_rank(parts, outer):
+    rows, width = parts[0].shape[0] // outer, parts[0].shape[1]
+    vmem = pl.BlockSpec(memory_space=pltpu.VMEM)
+    out = pl.pallas_call(
+        functools.partial(place_kernel, outer),
+        in_specs=[pl.BlockSpec(memory_space=pltpu.SMEM)] + [vmem] * len(parts),
+        out_specs=vmem,
+        out_shape=jax.ShapeDtypeStruct((outer, len(parts), rows, width), parts[0].dtype),
+        compiler_params=pltpu.CompilerParams(vmem_limit_bytes=40 << 20),
+        name="place",
+    )(lax.axis_index("ctx").reshape(1), *parts)
+    return out.reshape(-1, width)
+
+
 def spread_kernel(dp_size, chunk, gate_ref, up_ref, out_ref):
     ranks, _, width = out_ref.shape
     for side, ref in enumerate((gate_ref, up_ref)):
@@ -439,6 +456,179 @@
     return pl.pallas_call(
         functools.partial(merge_kernel, dp_size, chunk), out_shape=[shape, shape], name="merge"
     )(parts)
+
+
+def tiles(width, size):
+    return [slice(at, min(at + size, width)) for at in range(0, width, size)]
+
+
+def gate_up_kernel(gate_w_ref, up_w_ref, *refs):
+    *piece_refs, gate_ref, up_ref, active_ref, hidden_ref, rows, arrived, left = refs
+    copy_out = pltpu.make_async_copy(rows, hidden_ref, left)
+
+    @pl.when(pl.program_id(0) == 0)
+    def _():
+        copies, at = [], 0
+        for k, ref in enumerate(piece_refs):
+            here = pl.ds(at, ref.shape[0])
+            copies.append(pltpu.make_async_copy(ref, rows.at[here, :], arrived.at[k]))
+            copies[-1].start()
+            at += ref.shape[0]
+        for copy in copies:
+            copy.wait()
+        copy_out.start()
+
+    width = gate_ref.shape[1]
+    sides = jnp.concatenate([gate_w_ref[...], up_w_ref[...]], 1)
+    both = multiply(rows[...], sides)
+    gate, up = both[:, :width], both[:, width:]
+    gate_ref[...] = gate
+    up_ref[...] = up
+    active_ref[...] = (gate * jax.nn.sigmoid(gate) * up).astype(LOW)
+
+    @pl.when(pl.program_id(0) == pl.num_programs(0) - 1)
+    def _():
+        copy_out.wait()
+
+
+def gate_up(pieces, weight):
+    depth, width = weight.shape[0], weight.shape[1] // 2
+    count = sum(piece.shape[0] for piece in pieces)
+    if width % LANES:
+        hidden = jnp.concatenate(pieces, 0)
+        gate, up = multiply(hidden, weight[:, :width]), multiply(hidden, weight[:, width:])
+        return gate, up, (gate * jax.nn.sigmoid(gate) * up).astype(LOW), hidden
+    steps = width // LANES
+    there = pl.BlockSpec(memory_space=pl.ANY)
+    block = pl.BlockSpec((count, LANES), lambda j: (0, j))
+    return pl.pallas_call(
+        gate_up_kernel,
+        grid=(steps,),
+        in_specs=[
+            pl.BlockSpec((depth, LANES), lambda j: (0, j)),
+            pl.BlockSpec((depth, LANES), lambda j: (0, j + steps)),
+        ]
+        + [there] * len(pieces),
+        out_specs=[block, block, block, there],
+        out_shape=[
+            jax.ShapeDtypeStruct((count, width), WIDE),
+            jax.ShapeDtypeStruct((count, width), WIDE),
+            jax.ShapeDtypeStruct((count, width), LOW),
+            jax.ShapeDtypeStruct((count, depth), LOW),
+        ],
+        scratch_shapes=[
+            pltpu.VMEM((count, depth), LOW),
+            pltpu.SemaphoreType.DMA((len(pieces),)),
+            pltpu.SemaphoreType.DMA,
+        ],
+        compiler_params=pltpu.CompilerParams(vmem_limit_bytes=40 << 20),
+        cost_estimate=pl.CostEstimate(
+            flops=4 * count * depth * width, bytes_accessed=36 << 20, transcendentals=count * width
+        ),
+        name="gate_up",
+    )(weight, weight, *pieces)
+
+
+def mlp_back_kernel(
+    top_ref, gate_ref, up_ref, down_ref, weight_ref, grads_ref, part_ref, down, weight, arrived
+):
+    width = gate_ref.shape[1]
+    first = pl.program_id(0) == 0
+    copy_down = pltpu.make_async_copy(down_ref, down, arrived.at[0])
+    copy_weight = pltpu.make_async_copy(weight_ref, weight, arrived.at[1])
+
+    @pl.when(first)
+    def _():
+        copy_down.start()
+        copy_weight.start()
+        copy_down.wait()
+
+    top = top_ref[...]
+    for cut in tiles(width, 2 * LANES):
+        shifted = slice(width + cut.start, width + cut.stop)
+        slope = against(top, down[cut, :])
+        gate, up = gate_ref[:, cut], up_ref[:, cut]
+        sigmoid = jax.nn.sigmoid(gate)
+        swished = gate * sigmoid
+        grads_ref[:, cut] = (slope * up * sigmoid * (1.0 + gate * (1.0 - sigmoid))).astype(LOW)
+        grads_ref[:, shifted] = (slope * swished).astype(LOW)
+
+    @pl.when(first)
+    def _():
+        copy_weight.wait()
+
+    grads = grads_ref[...]
+    for cut in tiles(part_ref.shape[1], 2 * LANES):
+        part_ref[:, cut] = against(grads, weight[cut, :]).astype(LOW)
+
+
+def mlp_back(top, gate, up, down, weight, rows):
+    count, depth = top.shape
+    width = gate.shape[1]
+    block = lambda w: pl.BlockSpec((rows, w), lambda i: (i, 0))
+    there = pl.BlockSpec(memory_space=pl.ANY)
+    return pl.pallas_call(
+        mlp_back_kernel,
+        grid=(count // rows,),
+        in_specs=[block(depth), block(width), block(width), there, there],
+        out_specs=[block(2 * width), block(depth)],
+        out_shape=[
+            jax.ShapeDtypeStruct((count, 2 * width), LOW),
+            jax.ShapeDtypeStruct((count, depth), LOW),
+        ],
+        scratch_shapes=[
+            pltpu.VMEM(down.shape, LOW),
+            pltpu.VMEM(weight.shape, LOW),
+            pltpu.SemaphoreType.DMA((2,)),
+        ],
+        compiler_params=pltpu.CompilerParams(vmem_limit_bytes=56 << 20),
+        cost_estimate=pl.CostEstimate(
+            flops=6 * count * depth * width, bytes_accessed=40 << 20, transcendentals=count * width
+        ),
+        name="mlp_back",
+    )(top, gate, up, down, weight)
+
+
+def out_back_kernel(weight_ref, attn_ref, *refs):
+    *piece_refs, grad_ref, sums_ref, rows, arrived = refs
+    copies, at = [], 0
+    for k, ref in enumerate(piece_refs):
+        here = pl.ds(at, ref.shape[0])
+        copies.append(pltpu.make_async_copy(ref, rows.at[here, :], arrived.at[k]))
+        copies[-1].start()
+        at += ref.shape[0]
+    turned_attn = attn_ref[...].T
+    for copy in copies:
+        copy.wait()
+    everything = rows[...]
+    for cut in tiles(weight_ref.shape[0], 2 * LANES):
+        grad_ref[:, cut] = against(everything, weight_ref[cut, :]).astype(LOW)
+    for cut in tiles(weight_ref.shape[1], 2 * LANES):
+        sums_ref[:, cut] = multiply(turned_attn, rows[:, cut]).astype(LOW)
+
+
+def out_back(pieces, weight, attn):
+    count, width = attn.shape
+    depth = weight.shape[1]
+    vmem = pl.BlockSpec(memory_space=pltpu.VMEM)
+    return pl.pallas_call(
+        out_back_kernel,
+        in_specs=[vmem, vmem] + [pl.BlockSpec(memory_space=pl.ANY)] * len(pieces),
+        out_specs=[vmem, vmem],
+        out_shape=[
+            jax.ShapeDtypeStruct((count, width), LOW),
+            jax.ShapeDtypeStruct((width, depth), LOW),
+        ],
+        scratch_shapes=[
+            pltpu.VMEM((count, depth), LOW),
+            pltpu.SemaphoreType.DMA((len(pieces),)),
+        ],
+        compiler_params=pltpu.CompilerParams(vmem_limit_bytes=48 << 20),
+        cost_estimate=pl.CostEstimate(
+            flops=4 * count * depth * width, bytes_accessed=16 << 20, transcendentals=0
+        ),
+        name="out_back",
+    )(weight, attn, *pieces)
 
 
 def norm_scale(values):
@@ -514,23 +704,23 @@
         )
 
     cuts = model_width // query_width
+    gathered_out = dp_gather(w_out)
     parts_qkv = exchanged(pick_attn)
-    parts_qkv, (block_out, x_low, columns) = tied_lists(
-        parts_qkv,
-        [regrouped(w_out), x_low, spread(w_gate, w_up, dp_size, ctx_size, ff_chunk)],
+    parts_qkv, (x_low, columns) = tied_lists(
+        parts_qkv, [x_low, spread(w_gate, w_up, dp_size, ctx_size, ff_chunk)]
     )
     block_qkv = jnp.concatenate(in_rank_order(parts_qkv), 0)
-    gathered_attn = dp_gather(fold(block_qkv, block_out, 1))
-    x_parts, _ = ctx_gather(x_low)
-    x_parts, (columns,) = tied_lists(x_parts, [columns])
-    x_all = jnp.concatenate(x_parts, 0)
+    gathered_qkv = dp_gather(block_qkv)
     parts_gate_up = exchanged(
         lambda rank: lax.dynamic_index_in_dim(columns, rank, 0, keepdims=False)
     )
-    gathered_qkv, part_out = unfold(gathered_attn, query_width, cuts, dp_size)
-    part_qkv = gathered_qkv[:, :qkv_width]
-    gains = gathered_qkv[:, qkv_width:].astype(WIDE).T
-    gain_attn, gain_mlp = gains[0], gains[1]
+    x_parts, _ = ctx_gather(x_low)
+    out_rows = gathered_out.shape[0] // ctx_size
+    x_parts, (gathered_out,) = tied_lists(x_parts, [gathered_out])
+    parts_out = exchanged(
+        lambda rank: lax.dynamic_slice_in_dim(gathered_out, rank * out_rows, out_rows, 0)
+    )
+    x_all = jnp.concatenate(x_parts, 0)
 
     sent = block_qkv.reshape(ctx_size, gain_rows, -1)[:, :, qkv_width + 2 :].astype(WIDE)
     sent = LANES * sent[..., :position_width] + sent[..., position_width : 2 * position_width]
@@ -547,41 +737,40 @@
     order = jnp.concatenate([block_order[r] for r in ranks])
 
     x_wide = x_all.astype(WIDE)
-    normed_attn = x_wide * norm_scale(x_wide)
+    scale_all = norm_scale(x_wide)
+    parts_gate_up, (cosine, sine, scale_all) = tied_lists(parts_gate_up, [cosine, sine, scale_all])
+    gathered_qkv, block_gate_up = tied(
+        gathered_qkv, jnp.concatenate(in_rank_order(parts_gate_up), 0)
+    )
+    part_gate_up = dp_gather(block_gate_up)
+    part_qkv = gathered_qkv[:, :qkv_width]
+    gains = gathered_qkv[:, qkv_width:].astype(WIDE).T
+    gain_attn, gain_mlp = gains[0], gains[1]
+    normed_attn = x_wide * scale_all
     hidden_attn = (normed_attn * gain_attn).astype(LOW)
-    (qkv,), parts_gate_up = tied_lists([multiply(hidden_attn, part_qkv)], parts_gate_up)
-    part_gate_up = dp_gather(jnp.concatenate(in_rank_order(parts_gate_up), 0))
+    qkv = multiply(hidden_attn, part_qkv)
+    x_rows = x_low.astype(WIDE)
+
     attn_low, rotated, keys, values, log_total = attend(order, qkv, cosine, sine, block_rows)
-    part_mixed = multiply(attn_low, part_out).astype(LOW)
-
-    x_rows = x_low.astype(WIDE)
-    mixed, _ = ctx_scatter_sum(part_mixed)
-    middle, w_down = tied(x_rows + mixed, w_down)
+    (attn_low,), parts_out = tied_lists([attn_low], parts_out)
+    part_out = placed_by_rank(parts_out, dp_size // ctx_size)
+    mixed, _ = ctx_scatter_sum(multiply(attn_low, part_out).astype(LOW))
+    middle = x_rows + mixed
+    middle, w_down = tied(middle, w_down)
     part_down = dp_gather(w_down)
     scale_mlp = norm_scale(middle)
     normed_mlp = middle * scale_mlp
     hidden_parts, _ = ctx_gather((normed_mlp * gain_mlp).astype(LOW))
     hidden_parts, (grad_top,) = tied_lists(hidden_parts, [grad_top])
-    hidden_mlp = jnp.concatenate(hidden_parts, 0)
-    gate_rows = multiply(hidden_mlp, part_gate_up[:, :ff_width])
-    up_rows = multiply(hidden_mlp, part_gate_up[:, ff_width:])
-    sigmoid_gate = jax.nn.sigmoid(gate_rows)
-    swished = gate_rows * sigmoid_gate
-    top_parts, (gate_rows, activated) = ctx_gather(
-        grad_top, [gate_rows], [(swished * up_rows).astype(LOW)]
+    top_parts, (gate_rows, up_rows, activated, hidden_mlp) = ctx_gather(
+        grad_top, gate_up(hidden_parts, part_gate_up)
     )
     top_all = jnp.concatenate(top_parts, 0)
     part_down_w, part_down = tied(outer_sum(activated, top_all).astype(LOW), part_down)
     grad_down = dp_scatter_sum(part_down_w)
 
-    grad_activated = against(top_all, part_down)
-    grad_gate = (
-        grad_activated * up_rows * sigmoid_gate * (1.0 + gate_rows * (1.0 - sigmoid_gate))
-    ).astype(LOW)
-    grad_up = (grad_activated * swished).astype(LOW)
-    grad_gate_up = jnp.concatenate([grad_gate, grad_up], 1)
-    part_hidden_mlp, grad_gate_up = tied(
-        against(grad_gate_up, part_gate_up).astype(LOW), grad_gate_up
+    grad_gate_up, part_hidden_mlp = mlp_back(
+        top_all, gate_rows, up_rows, part_down, part_gate_up, row_count
     )
     grad_hidden_mlp, (part_gate_up_w,) = ctx_scatter_sum(
         part_hidden_mlp, [outer_sum(hidden_mlp, grad_gate_up).astype(LOW)]
@@ -593,25 +782,33 @@
     branch_parts, (part_result, grad_down) = ctx_gather(
         grad_middle.astype(LOW), [multiply(activated, part_down).astype(LOW)], [grad_down]
     )
-    grad_branch = jnp.concatenate(branch_parts, 0)
-    grad_attn, part_result = tied(against(grad_branch, part_out).astype(LOW), part_result)
+    grad_attn, part_out_w = out_back(branch_parts, part_out, attn_low)
+    split_out = part_out_w.reshape(dp_size // ctx_size, ctx_size, -1, model_width)
+    parts_out_w = exchanged(
+        lambda rank: lax.dynamic_index_in_dim(split_out, rank, 1, keepdims=False)
+    )
+    grad_attn, part_result = tied(grad_attn, part_result)
     grad_qkv = attend_back(
         order, rotated, grad_attn, attn_low, log_total, keys, values, cosine, sine, block_rows
     )
-    part_result, (grad_qkv,) = ctx_scatter_sum(part_result, [grad_qkv])
+    part_result, (grad_qkv, *parts_out_w) = ctx_scatter_sum(
+        part_result, [grad_qkv], parts_out_w
+    )
+    part_out_w = jnp.stack(in_rank_order(parts_out_w)).reshape(-1, model_width)
     outputs = (middle + part_result).astype(LOW).reshape(inputs.shape)
     part_hidden_attn = against(grad_qkv, part_qkv)
     gain_attn_grad = jnp.sum(part_hidden_attn * normed_attn, 0)
     gain_grads = jnp.pad(
         jnp.stack([gain_attn_grad, gain_mlp_grad], 1).astype(LOW), ((0, 0), (0, LANES - 2))
     )
-    part_hidden_attn, grad_qkv, outputs = tied(part_hidden_attn.astype(LOW), grad_qkv, outputs)
     part_qkv_w = jnp.concatenate([outer_sum(hidden_attn, grad_qkv).astype(LOW), gain_grads], 1)
-    part_out_w = outer_sum(attn_low, grad_branch).astype(LOW)
-    grad_hidden_attn, (part_attn_w,) = ctx_scatter_sum(
-        part_hidden_attn, [fold(part_qkv_w, part_out_w, dp_size)]
+    part_attn_w, part_hidden_attn, outputs = tied(
+        fold(part_qkv_w, part_out_w, dp_size), part_hidden_attn.astype(LOW), outputs
     )
     grad_attn_w = dp_scatter_sum(part_attn_w)
+    grad_hidden_attn, (grad_gate_up_w,) = ctx_scatter_sum(
+        part_hidden_attn, (), [grad_gate_up_w]
+    )
     scale_attn = norm_scale(x_rows)
     _, grad_in_norm = norm_back(grad_hidden_attn, x_rows * scale_attn, scale_attn, gain_attn)
     grad_inputs = (grad_middle + grad_in_norm).reshape(inputs.shape)
@@ -621,7 +818,7 @@
     out_down = grad_down.astype(WIDE)
     grad_attn_w, out_gate, out_up, grad_inputs = tied(grad_attn_w, out_gate, out_up, grad_inputs)
     grad_qkv_w, grad_out_w = unfold(grad_attn_w, query_width, cuts, 1)
-    out_out = regrouped(grad_out_w, back=True).astype(WIDE)
+    out_out = grad_out_w.astype(WIDE)
     qkv_rows = columns_to_rows(grad_qkv_w)
     out_query = jnp.concatenate([part[:, :query_width] for part in qkv_rows], 1).astype(WIDE)
     rests = [part[:, query_width:].astype(WIDE) for part in qkv_rows]

time: 576 us -> 532 us (0.924)
  the two profiles are of different devices: /device:TPU:6 before, /device:TPU:0 now
where the time goes in v3:
time: 532 us; the launch traced here: 522 us
  waiting for transfers between devices  167 us (31%)
  Pallas kernels  112 us (21%)
  starting transfers between devices  67.6 us (13%)
  local copies, waits for them, and re-layouts  57.9 us (11%)
  matrix products  56.1 us (11%)
  other arithmetic  46.2 us (9%)
  between operations  15.5 us (3%)
    ppermute x58, waiting for transfers between devices, swapped(): return lax.ppermute(block, axis, route)  166 us
    ppermute x58, starting transfers between devices, swapped(): return lax.ppermute(block, axis, route)  67.3 us
    unnamed x133, local copies, waits for them, and re-layouts  37.8 us
    pallas_call x1, Pallas kernels, attend_back(): pl.pallas_call(functools.partial(attend_back_kernel, pairs, 2 * rows), gr...  30.9 us
    dot_general x3, matrix products, outer_sum(): lax.dot_general(left, right, (((0,), (0,)), ((), ())), preferred_element_...  30.6 us
    pallas_call x1, Pallas kernels, mlp_back(): pl.pallas_call(mlp_back_kernel, grid=(count // rows,), in_specs=[block(de...  29.1 us
    dot_general x3, matrix products, multiply(): return jnp.dot(left, right, preferred_element_type=WIDE)  18.9 us
    pallas_call x1, Pallas kernels, gate_up(): pl.pallas_call(gate_up_kernel, grid=(steps,), in_specs=[pl.BlockSpec((dep...  18.9 us
  transfers between devices with their start and end apart: 65, of which 32 were waited for; matrix products, arithmetic and copies ran while one was open for 25% of the time, Pallas kernels for 21%

profile of v3, /device:TPU:0, one launch (start us, length us, event | category | flops | bytes accessed | tf_op | source)
XLA Modules:
  0.0 522.5 jit_solution(12635163012861459191)
XLA Ops:
  30.6 10.5 %collective-permute-done.4 = bf16[128,2048]{1,0:T(8,128)(2,1)} collective-permute-done((bf16[128,2048]{1,0:T(8,128)(2,1)}, bf16[128,2048]{1,0:T(8,128)(2,1)}, u32[]{:S(2)}, u32[]{:S(2)}) %collective-permute-start.4) | collective-permute-done | bytes 524320 | tf_op jit(solution)/shard_map/ppermute | solution.py:37
  41.1 7.7 %collective-permute-done.3 = bf16[128,2048]{1,0:T(8,128)(2,1)} collective-permute-done((bf16[128,2048]{1,0:T(8,128)(2,1)}, bf16[128,2048]{1,0:T(8,128)(2,1)}, u32[]{:S(2)}, u32[]{:S(2)}) %collective-permute-start.3) | collective-permute-done | bytes 524320 | tf_op jit(solution)/shard_map/ppermute | solution.py:37
  58.2 11.9 %collective-permute-done.7 = bf16[128,2048]{1,0:T(8,128)(2,1)S(1)} collective-permute-done((bf16[128,2048]{1,0:T(8,128)(2,1)}, bf16[128,2048]{1,0:T(8,128)(2,1)S(1)}, u32[]{:S(2)}, u32[]{:S(2)}) %collective-permute-start.7) | collective-permute-done | bytes 524320 | tf_op jit(solution)/shard_map/ppermute | solution.py:37
  91.6 8.0 %fusion.11.q_ref.kv_ref = f32[1024,640]{1,0:T(8,128)} fusion(bf16[2048,768]{1,0:T(8,128)(2,1)S(1)} %copy-done.54, bf16[1024,2048]{1,0:T(8,128)(2,1)} %copy-done.42, f32[2048]{0:T(1024)S(1)} %get-tuple-element.252, f32[1024]{0:T(1024)S(1)} %add_rsqrt_fusion), kind=kOutput, calls=%fused_computation.22 | convolution fusion | flops 2692743168 | bytes 9449472 | tf_op jit(solution)/shard_map/dot_general | solution.py:24
  99.6 17.2 %attend.1 = (bf16[1024,512]{1,0:T(8,128)(2,1)S(1)}, bf16[1024,512]{1,0:T(8,128)(2,1)S(1)}, bf16[1024,128]{1,0:T(8,128)(2,1)S(1)}, bf16[1024,128]{1,0:T(8,128)(2,1)S(1)}, f32[1024,128]{1,0:T(8,128)S(1)}) custom-call(s32[8]{0:T(128)S(1)} %pad_add_fusion.order, f32[1024,640]{1,0:T(8,128)} %fusion.11.q_ref.kv_ref, f32[1024,640]{1,0:T(8,128)} %fusion.11.q_ref.kv_ref, ...), custom_call_target="tpu_custom_call" | custom-call | flops 2147483648 | bytes 8388608 | tf_op jit(solution)/shard_map/attend/pallas_call | solution.py:306
  130.4 21.0 %collective-permute-done.15 = bf16[2,256,1024]{2,1,0:T(8,128)(2,1)S(1)} collective-permute-done((bf16[2,256,1024]{2,1,0:T(8,128)(2,1)S(1)}, bf16[2,256,1024]{2,1,0:T(8,128)(2,1)S(1)}, u32[]{:S(2)}, u32[]{:S(2)}) %collective-permute-start.15) | collective-permute-done | bytes 1048608 | tf_op jit(solution)/shard_map/ppermute | solution.py:37
  155.7 9.1 %collective-permute-done.18 = bf16[256,1024]{1,0:T(8,128)(2,1)S(1)} collective-permute-done((bf16[256,1024]{1,0:T(8,128)(2,1)S(1)}, bf16[256,1024]{1,0:T(8,128)(2,1)S(1)}, u32[]{:S(2)}, u32[]{:S(2)}) %collective-permute-start.18) | collective-permute-done | bytes 524320 | tf_op jit(solution)/shard_map/ppermute | solution.py:37
  171.7 10.8 %collective-permute-done.20.refs_4_ = bf16[128,2048]{1,0:T(8,128)(2,1)S(1)} collective-permute-done((bf16[128,2048]{1,0:T(8,128)(2,1)S(1)}, bf16[128,2048]{1,0:T(8,128)(2,1)S(1)}, u32[]{:S(2)}, u32[]{:S(2)}) %collective-permute-start.20) | collective-permute-done | bytes 524320 | tf_op jit(solution)/shard_map/ppermute | solution.py:37
  186.2 9.3 %collective-permute-done.21.refs_2_ = bf16[128,2048]{1,0:T(8,128)(2,1)S(1)} collective-permute-done((bf16[128,2048]{1,0:T(8,128)(2,1)S(1)}, bf16[128,2048]{1,0:T(8,128)(2,1)S(1)}, u32[]{:S(2)}, u32[]{:S(2)}) %collective-permute-start.21) | collective-permute-done | bytes 524320 | tf_op jit(solution)/shard_map/ppermute | solution.py:37
  195.5 5.4 %collective-permute-done.23.refs_5_ = bf16[128,2048]{1,0:T(8,128)(2,1)S(1)} collective-permute-done((bf16[128,2048]{1,0:T(8,128)(2,1)S(1)}, bf16[128,2048]{1,0:T(8,128)(2,1)S(1)}, u32[]{:S(2)}, u32[]{:S(2)}) %collective-permute-start.23) | collective-permute-done | bytes 524320 | tf_op jit(solution)/shard_map/ppermute | solution.py:37
  210.4 18.9 %gate_up.1 = (f32[1024,1408]{1,0:T(8,128)}, f32[1024,1408]{1,0:T(8,128)}, bf16[1024,1408]{1,0:T(8,128)(2,1)S(1)}, bf16[1024,2048]{1,0:T(8,128)(2,1)S(1)}) custom-call(bf16[2048,2816]{1,0:T(8,128)(2,1)} %all-gather.9.cloned.1.call-done.gate_w_ref.up_w_ref.weight_ref, bf16[2048,2816]{1,0:T(8,128)(2,1)} %all-gather.9.cloned.1.call-done.gate_w_ref.up_w_ref.weight_ref, ...), custom_call_target="tpu_custom_call" | custom-call | flops 11811160064 | bytes 37748736 | tf_op jit(solution)/shard_map/gate_up/pallas_call | solution.py:504
  235.0 5.7 %collective-permute-done.29 = bf16[128,2048]{1,0:T(8,128)(2,1)S(1)} collective-permute-done((bf16[128,2048]{1,0:T(8,128)(2,1)}, bf16[128,2048]{1,0:T(8,128)(2,1)S(1)}, u32[]{:S(2)}, u32[]{:S(2)}) %collective-permute-start.29) | collective-permute-done | bytes 524320 | tf_op jit(solution)/shard_map/ppermute | solution.py:37
  247.2 8.1 %convolution_convert_fusion.1 = bf16[1408,2048]{1,0:T(8,128)(2,1)} fusion(bf16[1024,1408]{1,0:T(8,128)(2,1)S(1)} %get-tuple-element.196, bf16[1024,2048]{1,0:T(8,128)(2,1)S(1)} %constant_dynamic-update-slice_fusion.7.top_ref), kind=kOutput, calls=%fused_computation.8 | convolution fusion | flops 5908463616 | bytes 12845056 | tf_op jit(solution)/shard_map/dot_general | solution.py:32
  255.3 29.1 %mlp_back.1 = (bf16[1024,2816]{1,0:T(8,128)(2,1)}, bf16[1024,2048]{1,0:T(8,128)(2,1)}) custom-call(bf16[1024,2048]{1,0:T(8,128)(2,1)} %copy-done.53, f32[1024,1408]{1,0:T(8,128)} %get-tuple-element.194.gate_ref, f32[1024,1408]{1,0:T(8,128)} %get-tuple-element.195.up_ref, bf16[1408,2048]{1,0:T(8,128)(2,1)} %all-gather.11.cloned.1.call-done.down_ref, ...), custom_call_target="tpu_custom_call" | custom-call | flops 17716740096 | bytes 41943040 | tf_op jit(solution)/shard_map/mlp_back/pallas_call | solution.py:570
  289.8 17.3 %convolution_convert_fusion = bf16[2048,2816]{1,0:T(8,128)(2,1)} fusion(bf16[1024,2048]{1,0:T(8,128)(2,1)S(1)} %copy-done.28, bf16[1024,2816]{1,0:T(8,128)(2,1)} %get-tuple-element.201), kind=kOutput, calls=%fused_computation | convolution fusion | flops 11816927232 | bytes 21495808 | tf_op jit(solution)/shard_map/dot_general | solution.py:32
  314.0 7.1 %collective-permute-done.34 = bf16[256,1024]{1,0:T(8,128)(2,1)S(1)} collective-permute-done((bf16[256,1024]{1,0:T(8,128)(2,1)S(1)}, bf16[256,1024]{1,0:T(8,128)(2,1)S(1)}, u32[]{:S(2)}, u32[]{:S(2)}) %collective-permute-start.34) | collective-permute-done | bytes 524320 | tf_op jit(solution)/shard_map/ppermute | solution.py:37
  328.6 8.6 %convolution_convert_fusion.2 = bf16[1024,2048]{1,0:T(8,128)(2,1)} fusion(bf16[1024,1408]{1,0:T(8,128)(2,1)S(1)} %copy-done.26, bf16[1408,2048]{1,0:T(8,128)(2,1)S(1)} %bitcast.259), kind=kOutput, calls=%fused_computation.11 | convolution fusion | flops 5907677184 | bytes 12845056 | tf_op jit(solution)/shard_map/dot_general | solution.py:24
  341.8 10.3 %collective-permute-done.37.refs_2_ = bf16[128,2048]{1,0:T(8,128)(2,1)S(1)} collective-permute-done((bf16[128,2048]{1,0:T(8,128)(2,1)S(1)}, bf16[128,2048]{1,0:T(8,128)(2,1)S(1)}, u32[]{:S(2)}, u32[]{:S(2)}) %collective-permute-start.37) | collective-permute-done | bytes 524320 | tf_op jit(solution)/shard_map/ppermute | solution.py:37
  352.1 5.4 %collective-permute-done.39.refs_5_ = bf16[128,2048]{1,0:T(8,128)(2,1)S(1)} collective-permute-done((bf16[128,2048]{1,0:T(8,128)(2,1)S(1)}, bf16[128,2048]{1,0:T(8,128)(2,1)S(1)}, u32[]{:S(2)}, u32[]{:S(2)}) %collective-permute-start.39) | collective-permute-done | bytes 524320 | tf_op jit(solution)/shard_map/ppermute | solution.py:37
  360.1 9.1 %out_back.1 = (bf16[1024,512]{1,0:T(8,128)(2,1)S(1)}, bf16[512,2048]{1,0:T(8,128)(2,1)}) custom-call(bf16[512,2048]{1,0:T(8,128)(2,1)} %bitcast.226, bf16[1024,512]{1,0:T(8,128)(2,1)S(1)} %copy-done.18, bf16[256,2048]{1,0:T(8,128)(2,1)} %copy-done.47, bf16[128,2048]{1,0:T(8,128)(2,1)S(1)} %collective-permute-done.35.refs_1_, ...), custom_call_target="tpu_custom_call" | custom-call | flops 4294967296 | bytes 16777216 | tf_op jit(solution)/shard_map/out_back/pallas_call | solution.py:614
  377.6 30.9 %attend_back.1 = bf16[1024,640]{1,0:T(8,128)(2,1)} custom-call(s32[8]{0:T(128)S(1)} %pad_add_fusion.order, bf16[1024,512]{1,0:T(8,128)(2,1)S(1)} %copy-done.20, bf16[1024,512]{1,0:T(8,128)(2,1)S(1)} %get-tuple-element.217.grad_ref, bf16[1024,512]{1,0:T(8,128)(2,1)S(1)} %copy-done.18, f32[1024,128]{1,0:T(8,128)S(1)} %copy-done.22, ...), custom_call_target="tpu_custom_call" | custom-call | flops 5368709120 | bytes 8388608 | tf_op jit(solution)/shard_map/attend_back/pallas_call | solution.py:334
  411.3 6.6 %fusion.69 = (bf16[1024,2048]{1,0:T(8,128)(2,1)}, bf16[2048]{0:T(1024)(128)(2,1)S(1)}) fusion(f32[1024]{0:T(1024)S(1)} %add_rsqrt_fusion, bf16[1024,2048]{1,0:T(8,128)(2,1)S(1)} %copy-done.43, bf16[1024,640]{1,0:T(8,128)(2,1)} %attend_back.1, bf16[2048,768]{1,0:T(8,128)(2,1)S(1)} %copy-done.55), kind=kOutput, calls=%fused_computation.247 | convolution fusion | flops 2694838272 | bytes 12328960 | tf_op jit(solution)/shard_map/dot_general | solution.py:28
  445.2 16.2 %collective-permute-done.48 = bf16[2,256,1024]{2,1,0:T(8,128)(2,1)S(1)} collective-permute-done((bf16[2,256,1024]{2,1,0:T(8,128)(2,1)S(1)}, bf16[2,256,1024]{2,1,0:T(8,128)(2,1)S(1)}, u32[]{:S(2)}, u32[]{:S(2)}) %collective-permute-start.48) | collective-permute-done | bytes 1048608 | tf_op jit(solution)/shard_map/ppermute | solution.py:37
  468.4 10.5 %collective-permute-done.51 = bf16[256,1024]{1,0:T(8,128)(2,1)S(1)} collective-permute-done((bf16[256,1024]{1,0:T(8,128)(2,1)S(1)}, bf16[256,1024]{1,0:T(8,128)(2,1)S(1)}, u32[]{:S(2)}, u32[]{:S(2)}) %collective-permute-start.51) | collective-permute-done | bytes 524320 | tf_op jit(solution)/shard_map/ppermute | solution.py:37
  (382 shorter events, 212.1 us)
Async XLA Ops:
  7.2 62.9 %all-gather.5.cloned.1.call-start = ((), (), s32[]{:S(2)}) async-start(), calls=%async_computation.3 | async-start | bytes 2359296 | tf_op jit(solution)/shard_map/all_gather | solution.py:119
  7.9 74.2 %all-gather.7.cloned.1.call-start = ((), (), s32[]{:S(2)}) async-start(), calls=%async_computation.4 | async-start | bytes 3538944 | tf_op jit(solution)/shard_map/all_gather | solution.py:119
  23.2 185.1 %all-gather.9.cloned.1.call-start = ((), (), s32[]{:S(2)}) async-start(), calls=%async_computation.5 | async-start | bytes 12976128 | tf_op jit(solution)/shard_map/all_gather | solution.py:119
  24.3 30.7 %collective-permute-start.5 = (bf16[128,2048]{1,0:T(8,128)(2,1)}, bf16[128,2048]{1,0:T(8,128)(2,1)}, u32[]{:S(2)}, u32[]{:S(2)}) collective-permute-start(bf16[128,2048]{1,0:T(8,128)(2,1)} %get-tuple-element.331), channel_id=1, source_target_pairs={{0,1},{1,0},{2,3},{3,2},{4,5},{5,4},{6,7},{7,6},{8,9},{9,8},{10,11... | collective-permute-start | bytes 1572872 | tf_op jit(solution)/shard_map/ppermute | solution.py:37
  27.1 29.8 %collective-permute-start.6 = (bf16[128,2048]{1,0:T(8,128)(2,1)}, bf16[128,2048]{1,0:T(8,128)(2,1)}, u32[]{:S(2)}, u32[]{:S(2)}) collective-permute-start(bf16[128,2048]{1,0:T(8,128)(2,1)} %get-tuple-element.332), channel_id=1, source_target_pairs={{0,2},{1,3},{2,0},{3,1},{4,6},{5,7},{6,4},{7,5},{8,10},{9,11},{10,... | collective-permute-start | bytes 1572872 | tf_op jit(solution)/shard_map/ppermute | solution.py:37
  52.0 25.7 %collective-permute-start.11 = (bf16[64,2816]{1,0:T(8,128)(2,1)}, bf16[64,2816]{1,0:T(8,128)(2,1)}, u32[]{:S(2)}, u32[]{:S(2)}) collective-permute-start(bf16[64,2816]{1,0:T(8,128)(2,1)} %get-tuple-element.319), channel_id=1, source_target_pairs={{0,3},{1,2},{2,1},{3,0},{4,7},{5,6},{6,5},{7,4},{8,11},{9,10},{10,... | collective-permute-start | bytes 1081352 | tf_op jit(solution)/shard_map/ppermute | solution.py:37
  82.1 173.2 %all-gather.11.cloned.1.call-start = ((), (), s32[]{:S(2)}) async-start(), calls=%async_computation.6 | async-start | bytes 6488064 | tf_op jit(solution)/shard_map/all_gather | solution.py:119
  84.2 35.1 %collective-permute-start.14 = (bf16[128,2048]{1,0:T(8,128)(2,1)}, bf16[128,2048]{1,0:T(8,128)(2,1)S(1)}, u32[]{:S(2)}, u32[]{:S(2)}) collective-permute-start(bf16[128,2048]{1,0:T(8,128)(2,1)} %get-tuple-element.303), channel_id=1, source_target_pairs={{0,3},{1,2},{2,1},{3,0},{4,7},{5,6},{6,5},{7,4},{8,11},{9,10},{10,... | collective-permute-start | bytes 1572872 | tf_op jit(solution)/shard_map/ppermute | solution.py:37
  85.7 34.4 %collective-permute-start.13 = (bf16[128,2048]{1,0:T(8,128)(2,1)}, bf16[128,2048]{1,0:T(8,128)(2,1)S(1)}, u32[]{:S(2)}, u32[]{:S(2)}) collective-permute-start(bf16[128,2048]{1,0:T(8,128)(2,1)} %get-tuple-element.304), channel_id=1, source_target_pairs={{0,2},{1,3},{2,0},{3,1},{4,6},{5,7},{6,4},{7,5},{8,10},{9,11},{10,... | collective-permute-start | bytes 1572872 | tf_op jit(solution)/shard_map/ppermute | solution.py:37
  86.6 34.3 %collective-permute-start.12 = (bf16[128,2048]{1,0:T(8,128)(2,1)}, bf16[128,2048]{1,0:T(8,128)(2,1)S(1)}, u32[]{:S(2)}, u32[]{:S(2)}) collective-permute-start(bf16[128,2048]{1,0:T(8,128)(2,1)} %get-tuple-element.305), channel_id=1, source_target_pairs={{0,1},{1,0},{2,3},{3,2},{4,5},{5,4},{6,7},{7,6},{8,9},{9,8},{10,11... | collective-permute-start | bytes 1572872 | tf_op jit(solution)/shard_map/ppermute | solution.py:37
  166.2 192.6 %reduce-scatter.4.cloned.1.call-start = ((), (), s32[]{:S(2)}) async-start(), calls=%async_computation.7 | async-start | bytes 6488064 | tf_op jit(solution)/shard_map/reduce_scatter | solution.py:123
  171.0 24.5 %collective-permute-start.21 = (bf16[128,2048]{1,0:T(8,128)(2,1)S(1)}, bf16[128,2048]{1,0:T(8,128)(2,1)S(1)}, u32[]{:S(2)}, u32[]{:S(2)}) collective-permute-start(bf16[128,2048]{1,0:T(8,128)(2,1)S(1)} %get-tuple-element.329), channel_id=1, source_target_pairs={{0,1},{1,0},{2,3},{3,2},{4,5},{5,4},{6,7},{7,6},{8,9},{9,8},{10,11... | collective-permute-start | bytes 1572872 | tf_op jit(solution)/shard_map/ppermute | solution.py:37
  171.4 24.1 %collective-permute-start.22 = (bf16[128,2048]{1,0:T(8,128)(2,1)S(1)}, bf16[128,2048]{1,0:T(8,128)(2,1)S(1)}, u32[]{:S(2)}, u32[]{:S(2)}) collective-permute-start(bf16[128,2048]{1,0:T(8,128)(2,1)S(1)} %get-tuple-element.330), channel_id=1, source_target_pairs={{0,2},{1,3},{2,0},{3,1},{4,6},{5,7},{6,4},{7,5},{8,10},{9,11},{10,... | collective-permute-start | bytes 1572872 | tf_op jit(solution)/shard_map/ppermute | solution.py:37
  204.2 30.8 %collective-permute-start.27 = (bf16[128,2048]{1,0:T(8,128)(2,1)}, bf16[128,2048]{1,0:T(8,128)(2,1)}, u32[]{:S(2)}, u32[]{:S(2)}) collective-permute-start(bf16[128,2048]{1,0:T(8,128)(2,1)} %get-tuple-element.327), channel_id=1, source_target_pairs={{0,1},{1,0},{2,3},{3,2},{4,5},{5,4},{6,7},{7,6},{8,9},{9,8},{10,11... | collective-permute-start | bytes 1572872 | tf_op jit(solution)/shard_map/ppermute | solution.py:37
  205.7 25.6 %collective-permute-start.26 = (bf16[128,2048]{1,0:T(8,128)(2,1)}, bf16[128,2048]{1,0:T(8,128)(2,1)}, u32[]{:S(2)}, u32[]{:S(2)}) collective-permute-start(bf16[128,2048]{1,0:T(8,128)(2,1)} %get-tuple-element.327), channel_id=1, source_target_pairs={{0,2},{1,3},{2,0},{3,1},{4,6},{5,7},{6,4},{7,5},{8,10},{9,11},{10,... | collective-permute-start | bytes 1572872 | tf_op jit(solution)/shard_map/ppermute | solution.py:37
  206.7 28.3 %collective-permute-start.28 = (bf16[128,2048]{1,0:T(8,128)(2,1)}, bf16[128,2048]{1,0:T(8,128)(2,1)}, u32[]{:S(2)}, u32[]{:S(2)}) collective-permute-start(bf16[128,2048]{1,0:T(8,128)(2,1)} %get-tuple-element.328), channel_id=1, source_target_pairs={{0,2},{1,3},{2,0},{3,1},{4,6},{5,7},{6,4},{7,5},{8,10},{9,11},{10,... | collective-permute-start | bytes 1572872 | tf_op jit(solution)/shard_map/ppermute | solution.py:37
  207.7 23.6 %collective-permute-start.25 = (bf16[128,2048]{1,0:T(8,128)(2,1)}, bf16[128,2048]{1,0:T(8,128)(2,1)}, u32[]{:S(2)}, u32[]{:S(2)}) collective-permute-start(bf16[128,2048]{1,0:T(8,128)(2,1)} %get-tuple-element.328), channel_id=1, source_target_pairs={{0,1},{1,0},{2,3},{3,2},{4,5},{5,4},{6,7},{7,6},{8,9},{9,8},{10,11... | collective-permute-start | bytes 1572872 | tf_op jit(solution)/shard_map/ppermute | solution.py:37
  255.3 227.6 %reduce-scatter.8.cloned.1.call-start = ((), (), s32[]{:S(2)}) async-start(), calls=%async_computation.9 | async-start | bytes 12976128 | tf_op jit(solution)/shard_map/reduce_scatter | solution.py:123
  309.3 193.2 %reduce-scatter.6.cloned.1.call-start = ((), (), s32[]{:S(2)}) async-start(), calls=%async_computation.8 | async-start | bytes 5898240 | tf_op jit(solution)/shard_map/reduce_scatter | solution.py:123
  369.6 38.9 %collective-permute-start.41 = (bf16[2,256,1024]{2,1,0:T(8,128)(2,1)S(1)}, bf16[2,256,1024]{2,1,0:T(8,128)(2,1)S(1)}, u32[]{:S(2)}, u32[]{:S(2)}) collective-permute-start(bf16[2,256,1024]{2,1,0:T(8,128)(2,1)S(1)} %pad_maximum_fusion.11), channel_id=1, source_target_pairs={{0,1},{1,0},{2,3},{3,2},{4,5},{5,4},{6,7},{7,6},{8,9},{9,8},{10,11... | collective-permute-start | bytes 3145736 | tf_op jit(solution)/shard_map/ppermute | solution.py:37
  372.1 37.5 %collective-permute-start.42 = (bf16[2,256,1024]{2,1,0:T(8,128)(2,1)}, bf16[2,256,1024]{2,1,0:T(8,128)(2,1)S(1)}, u32[]{:S(2)}, u32[]{:S(2)}) collective-permute-start(bf16[2,256,1024]{2,1,0:T(8,128)(2,1)} %pad_maximum_fusion.12), channel_id=1, source_target_pairs={{0,2},{1,3},{2,0},{3,1},{4,6},{5,7},{6,4},{7,5},{8,10},{9,11},{10,... | collective-permute-start | bytes 3145736 | tf_op jit(solution)/shard_map/ppermute | solution.py:37
  374.0 57.1 %collective-permute-start.47 = (bf16[2,64,2048]{2,1,0:T(8,128)(2,1)}, bf16[2,64,2048]{2,1,0:T(8,128)(2,1)}, u32[]{:S(2)}, u32[]{:S(2)}) collective-permute-start(bf16[2,64,2048]{2,1,0:T(8,128)(2,1)} %get-tuple-element.299), channel_id=1, source_target_pairs={{0,3},{1,2},{2,1},{3,0},{4,7},{5,6},{6,5},{7,4},{8,11},{9,10},{10,... | collective-permute-start | bytes 1572872 | tf_op jit(solution)/shard_map/ppermute | solution.py:37
  375.4 55.7 %collective-permute-start.46 = (bf16[2,64,2048]{2,1,0:T(8,128)(2,1)}, bf16[2,64,2048]{2,1,0:T(8,128)(2,1)}, u32[]{:S(2)}, u32[]{:S(2)}) collective-permute-start(bf16[2,64,2048]{2,1,0:T(8,128)(2,1)} %get-tuple-element.300), channel_id=1, source_target_pairs={{0,2},{1,3},{2,0},{3,1},{4,6},{5,7},{6,4},{7,5},{8,10},{9,11},{10,... | collective-permute-start | bytes 1572872 | tf_op jit(solution)/shard_map/ppermute | solution.py:37
  376.2 55.0 %collective-permute-start.45 = (bf16[2,64,2048]{2,1,0:T(8,128)(2,1)}, bf16[2,64,2048]{2,1,0:T(8,128)(2,1)}, u32[]{:S(2)}, u32[]{:S(2)}) collective-permute-start(bf16[2,64,2048]{2,1,0:T(8,128)(2,1)} %get-tuple-element.301), channel_id=1, source_target_pairs={{0,1},{1,0},{2,3},{3,2},{4,5},{5,4},{6,7},{7,6},{8,9},{9,8},{10,11... | collective-permute-start | bytes 1572872 | tf_op jit(solution)/shard_map/ppermute | solution.py:37
  (101 other events, 908.3 us)
Sparse Core Ops, SparseCore 0:
  9.6 31.8 all-gather.4
  43.7 37.7 all-gather.6
  83.7 106.9 all-gather.8
  192.2 58.7 all-gather.10
  255.4 62.4 reduce-scatter.3
  320.1 117.6 reduce-scatter.7
  440.5 60.2 reduce-scatter.5

commit v4 on v3

--- a/solution.py
+++ b/solution.py
@@ -61,6 +61,27 @@
     second = second(*first) if callable(second) else second
     got, second = tied_lists(late + far, second)
     return [block, near[0], *got[:2], near[1], *got[2:]], first + second
+
+
+def gather_start(block):
+    if lax.axis_size("ctx") != 4:
+        return []
+    top, low = split_rows(block, 2)
+    return [swapped(top, 1), swapped(low, 2)]
+
+
+def gather_rest(block, near):
+    size = lax.axis_size("ctx")
+    if size != 4:
+        return [swapped(block, k) for k in range(1, size)]
+    top, low = split_rows(block, 2)
+    return [swapped(near[0], 2), swapped(near[1], 1), swapped(low, 1), swapped(top, 2)]
+
+
+def gather_end(block, near, rest):
+    if lax.axis_size("ctx") != 4:
+        return [block, *rest]
+    return [block, near[0], rest[2], rest[3], near[1], rest[0], rest[1]]
 
 
 def ctx_scatter_sum(values, first=(), second=()):
@@ -251,34 +272,30 @@
     queries_t = [q.T for q in queries]
     grads_t = [g.T for g in grads]
 
-    def one_chunk(c, dq, masked):
-        place_c = pl.ds(pl.multiple_of(c * chunk, chunk), chunk)
-        keys = keys_ref[place_c, :]
-        values = values_ref[place_c, :]
-        dk = dkeys[c]
-        dv = dvalues[c]
-        new = []
-        for p in range(pairs):
-            weights = jnp.exp(against(queries[p], keys) - lses[p])
-            if masked:
-                weights = jnp.where(seen(2 * rows, chunk, last_key), weights, 0.0)
-            slopes = against(grads[p], values)
-            ds = (weights * (slopes - deltas[p])).astype(LOW)
-            new.append(dq[p] + multiply(ds, keys))
-            dk = dk + multiply(queries_t[p], ds)
-            dv = dv + multiply(grads_t[p], weights.astype(LOW))
-        dkeys[c] = dk
-        dvalues[c] = dv
-        return tuple(new)
-
-    start = tuple(jnp.zeros((2 * rows, LANES), WIDE) for _ in range(pairs))
-    dq = lax.fori_loop(0, last_chunk, lambda c, d: one_chunk(c, d, False), start)
-    dq = one_chunk(last_chunk, dq, True)
     cosine, sine = cosb_ref[...], sinb_ref[...]
-    for p in range(pairs):
-        pair = one_pair(dq[p]) * scale
-        pair = pair * cosine - turned(pair) * sine
-        dqkv_ref[here, p * LANES : (p + 1) * LANES] = pair.astype(LOW)
+    for count in range(1, chunks + 1):
+
+        @pl.when(last_chunk == count - 1)
+        def _(count=count):
+            visible = seen(2 * rows, chunk, last_key)
+            for p in range(pairs):
+                dq = None
+                for c in range(count):
+                    place_c = slice(c * chunk, (c + 1) * chunk)
+                    keys = keys_ref[place_c, :]
+                    values = values_ref[place_c, :]
+                    weights = jnp.exp(against(queries[p], keys) - lses[p])
+                    if c == count - 1:
+                        weights = jnp.where(visible, weights, 0.0)
+                    slopes = against(grads[p], values)
+                    ds = (weights * (slopes - deltas[p])).astype(LOW)
+                    part = multiply(ds, keys)
+                    dq = part if dq is None else dq + part
+                    dkeys[c] += multiply(queries_t[p], ds)
+                    dvalues[c] += multiply(grads_t[p], weights.astype(LOW))
+                pair = one_pair(dq) * scale
+                pair = pair * cosine - turned(pair) * sine
+                dqkv_ref[here, p * LANES : (p + 1) * LANES] = pair.astype(LOW)
 
     @pl.when(step == steps - 1)
     def _():
@@ -318,7 +335,7 @@
             jax.ShapeDtypeStruct((seq, LANES), LOW),
             jax.ShapeDtypeStruct((seq, LANES), WIDE),
         ],
-        compiler_params=pltpu.CompilerParams(vmem_limit_bytes=48 << 20),
+        compiler_params=pltpu.CompilerParams(vmem_limit_bytes=60 << 20),
         cost_estimate=pl.CostEstimate(flops=2 * 2 * seq * seq * width, bytes_accessed=8 << 20, transcendentals=seq * seq * width // HEAD_DIM // 2),
         name="attend",
     )(order, qkv, qkv, cosine, sine, cosine, sine)
@@ -346,76 +363,128 @@
             ],
         ),
         out_shape=jax.ShapeDtypeStruct((seq, width + LANES), LOW),
-        compiler_params=pltpu.CompilerParams(vmem_limit_bytes=48 << 20),
+        compiler_params=pltpu.CompilerParams(vmem_limit_bytes=60 << 20),
         cost_estimate=pl.CostEstimate(flops=5 * 2 * seq * seq * width, bytes_accessed=8 << 20, transcendentals=seq * seq * width // HEAD_DIM // 2),
         name="attend_back",
     )(order, rotated, grad, out, lse, cosine, sine, keys, values, cosine, sine)
 
 
-def fold_kernel(count, cuts, qkv_ref, out_ref, joined_ref):
-    rows, cut = out_ref.shape[0] // count, out_ref.shape[1] // cuts
-    width = qkv_ref.shape[1]
-    joined_ref[:, :width] = qkv_ref[...]
+def attn_sums_kernel(count, me_ref, hidden_ref, grad_ref, weight_ref, slopes_ref, *refs):
+    *out_refs, joined_ref = refs
+    outer, chunk = count // len(out_refs), joined_ref.shape[0] // count
+    rows = out_refs[0].shape[0] // outer
+    cuts = chunk // rows
+    cut = out_refs[0].shape[1] // cuts
+    width = grad_ref.shape[1]
+    for k, ref in enumerate(out_refs):
+        for i in range(outer):
+            block = (me_ref[0] ^ k) * outer + i
+            for j in range(cuts):
+                there = pl.ds(pl.multiple_of(block * chunk, chunk) + j * rows, rows)
+                joined_ref[there, width + LANES :] = ref[
+                    i * rows : (i + 1) * rows, j * cut : (j + 1) * cut
+                ]
+    grad = grad_ref[...]
+    lane = lane_of((chunk, LANES))
     for d in range(count):
-        for j in range(cuts):
-            there = (d * cuts + j) * rows
-            joined_ref[there : there + rows, width:] = out_ref[
-                d * rows : (d + 1) * rows, j * cut : (j + 1) * cut
-            ]
-
-
-def fold(qkv, out, count):
-    cuts = qkv.shape[0] // out.shape[0]
-    width = qkv.shape[1] + out.shape[1] // cuts
+        here = slice(d * chunk, (d + 1) * chunk)
+        sums = lax.dot_general(
+            hidden_ref[:, here], grad, (((0,), (0,)), ((), ())), preferred_element_type=WIDE
+        )
+        joined_ref[here, :width] = sums.astype(LOW)
+        gain = weight_ref[here, width:].astype(WIDE)[:, :1]
+        slope = jnp.sum(sums * weight_ref[here, :width].astype(WIDE), 1, keepdims=True) / gain
+        both = jnp.where(lane == 0, slope, slopes_ref[here, :])
+        joined_ref[here, width : width + LANES] = both.astype(LOW)
+
+
+def attn_sums(hidden, grad, weight, slopes, parts, count):
+    depth, width = hidden.shape[1], grad.shape[1]
+    total = sum(part.shape[0] for part in parts)
+    full = width + LANES + parts[0].shape[1] * total // depth
+    vmem = pl.BlockSpec(memory_space=pltpu.VMEM)
     return pl.pallas_call(
-        functools.partial(fold_kernel, count, cuts),
-        out_shape=jax.ShapeDtypeStruct((qkv.shape[0], width), qkv.dtype),
-        compiler_params=pltpu.CompilerParams(vmem_limit_bytes=40 << 20),
-        name="fold",
-    )(qkv, out)
-
-
-def unfold_kernel(count, cuts, joined_ref, qkv_ref, out_ref):
-    rows, cut = out_ref.shape[0] // count, out_ref.shape[1] // cuts
-    width = qkv_ref.shape[1]
-    qkv_ref[...] = joined_ref[:, :width]
-    for d in range(count):
-        for j in range(cuts):
-            there = (d * cuts + j) * rows
-            out_ref[d * rows : (d + 1) * rows, j * cut : (j + 1) * cut] = joined_ref[
-                there : there + rows, width:
-            ]
-
-
-def unfold(joined, cut, cuts, count):
-    rows, width = joined.shape
+        functools.partial(attn_sums_kernel, count),
+        in_specs=[pl.BlockSpec(memory_space=pltpu.SMEM)] + [vmem] * (4 + len(parts)),
+        out_specs=vmem,
+        out_shape=jax.ShapeDtypeStruct((depth, full), LOW),
+        compiler_params=pltpu.CompilerParams(vmem_limit_bytes=60 << 20),
+        cost_estimate=pl.CostEstimate(
+            flops=2 * hidden.shape[0] * depth * width, bytes_accessed=16 << 20, transcendentals=0
+        ),
+        name="attn_sums",
+    )(lax.axis_index("ctx").reshape(1), hidden, grad, weight, slopes, *parts)
+
+
+def finish_kernel(sharers, me_ref, joined_ref, *refs):
+    *part_refs, query_ref, key_ref, value_ref, out_ref, gains_ref = refs
+    ranks = len(part_refs)
+    rows, full = part_refs[0].shape
+    width = full - LANES
+    query_width = query_ref.shape[1] // ranks
+    head_dim = (width - query_width) // 2
+    for k, ref in enumerate(part_refs):
+        there = pl.ds(pl.multiple_of((me_ref[0] ^ k) * query_width, query_width), query_width)
+        query_ref[:, there] = ref[:, :query_width].astype(WIDE)
+    rests = [ref[:, query_width:width].astype(WIDE) for ref in part_refs]
+    gains_ref[...] = sum(ref[:, width:].astype(WIDE) for ref in part_refs)
+    for group in range(ranks // sharers):
+        total = jnp.zeros((rows, 2 * head_dim), WIDE)
+        for k, rest in enumerate(rests):
+            total = total + jnp.where((me_ref[0] ^ k) // sharers == group, rest, 0.0)
+        here = slice(group * head_dim, (group + 1) * head_dim)
+        key_ref[:, here] = total[:, :head_dim]
+        value_ref[:, here] = total[:, head_dim:]
+    cut = joined_ref.shape[1] - full
+    for j in range(out_ref.shape[1] // cut):
+        out_ref[:, j * cut : (j + 1) * cut] = joined_ref[
+            j * rows : (j + 1) * rows, full:
+        ].astype(WIDE)
+
+
+def finish(joined, parts, sharers):
+    ranks, rows = len(parts), parts[0].shape[0]
+    depth = joined.shape[0] // rows * (joined.shape[1] - parts[0].shape[1])
+    head_dim = HEAD_DIM
+    query_width = parts[0].shape[1] - 2 * head_dim - LANES
+    vmem = pl.BlockSpec(memory_space=pltpu.VMEM)
+    widths = [ranks * query_width] + [ranks // sharers * head_dim] * 2 + [depth, LANES]
     return pl.pallas_call(
-        functools.partial(unfold_kernel, count, cuts),
-        out_shape=[
-            jax.ShapeDtypeStruct((rows, width - cut), joined.dtype),
-            jax.ShapeDtypeStruct((rows // cuts, cut * cuts), joined.dtype),
-        ],
-        compiler_params=pltpu.CompilerParams(vmem_limit_bytes=40 << 20),
-        name="unfold",
-    )(joined)
+        functools.partial(finish_kernel, sharers),
+        in_specs=[pl.BlockSpec(memory_space=pltpu.SMEM)] + [vmem] * (1 + ranks),
+        out_specs=[vmem] * 5,
+        out_shape=[jax.ShapeDtypeStruct((rows, width), WIDE) for width in widths],
+        name="finish",
+    )(lax.axis_index("ctx").reshape(1), joined, *parts)
 
 
 def place_kernel(outer, me_ref, *refs):
-    *part_refs, out_ref = refs
+    *part_refs, out_ref, arrived = refs
     rows = out_ref.shape[2]
-    for k, ref in enumerate(part_refs):
-        for i in range(outer):
-            out_ref[i, me_ref[0] ^ k] = ref[i * rows : (i + 1) * rows, :]
+    copies = [
+        pltpu.make_async_copy(
+            ref.at[pl.ds(i * rows, rows), :],
+            out_ref.at[i, me_ref[0] ^ k],
+            arrived.at[k * outer + i],
+        )
+        for k, ref in enumerate(part_refs)
+        for i in range(outer)
+    ]
+    for copy in copies:
+        copy.start()
+    for copy in copies:
+        copy.wait()
 
 
 def placed_by_rank(parts, outer):
     rows, width = parts[0].shape[0] // outer, parts[0].shape[1]
-    vmem = pl.BlockSpec(memory_space=pltpu.VMEM)
     out = pl.pallas_call(
         functools.partial(place_kernel, outer),
-        in_specs=[pl.BlockSpec(memory_space=pltpu.SMEM)] + [vmem] * len(parts),
-        out_specs=vmem,
+        in_specs=[pl.BlockSpec(memory_space=pltpu.SMEM)]
+        + [pl.BlockSpec(memory_space=pltpu.HBM)] * len(parts),
+        out_specs=pl.BlockSpec(memory_space=pltpu.VMEM),
         out_shape=jax.ShapeDtypeStruct((outer, len(parts), rows, width), parts[0].dtype),
+        scratch_shapes=[pltpu.SemaphoreType.DMA((outer * len(parts),))],
         compiler_params=pltpu.CompilerParams(vmem_limit_bytes=40 << 20),
         name="place",
     )(lax.axis_index("ctx").reshape(1), *parts)
@@ -508,7 +577,7 @@
             pl.BlockSpec((depth, LANES), lambda j: (0, j)),
             pl.BlockSpec((depth, LANES), lambda j: (0, j + steps)),
         ]
-        + [there] * len(pieces),
+        + [pl.BlockSpec(memory_space=pltpu.HBM)] * len(pieces),
         out_specs=[block, block, block, there],
         out_shape=[
             jax.ShapeDtypeStruct((count, width), WIDE),
@@ -521,12 +590,48 @@
             pltpu.SemaphoreType.DMA((len(pieces),)),
             pltpu.SemaphoreType.DMA,
         ],
-        compiler_params=pltpu.CompilerParams(vmem_limit_bytes=40 << 20),
+        compiler_params=pltpu.CompilerParams(vmem_limit_bytes=60 << 20),
         cost_estimate=pl.CostEstimate(
             flops=4 * count * depth * width, bytes_accessed=36 << 20, transcendentals=count * width
         ),
         name="gate_up",
     )(weight, weight, *pieces)
+
+
+def down_sums_kernel(active_ref, *refs):
+    *piece_refs, sums_ref, rows_ref, arrived = refs
+    copies, at = [], 0
+    for k, ref in enumerate(piece_refs):
+        here = pl.ds(at, ref.shape[0])
+        copies.append(pltpu.make_async_copy(ref, rows_ref.at[here, :], arrived.at[k]))
+        copies[-1].start()
+        at += ref.shape[0]
+    turned_active = active_ref[...].T
+    for copy in copies:
+        copy.wait()
+    for cut in tiles(sums_ref.shape[1], 2 * LANES):
+        sums_ref[:, cut] = multiply(turned_active, rows_ref[:, cut]).astype(LOW)
+
+
+def down_sums(active, pieces):
+    count, width = active.shape
+    depth = pieces[0].shape[1]
+    vmem = pl.BlockSpec(memory_space=pltpu.VMEM)
+    return pl.pallas_call(
+        down_sums_kernel,
+        in_specs=[vmem] + [pl.BlockSpec(memory_space=pl.ANY)] * len(pieces),
+        out_specs=[vmem, vmem],
+        out_shape=[
+            jax.ShapeDtypeStruct((width, depth), LOW),
+            jax.ShapeDtypeStruct((count, depth), LOW),
+        ],
+        scratch_shapes=[pltpu.SemaphoreType.DMA((len(pieces),))],
+        compiler_params=pltpu.CompilerParams(vmem_limit_bytes=60 << 20),
+        cost_estimate=pl.CostEstimate(
+            flops=2 * count * depth * width, bytes_accessed=18 << 20, transcendentals=0
+        ),
+        name="down_sums",
+    )(active, *pieces)
 
 
 def mlp_back_kernel(
@@ -581,7 +686,7 @@
             pltpu.VMEM(weight.shape, LOW),
             pltpu.SemaphoreType.DMA((2,)),
         ],
-        compiler_params=pltpu.CompilerParams(vmem_limit_bytes=56 << 20),
+        compiler_params=pltpu.CompilerParams(vmem_limit_bytes=60 << 20),
         cost_estimate=pl.CostEstimate(
             flops=6 * count * depth * width, bytes_accessed=40 << 20, transcendentals=count * width
         ),
@@ -613,7 +718,7 @@
     vmem = pl.BlockSpec(memory_space=pltpu.VMEM)
     return pl.pallas_call(
         out_back_kernel,
-        in_specs=[vmem, vmem] + [pl.BlockSpec(memory_space=pl.ANY)] * len(pieces),
+        in_specs=[vmem, vmem] + [pl.BlockSpec(memory_space=pltpu.HBM)] * len(pieces),
         out_specs=[vmem, vmem],
         out_shape=[
             jax.ShapeDtypeStruct((count, width), LOW),
@@ -623,7 +728,7 @@
             pltpu.VMEM((count, depth), LOW),
             pltpu.SemaphoreType.DMA((len(pieces),)),
         ],
-        compiler_params=pltpu.CompilerParams(vmem_limit_bytes=48 << 20),
+        compiler_params=pltpu.CompilerParams(vmem_limit_bytes=60 << 20),
         cost_estimate=pl.CostEstimate(
             flops=4 * count * depth * width, bytes_accessed=16 << 20, transcendentals=0
         ),
@@ -642,6 +747,34 @@
         gain_grad,
         scale_rows * (scaled - normed * jnp.mean(scaled * normed, -1, keepdims=True)),
     )
+
+
+def join_kernel(me_ref, *refs):
+    *block_refs, out_ref = refs
+    count = len(block_refs) // 2
+    for k in range(count):
+        out_ref[me_ref[0] ^ (2 * k)] = block_refs[k][...]
+        out_ref[me_ref[0] ^ (2 * k + 1)] = block_refs[count + k][...]
+
+
+def dp_blocks(block):
+    return [block] + [swapped(block, 2 * k, "dp") for k in range(1, lax.axis_size("dp") // 2)]
+
+
+def dp_joined(blocks):
+    rows, width = blocks[0].shape
+    count = 2 * len(blocks)
+    others = [swapped(block, 1, "dp") for block in blocks]
+    vmem = pl.BlockSpec(memory_space=pltpu.VMEM)
+    out = pl.pallas_call(
+        join_kernel,
+        in_specs=[pl.BlockSpec(memory_space=pltpu.SMEM)] + [vmem] * count,
+        out_specs=vmem,
+        out_shape=jax.ShapeDtypeStruct((count, rows, width), blocks[0].dtype),
+        compiler_params=pltpu.CompilerParams(vmem_limit_bytes=40 << 20),
+        name="join",
+    )(lax.axis_index("dp").reshape(1), *blocks, *others)
+    return out.reshape(count * rows, width)
 
 
 def split_rows(values, count):
@@ -704,7 +837,7 @@
         )
 
     cuts = model_width // query_width
-    gathered_out = dp_gather(w_out)
+    blocks_out = dp_blocks(w_out)
     parts_qkv = exchanged(pick_attn)
     parts_qkv, (x_low, columns) = tied_lists(
         parts_qkv, [x_low, spread(w_gate, w_up, dp_size, ctx_size, ff_chunk)]
@@ -714,12 +847,12 @@
     parts_gate_up = exchanged(
         lambda rank: lax.dynamic_index_in_dim(columns, rank, 0, keepdims=False)
     )
-    x_parts, _ = ctx_gather(x_low)
-    out_rows = gathered_out.shape[0] // ctx_size
-    x_parts, (gathered_out,) = tied_lists(x_parts, [gathered_out])
-    parts_out = exchanged(
-        lambda rank: lax.dynamic_slice_in_dim(gathered_out, rank * out_rows, out_rows, 0)
-    )
+    x_parts, (block_gate_up,) = ctx_gather(
+        x_low, [jnp.concatenate(in_rank_order(parts_gate_up), 0)]
+    )
+    part_gate_up = dp_gather(block_gate_up)
+    x_parts[-1], grad_top = tied(x_parts[-1], grad_top)
+    near = gather_start(grad_top)
     x_all = jnp.concatenate(x_parts, 0)
 
     sent = block_qkv.reshape(ctx_size, gain_rows, -1)[:, :, qkv_width + 2 :].astype(WIDE)
@@ -738,11 +871,15 @@
 
     x_wide = x_all.astype(WIDE)
     scale_all = norm_scale(x_wide)
-    parts_gate_up, (cosine, sine, scale_all) = tied_lists(parts_gate_up, [cosine, sine, scale_all])
-    gathered_qkv, block_gate_up = tied(
-        gathered_qkv, jnp.concatenate(in_rank_order(parts_gate_up), 0)
-    )
-    part_gate_up = dp_gather(block_gate_up)
+    (gathered_qkv, cosine, sine, scale_all), waited = tied_lists(
+        [gathered_qkv, cosine, sine, scale_all], [*blocks_out, *near]
+    )
+    blocks_out, near = waited[: len(blocks_out)], waited[len(blocks_out) :]
+    gathered_out = dp_joined(blocks_out)
+    out_rows = gathered_out.shape[0] // ctx_size
+    parts_out = exchanged(
+        lambda rank: lax.dynamic_slice_in_dim(gathered_out, rank * out_rows, out_rows, 0)
+    )
     part_qkv = gathered_qkv[:, :qkv_width]
     gains = gathered_qkv[:, qkv_width:].astype(WIDE).T
     gain_attn, gain_mlp = gains[0], gains[1]
@@ -761,12 +898,14 @@
     scale_mlp = norm_scale(middle)
     normed_mlp = middle * scale_mlp
     hidden_parts, _ = ctx_gather((normed_mlp * gain_mlp).astype(LOW))
-    hidden_parts, (grad_top,) = tied_lists(hidden_parts, [grad_top])
-    top_parts, (gate_rows, up_rows, activated, hidden_mlp) = ctx_gather(
-        grad_top, gate_up(hidden_parts, part_gate_up)
-    )
-    top_all = jnp.concatenate(top_parts, 0)
-    part_down_w, part_down = tied(outer_sum(activated, top_all).astype(LOW), part_down)
+    hidden_parts[2], grad_top, *near = tied(hidden_parts[2], grad_top, *near)
+    rest = gather_rest(grad_top, near)
+    rest, (gate_rows, up_rows, activated, hidden_mlp) = tied_lists(
+        rest, gate_up(hidden_parts, part_gate_up)
+    )
+    top_parts = gather_end(grad_top, near, rest)
+    part_down_w, top_all = down_sums(activated, top_parts)
+    part_down_w, part_down = tied(part_down_w, part_down)
     grad_down = dp_scatter_sum(part_down_w)
 
     grad_gate_up, part_hidden_mlp = mlp_back(
@@ -782,33 +921,25 @@
     branch_parts, (part_result, grad_down) = ctx_gather(
         grad_middle.astype(LOW), [multiply(activated, part_down).astype(LOW)], [grad_down]
     )
+    branch_parts, (part_result,) = tied_lists(branch_parts, [part_result])
     grad_attn, part_out_w = out_back(branch_parts, part_out, attn_low)
     split_out = part_out_w.reshape(dp_size // ctx_size, ctx_size, -1, model_width)
     parts_out_w = exchanged(
-        lambda rank: lax.dynamic_index_in_dim(split_out, rank, 1, keepdims=False)
-    )
-    grad_attn, part_result = tied(grad_attn, part_result)
+        lambda rank: lax.dynamic_index_in_dim(split_out, rank, 1, False).reshape(-1, model_width)
+    )
     grad_qkv = attend_back(
         order, rotated, grad_attn, attn_low, log_total, keys, values, cosine, sine, block_rows
     )
     part_result, (grad_qkv, *parts_out_w) = ctx_scatter_sum(
-        part_result, [grad_qkv], parts_out_w
-    )
-    part_out_w = jnp.stack(in_rank_order(parts_out_w)).reshape(-1, model_width)
+        part_result, [grad_qkv, *parts_out_w]
+    )
     outputs = (middle + part_result).astype(LOW).reshape(inputs.shape)
-    part_hidden_attn = against(grad_qkv, part_qkv)
-    gain_attn_grad = jnp.sum(part_hidden_attn * normed_attn, 0)
-    gain_grads = jnp.pad(
-        jnp.stack([gain_attn_grad, gain_mlp_grad], 1).astype(LOW), ((0, 0), (0, LANES - 2))
-    )
-    part_qkv_w = jnp.concatenate([outer_sum(hidden_attn, grad_qkv).astype(LOW), gain_grads], 1)
-    part_attn_w, part_hidden_attn, outputs = tied(
-        fold(part_qkv_w, part_out_w, dp_size), part_hidden_attn.astype(LOW), outputs
+    slopes = jnp.pad(gain_mlp_grad[:, None], ((0, 0), (1, LANES - 2)))
+    part_attn_w = attn_sums(hidden_attn, grad_qkv, gathered_qkv, slopes, parts_out_w, dp_size)
+    grad_hidden_attn, (part_attn_w, grad_gate_up_w) = ctx_scatter_sum(
+        against(grad_qkv, part_qkv).astype(LOW), [part_attn_w], [grad_gate_up_w]
     )
     grad_attn_w = dp_scatter_sum(part_attn_w)
-    grad_hidden_attn, (grad_gate_up_w,) = ctx_scatter_sum(
-        part_hidden_attn, (), [grad_gate_up_w]
-    )
     scale_attn = norm_scale(x_rows)
     _, grad_in_norm = norm_back(grad_hidden_attn, x_rows * scale_attn, scale_attn, gain_attn)
     grad_inputs = (grad_middle + grad_in_norm).reshape(inputs.shape)
@@ -817,15 +948,13 @@
     out_gate, out_up = merge(gate_up_rows, dp_size, ff_chunk)
     out_down = grad_down.astype(WIDE)
     grad_attn_w, out_gate, out_up, grad_inputs = tied(grad_attn_w, out_gate, out_up, grad_inputs)
-    grad_qkv_w, grad_out_w = unfold(grad_attn_w, query_width, cuts, 1)
-    out_out = grad_out_w.astype(WIDE)
-    qkv_rows = columns_to_rows(grad_qkv_w)
-    out_query = jnp.concatenate([part[:, :query_width] for part in qkv_rows], 1).astype(WIDE)
-    rests = [part[:, query_width:].astype(WIDE) for part in qkv_rows]
-    kv_parts = [sum(rests[g * sharers : (g + 1) * sharers]) for g in range(KV_HEADS)]
-    out_key = jnp.concatenate([part[:, :head_dim] for part in kv_parts], 1)
-    out_value = jnp.concatenate([part[:, head_dim : 2 * head_dim] for part in kv_parts], 1)
-    out_gains = sum(rests)[:, 2 * head_dim : 2 * head_dim + 2].T
+    parts_qkv_w = exchanged(
+        lambda rank: lax.dynamic_slice(
+            grad_attn_w, (rank * gain_rows, 0), (gain_rows, qkv_width + LANES)
+        )
+    )
+    out_query, out_key, out_value, out_out, out_gains = finish(grad_attn_w, parts_qkv_w, sharers)
+    out_gains = out_gains[:, :2].T
     return (
         outputs,
         grad_inputs,

time: 532 us -> 523 us (0.983)
  Pallas kernels: 112 us -> 141 us
  matrix products: 56.1 us -> 38.7 us
  local copies, waits for them, and re-layouts: 57.9 us -> 43.7 us
    pallas_call x2 -> x4, Pallas kernels: 0.38 us -> 25.5 us  [the longest x1 12.6 us: down_sums(): pl.pallas_call(down_sums_kernel, in_specs=[vmem] + [pl.BlockSpec(memory_s...]
    unnamed x133 -> x108, local copies, waits for them, and re-layouts: 37.8 us -> 18.5 us
    ppermute x58 -> x65, waiting for transfers between devices: 166 us -> 151 us  [swapped(): return lax.ppermute(block, axis, route)]
    dot_general x3 -> x1, matrix products: 30.6 us -> 17.3 us  [outer_sum(): lax.dot_general(left, right, (((0,), (0,)), ((), ())), preferred_element_...]
    reduce_scatter x3, waiting for transfers between devices: 0.01 us -> 10.6 us  [dp_scatter_sum(): return lax.psum_scatter(block, 'dp', scatter_dimension=0, tiled=True)]
    convert_element_type x8, other arithmetic: 3.21 us -> 10.4 us  [ctx_scatter_sum(): got_left, got_right = (got_left.astype(WIDE), got_right.astype(WIDE))]
    ppermute x58 -> x65, starting transfers between devices: 67.3 us -> 68.6 us  [swapped(): return lax.ppermute(block, axis, route)]
  transfers between devices with their start and end apart: 65 -> 71, of which waited for: 32 -> 34; matrix products, arithmetic and copies ran while one was open for 25% -> 21% of each run, Pallas kernels for 21% -> 27%
where the time goes in v4:
time: 523 us; the launch traced here: 519 us
  waiting for transfers between devices  162 us (31%)
  Pallas kernels  141 us (27%)
  starting transfers between devices  69 us (13%)
  other arithmetic  49.2 us (9%)
  local copies, waits for them, and re-layouts  43.7 us (8%)
  matrix products  38.7 us (7%)
  between operations  15.4 us (3%)
    ppermute x65, waiting for transfers between devices, swapped(): return lax.ppermute(block, axis, route)  151 us
    ppermute x65, starting transfers between devices, swapped(): return lax.ppermute(block, axis, route)  68.6 us
    pallas_call x1, Pallas kernels, attend_back(): pl.pallas_call(functools.partial(attend_back_kernel, pairs, 2 * rows), gr...  29.8 us
    pallas_call x1, Pallas kernels, mlp_back(): pl.pallas_call(mlp_back_kernel, grid=(count // rows,), in_specs=[block(de...  29.2 us
    pallas_call x1, Pallas kernels, gate_up(): pl.pallas_call(gate_up_kernel, grid=(steps,), in_specs=[pl.BlockSpec((dep...  21.2 us
    pallas_call x1, Pallas kernels, attend(): pl.pallas_call(functools.partial(attend_kernel, pairs, 2 * rows), grid_sp...  18.8 us
    unnamed x108, local copies, waits for them, and re-layouts  18.5 us
    dot_general x1, matrix products, outer_sum(): lax.dot_general(left, right, (((0,), (0,)), ((), ())), preferred_element_...  17.3 us
  transfers between devices with their start and end apart: 71, of which 34 were waited for; matrix products, arithmetic and copies ran while one was open for 21% of the time, Pallas kernels for 27%

profile of v4, /device:TPU:0, one launch (start us, length us, event | category | flops | bytes accessed | tf_op | source)
XLA Modules:
  0.0 518.8 jit_solution(9230485775705864058)
XLA Ops:
  35.0 5.9 %collective-permute-done.6 = bf16[64,2816]{1,0:T(8,128)(2,1)S(1)} collective-permute-done((bf16[64,2816]{1,0:T(8,128)(2,1)S(1)}, bf16[64,2816]{1,0:T(8,128)(2,1)S(1)}, u32[]{:S(2)}, u32[]{:S(2)}) %collective-permute-start.6) | collective-permute-done | bytes 360480 | tf_op jit(solution)/shard_map/ppermute | solution.py:37
  44.1 8.0 %collective-permute-done.4 = bf16[128,2048]{1,0:T(8,128)(2,1)} collective-permute-done((bf16[128,2048]{1,0:T(8,128)(2,1)}, bf16[128,2048]{1,0:T(8,128)(2,1)}, u32[]{:S(2)}, u32[]{:S(2)}) %collective-permute-start.4) | collective-permute-done | bytes 524320 | tf_op jit(solution)/shard_map/ppermute | solution.py:37
  66.0 5.3 %collective-permute-done.8 = bf16[128,2048]{1,0:T(8,128)(2,1)} collective-permute-done((bf16[128,2048]{1,0:T(8,128)(2,1)}, bf16[128,2048]{1,0:T(8,128)(2,1)}, u32[]{:S(2)}, u32[]{:S(2)}) %collective-permute-start.8) | collective-permute-done | bytes 524320 | tf_op jit(solution)/shard_map/ppermute | solution.py:37
  74.1 8.3 %collective-permute-done.10 = bf16[128,2048]{1,0:T(8,128)(2,1)} collective-permute-done((bf16[128,2048]{1,0:T(8,128)(2,1)}, bf16[128,2048]{1,0:T(8,128)(2,1)}, u32[]{:S(2)}, u32[]{:S(2)}) %collective-permute-start.10) | collective-permute-done | bytes 524320 | tf_op jit(solution)/shard_map/ppermute | solution.py:37
  110.6 18.8 %attend.1 = (bf16[1024,512]{1,0:T(8,128)(2,1)}, bf16[1024,512]{1,0:T(8,128)(2,1)}, bf16[1024,128]{1,0:T(8,128)(2,1)}, bf16[1024,128]{1,0:T(8,128)(2,1)}, f32[1024,128]{1,0:T(8,128)}) custom-call(s32[8]{0:T(128)} %pad_add_fusion.order, f32[1024,640]{1,0:T(8,128)} %fusion.6.q_ref.kv_ref, f32[1024,640]{1,0:T(8,128)} %fusion.6.q_ref.kv_ref, ...), custom_call_target="tpu_custom_call" | custom-call | flops 2147483648 | bytes 8388608 | tf_op jit(solution)/shard_map/attend/pallas_call | solution.py:323
  139.2 22.1 %collective-permute-done.24 = bf16[2,256,1024]{2,1,0:T(8,128)(2,1)S(1)} collective-permute-done((bf16[2,256,1024]{2,1,0:T(8,128)(2,1)S(1)}, bf16[2,256,1024]{2,1,0:T(8,128)(2,1)S(1)}, u32[]{:S(2)}, u32[]{:S(2)}) %collective-permute-start.24) | collective-permute-done | bytes 1048608 | tf_op jit(solution)/shard_map/ppermute | solution.py:37
  165.5 9.9 %collective-permute-done.27 = bf16[256,1024]{1,0:T(8,128)(2,1)S(1)} collective-permute-done((bf16[256,1024]{1,0:T(8,128)(2,1)S(1)}, bf16[256,1024]{1,0:T(8,128)(2,1)S(1)}, u32[]{:S(2)}, u32[]{:S(2)}) %collective-permute-start.27) | collective-permute-done | bytes 524320 | tf_op jit(solution)/shard_map/ppermute | solution.py:37
  181.4 10.8 %collective-permute-done.30.refs_1_ = bf16[128,2048]{1,0:T(8,128)(2,1)S(1)} collective-permute-done((bf16[128,2048]{1,0:T(8,128)(2,1)S(1)}, bf16[128,2048]{1,0:T(8,128)(2,1)S(1)}, u32[]{:S(2)}, u32[]{:S(2)}) %collective-permute-start.30) | collective-permute-done | bytes 524320 | tf_op jit(solution)/shard_map/ppermute | solution.py:37
  195.5 9.4 %collective-permute-done.29.refs_3_ = bf16[128,2048]{1,0:T(8,128)(2,1)S(1)} collective-permute-done((bf16[128,2048]{1,0:T(8,128)(2,1)S(1)}, bf16[128,2048]{1,0:T(8,128)(2,1)S(1)}, u32[]{:S(2)}, u32[]{:S(2)}) %collective-permute-start.29) | collective-permute-done | bytes 524320 | tf_op jit(solution)/shard_map/ppermute | solution.py:37
  204.8 7.3 %collective-permute-done.32.refs_5_ = bf16[128,2048]{1,0:T(8,128)(2,1)S(1)} collective-permute-done((bf16[128,2048]{1,0:T(8,128)(2,1)S(1)}, bf16[128,2048]{1,0:T(8,128)(2,1)S(1)}, u32[]{:S(2)}, u32[]{:S(2)}) %collective-permute-start.32) | collective-permute-done | bytes 524320 | tf_op jit(solution)/shard_map/ppermute | solution.py:37
  218.2 21.2 %gate_up.1 = (f32[1024,1408]{1,0:T(8,128)}, f32[1024,1408]{1,0:T(8,128)}, bf16[1024,1408]{1,0:T(8,128)(2,1)}, bf16[1024,2048]{1,0:T(8,128)(2,1)}) custom-call(bf16[2048,2816]{1,0:T(8,128)(2,1)} %all-gather.6.cloned.1.call-done.gate_w_ref.up_w_ref.weight_ref, bf16[2048,2816]{1,0:T(8,128)(2,1)} %all-gather.6.cloned.1.call-done.gate_w_ref.up_w_ref.weight_ref, ...), custom_call_target="tpu_custom_call" | custom-call | flops 11811160064 | bytes 37748736 | tf_op jit(solution)/shard_map/gate_up/pallas_call | solution.py:573
  239.4 12.6 %down_sums.1 = (bf16[1408,2048]{1,0:T(8,128)(2,1)}, bf16[1024,2048]{1,0:T(8,128)(2,1)}) custom-call(bf16[1024,1408]{1,0:T(8,128)(2,1)} %get-tuple-element.179.active_ref, bf16[256,2048]{1,0:T(8,128)(2,1)} %bitcast.216, bf16[128,2048]{1,0:T(8,128)(2,1)} %collective-permute-done.15.refs_1_, bf16[128,2048]{1,0:T(8,128)(2,1)} %collective-permute-done.36.refs_2_, ...), custom_call_target="tpu_custom_call" | custom-call | flops 5905580032 | bytes 18874368 | tf_op jit(solution)/shard_map/down_sums/pallas_call | solution.py:620
  252.2 29.2 %mlp_back.1 = (bf16[1024,2816]{1,0:T(8,128)(2,1)}, bf16[1024,2048]{1,0:T(8,128)(2,1)}) custom-call(bf16[1024,2048]{1,0:T(8,128)(2,1)} %get-tuple-element.184.top_ref, f32[1024,1408]{1,0:T(8,128)} %get-tuple-element.185.gate_ref, f32[1024,1408]{1,0:T(8,128)} %get-tuple-element.186.up_ref, bf16[1408,2048]{1,0:T(8,128)(2,1)} %all-gather.8.cloned.1.call-done.down_ref, ...), custom_call_target="tpu_custom_call" | custom-call | flops 17716740096 | bytes 41943040 | tf_op jit(solution)/shard_map/mlp_back/pallas_call | solution.py:675
  287.1 17.3 %convolution_convert_fusion = bf16[2048,2816]{1,0:T(8,128)(2,1)} fusion(bf16[1024,2048]{1,0:T(8,128)(2,1)S(1)} %copy-done.46, bf16[1024,2816]{1,0:T(8,128)(2,1)} %get-tuple-element.192), kind=kOutput, calls=%fused_computation | convolution fusion | flops 11816927232 | bytes 21495808 | tf_op jit(solution)/shard_map/dot_general | solution.py:32
  311.1 6.5 %collective-permute-done.41 = bf16[256,1024]{1,0:T(8,128)(2,1)S(1)} collective-permute-done((bf16[256,1024]{1,0:T(8,128)(2,1)S(1)}, bf16[256,1024]{1,0:T(8,128)(2,1)S(1)}, u32[]{:S(2)}, u32[]{:S(2)}) %collective-permute-start.41) | collective-permute-done | bytes 524320 | tf_op jit(solution)/shard_map/ppermute | solution.py:37
  327.0 8.4 %convolution_convert_fusion.2 = bf16[1024,2048]{1,0:T(8,128)(2,1)} fusion(bf16[1024,1408]{1,0:T(8,128)(2,1)S(1)} %copy-done.47, bf16[1408,2048]{1,0:T(8,128)(2,1)S(1)} %bitcast.242), kind=kOutput, calls=%fused_computation.7 | convolution fusion | flops 5907677184 | bytes 12845056 | tf_op jit(solution)/shard_map/dot_general | solution.py:24
  341.8 7.9 %collective-permute-done.44.refs_2_ = bf16[128,2048]{1,0:T(8,128)(2,1)S(1)} collective-permute-done((bf16[128,2048]{1,0:T(8,128)(2,1)S(1)}, bf16[128,2048]{1,0:T(8,128)(2,1)S(1)}, u32[]{:S(2)}, u32[]{:S(2)}) %collective-permute-start.44) | collective-permute-done | bytes 524320 | tf_op jit(solution)/shard_map/ppermute | solution.py:37
  350.6 5.6 %collective-permute-done.46.refs_5_ = bf16[128,2048]{1,0:T(8,128)(2,1)S(1)} collective-permute-done((bf16[128,2048]{1,0:T(8,128)(2,1)S(1)}, bf16[128,2048]{1,0:T(8,128)(2,1)S(1)}, u32[]{:S(2)}, u32[]{:S(2)}) %collective-permute-start.46) | collective-permute-done | bytes 524320 | tf_op jit(solution)/shard_map/ppermute | solution.py:37
  362.2 10.1 %out_back.1 = (bf16[1024,512]{1,0:T(8,128)(2,1)}, bf16[512,2048]{1,0:T(8,128)(2,1)}) custom-call(bf16[512,2048]{1,0:T(8,128)(2,1)} %bitcast.210, bf16[1024,512]{1,0:T(8,128)(2,1)} %get-tuple-element.152.attn_ref.out_ref, bf16[256,2048]{1,0:T(8,128)(2,1)} %copy-done.25, bf16[128,2048]{1,0:T(8,128)(2,1)} %copy-done.36, bf16[128,2048]{1,0:T(8,128)(2,1)} %copy-done.39, ...), custom_call_target="tpu_custom_call" | custom-call | flops 4294967296 | bytes 16777216 | tf_op jit(solution)/shard_map/out_back/pallas_call | solution.py:719
  378.8 29.8 %attend_back.1.grad_ref = bf16[1024,640]{1,0:T(8,128)(2,1)} custom-call(s32[8]{0:T(128)} %pad_add_fusion.order, bf16[1024,512]{1,0:T(8,128)(2,1)} %get-tuple-element.206.rot_ref, bf16[1024,512]{1,0:T(8,128)(2,1)} %get-tuple-element.214.grad_ref, bf16[1024,512]{1,0:T(8,128)(2,1)} %get-tuple-element.152.attn_ref.out_ref, ...), custom_call_target="tpu_custom_call" | custom-call | flops 5368709120 | bytes 8388608 | tf_op jit(solution)/shard_map/attend_back/pallas_call | solution.py:351
  408.7 5.7 %convolution_convert_fusion.1 = bf16[1024,2048]{1,0:T(8,128)(2,1)S(1)} fusion(bf16[1024,640]{1,0:T(8,128)(2,1)} %attend_back.1.grad_ref, bf16[2048,768]{1,0:T(8,128)(2,1)} %all-gather.4.cloned.1.call-done.weight_ref), kind=kOutput, calls=%fused_computation.6 | convolution fusion | flops 2686451712 | bytes 8126464 | tf_op jit(solution)/shard_map/dot_general | solution.py:28
  425.3 10.5 %attn_sums.1 = bf16[2048,1280]{1,0:T(8,128)(2,1)} custom-call(s32[1]{0:T(128)} %bitcast.33.me_ref, bf16[1024,2048]{1,0:T(8,128)(2,1)} %copy-done.10, bf16[1024,640]{1,0:T(8,128)(2,1)} %attend_back.1.grad_ref, bf16[2048,768]{1,0:T(8,128)(2,1)} %all-gather.4.cloned.1.call-done.weight_ref, f32[2048,128]{1,0:T(8,128)} %pad.9.slopes_ref, ...), custom_call_target="tpu_custom_call" | custom-call | flops 2684354560 | bytes 16777216 | tf_op jit(solution)/shard_map/attn_sums/pallas_call | solution.py:406
  457.1 8.0 %collective-permute-done.58 = bf16[256,1024]{1,0:T(8,128)(2,1)} collective-permute-done((bf16[256,1024]{1,0:T(8,128)(2,1)S(1)}, bf16[256,1024]{1,0:T(8,128)(2,1)}, u32[]{:S(2)}, u32[]{:S(2)}) %collective-permute-start.58) | collective-permute-done | bytes 524320 | tf_op jit(solution)/shard_map/ppermute | solution.py:37
  487.5 10.6 %reduce-scatter.6.cloned.1.call-done.joined_ref = bf16[256,1280]{1,0:T(8,128)(2,1)} async-done(((bf16[2048,1280]{1,0:T(8,128)(2,1)}), bf16[256,1280]{1,0:T(8,128)(2,1)}) %reduce-scatter.6.cloned.1.call-update) | async-done | bytes 655376 | tf_op jit(solution)/shard_map/reduce_scatter | solution.py:144
  (344 shorter events, 214.4 us)
Async XLA Ops:
  7.2 88.2 %all-gather.4.cloned.1.call-start = ((), (), s32[]{:S(2)}) async-start(), calls=%async_computation.3 | async-start | bytes 3538944 | tf_op jit(solution)/shard_map/all_gather | solution.py:140
  22.4 195.7 %all-gather.6.cloned.1.call-start = ((), (), s32[]{:S(2)}) async-start(), calls=%async_computation.4 | async-start | bytes 12976128 | tf_op jit(solution)/shard_map/all_gather | solution.py:140
  27.2 24.9 %collective-permute-start.4 = (bf16[128,2048]{1,0:T(8,128)(2,1)}, bf16[128,2048]{1,0:T(8,128)(2,1)}, u32[]{:S(2)}, u32[]{:S(2)}) collective-permute-start(bf16[128,2048]{1,0:T(8,128)(2,1)} %get-tuple-element.325), channel_id=1, source_target_pairs={{0,2},{1,3},{2,0},{3,1},{4,6},{5,7},{6,4},{7,5},{8,10},{9,11},{10,... | collective-permute-start | bytes 1572872 | tf_op jit(solution)/shard_map/ppermute | solution.py:37
  28.6 24.0 %collective-permute-start.3 = (bf16[128,2048]{1,0:T(8,128)(2,1)}, bf16[128,2048]{1,0:T(8,128)(2,1)}, u32[]{:S(2)}, u32[]{:S(2)}) collective-permute-start(bf16[128,2048]{1,0:T(8,128)(2,1)} %get-tuple-element.326), channel_id=1, source_target_pairs={{0,1},{1,0},{2,3},{3,2},{4,5},{5,4},{6,7},{7,6},{8,9},{9,8},{10,11... | collective-permute-start | bytes 1572872 | tf_op jit(solution)/shard_map/ppermute | solution.py:37
  52.6 199.5 %all-gather.8.cloned.1.call-start = ((), (), s32[]{:S(2)}) async-start(), calls=%async_computation.5 | async-start | bytes 6488064 | tf_op jit(solution)/shard_map/all_gather | solution.py:140
  52.8 39.1 %collective-permute-start.13 = (bf16[64,2048]{1,0:T(8,128)(2,1)S(1)}, bf16[64,2048]{1,0:T(8,128)(2,1)S(1)}, u32[]{:S(2)}, u32[]{:S(2)}) collective-permute-start(bf16[64,2048]{1,0:T(8,128)(2,1)S(1)} %copy-done.5), channel_id=1, source_target_pairs={{0,16},{4,20},{8,24},{12,28},{16,0},{20,4},{24,8},{28,12},{1,17},{... | collective-permute-start | bytes 786440 | tf_op jit(solution)/shard_map/ppermute | solution.py:37
  101.2 28.2 %collective-permute-start.23 = (bf16[128,2048]{1,0:T(8,128)(2,1)}, bf16[128,2048]{1,0:T(8,128)(2,1)S(1)}, u32[]{:S(2)}, u32[]{:S(2)}) collective-permute-start(bf16[128,2048]{1,0:T(8,128)(2,1)} %get-tuple-element.295), channel_id=1, source_target_pairs={{0,3},{1,2},{2,1},{3,0},{4,7},{5,6},{6,5},{7,4},{8,11},{9,10},{10,... | collective-permute-start | bytes 1572872 | tf_op jit(solution)/shard_map/ppermute | solution.py:37
  102.5 26.9 %collective-permute-start.22 = (bf16[128,2048]{1,0:T(8,128)(2,1)}, bf16[128,2048]{1,0:T(8,128)(2,1)S(1)}, u32[]{:S(2)}, u32[]{:S(2)}) collective-permute-start(bf16[128,2048]{1,0:T(8,128)(2,1)} %get-tuple-element.296), channel_id=1, source_target_pairs={{0,2},{1,3},{2,0},{3,1},{4,6},{5,7},{6,4},{7,5},{8,10},{9,11},{10,... | collective-permute-start | bytes 1572872 | tf_op jit(solution)/shard_map/ppermute | solution.py:37
  104.0 26.2 %collective-permute-start.21 = (bf16[128,2048]{1,0:T(8,128)(2,1)S(1)}, bf16[128,2048]{1,0:T(8,128)(2,1)S(1)}, u32[]{:S(2)}, u32[]{:S(2)}) collective-permute-start(bf16[128,2048]{1,0:T(8,128)(2,1)S(1)} %get-tuple-element.297), channel_id=1, source_target_pairs={{0,1},{1,0},{2,3},{3,2},{4,5},{5,4},{6,7},{7,6},{8,9},{9,8},{10,11... | collective-permute-start | bytes 1572872 | tf_op jit(solution)/shard_map/ppermute | solution.py:37
  137.1 24.2 %collective-permute-start.24 = (bf16[2,256,1024]{2,1,0:T(8,128)(2,1)S(1)}, bf16[2,256,1024]{2,1,0:T(8,128)(2,1)S(1)}, u32[]{:S(2)}, u32[]{:S(2)}) collective-permute-start(bf16[2,256,1024]{2,1,0:T(8,128)(2,1)S(1)} %pad_maximum_fusion.5), channel_id=1, source_target_pairs={{0,1},{1,0},{2,3},{3,2},{4,5},{5,4},{6,7},{7,6},{8,9},{9,8},{10,11... | collective-permute-start | bytes 3145736 | tf_op jit(solution)/shard_map/ppermute | solution.py:37
  138.6 23.9 %collective-permute-start.25 = (bf16[2,256,1024]{2,1,0:T(8,128)(2,1)S(1)}, bf16[2,256,1024]{2,1,0:T(8,128)(2,1)S(1)}, u32[]{:S(2)}, u32[]{:S(2)}) collective-permute-start(bf16[2,256,1024]{2,1,0:T(8,128)(2,1)S(1)} %pad_maximum_fusion.6), channel_id=1, source_target_pairs={{0,2},{1,3},{2,0},{3,1},{4,6},{5,7},{6,4},{7,5},{8,10},{9,11},{10,... | collective-permute-start | bytes 3145736 | tf_op jit(solution)/shard_map/ppermute | solution.py:37
  176.6 180.4 %reduce-scatter.4.cloned.1.call-start = ((), (), s32[]{:S(2)}) async-start(), calls=%async_computation.6 | async-start | bytes 6488064 | tf_op jit(solution)/shard_map/reduce_scatter | solution.py:144
  179.5 25.3 %collective-permute-start.29 = (bf16[128,2048]{1,0:T(8,128)(2,1)S(1)}, bf16[128,2048]{1,0:T(8,128)(2,1)S(1)}, u32[]{:S(2)}, u32[]{:S(2)}) collective-permute-start(bf16[128,2048]{1,0:T(8,128)(2,1)S(1)} %get-tuple-element.321), channel_id=1, source_target_pairs={{0,2},{1,3},{2,0},{3,1},{4,6},{5,7},{6,4},{7,5},{8,10},{9,11},{10,... | collective-permute-start | bytes 1572872 | tf_op jit(solution)/shard_map/ppermute | solution.py:37
  180.8 24.1 %collective-permute-start.28 = (bf16[128,2048]{1,0:T(8,128)(2,1)S(1)}, bf16[128,2048]{1,0:T(8,128)(2,1)S(1)}, u32[]{:S(2)}, u32[]{:S(2)}) collective-permute-start(bf16[128,2048]{1,0:T(8,128)(2,1)S(1)} %get-tuple-element.322), channel_id=1, source_target_pairs={{0,1},{1,0},{2,3},{3,2},{4,5},{5,4},{6,7},{7,6},{8,9},{9,8},{10,11... | collective-permute-start | bytes 1572872 | tf_op jit(solution)/shard_map/ppermute | solution.py:37
  213.0 26.4 %collective-permute-start.34 = (bf16[128,2048]{1,0:T(8,128)(2,1)}, bf16[128,2048]{1,0:T(8,128)(2,1)}, u32[]{:S(2)}, u32[]{:S(2)}) collective-permute-start(bf16[128,2048]{1,0:T(8,128)(2,1)} %collective-permute-done.15.refs_1_), channel_id=1, source_target_pairs={{0,2},{1,3},{2,0},{3,1},{4,6},{5,7},{6,4},{7,5},{8,10},{9,11},{10,... | collective-permute-start | bytes 1572872 | tf_op jit(solution)/shard_map/ppermute | solution.py:37
  213.8 25.6 %collective-permute-start.35 = (bf16[128,2048]{1,0:T(8,128)(2,1)}, bf16[128,2048]{1,0:T(8,128)(2,1)}, u32[]{:S(2)}, u32[]{:S(2)}) collective-permute-start(bf16[128,2048]{1,0:T(8,128)(2,1)} %collective-permute-done.16.refs_4_), channel_id=1, source_target_pairs={{0,1},{1,0},{2,3},{3,2},{4,5},{5,4},{6,7},{7,6},{8,9},{9,8},{10,11... | collective-permute-start | bytes 1572872 | tf_op jit(solution)/shard_map/ppermute | solution.py:37
  215.9 23.5 %collective-permute-start.37 = (bf16[128,2048]{1,0:T(8,128)(2,1)}, bf16[128,2048]{1,0:T(8,128)(2,1)}, u32[]{:S(2)}, u32[]{:S(2)}) collective-permute-start(bf16[128,2048]{1,0:T(8,128)(2,1)} %get-tuple-element.319), channel_id=1, source_target_pairs={{0,2},{1,3},{2,0},{3,1},{4,6},{5,7},{6,4},{7,5},{8,10},{9,11},{10,... | collective-permute-start | bytes 1572872 | tf_op jit(solution)/shard_map/ppermute | solution.py:37
  252.1 216.7 %reduce-scatter.8.cloned.1.call-start = ((), (), s32[]{:S(2)}) async-start(), calls=%async_computation.8 | async-start | bytes 12976128 | tf_op jit(solution)/shard_map/reduce_scatter | solution.py:144
  304.7 193.4 %reduce-scatter.6.cloned.1.call-start = ((), (), s32[]{:S(2)}) async-start(), calls=%async_computation.7 | async-start | bytes 5898240 | tf_op jit(solution)/shard_map/reduce_scatter | solution.py:144
  359.9 48.7 %collective-permute-start.48 = (bf16[2,256,1024]{2,1,0:T(8,128)(2,1)}, bf16[2,256,1024]{2,1,0:T(8,128)(2,1)}, u32[]{:S(2)}, u32[]{:S(2)}) collective-permute-start(bf16[2,256,1024]{2,1,0:T(8,128)(2,1)} %pad_maximum_fusion.9), channel_id=1, source_target_pairs={{0,1},{1,0},{2,3},{3,2},{4,5},{5,4},{6,7},{7,6},{8,9},{9,8},{10,11... | collective-permute-start | bytes 3145736 | tf_op jit(solution)/shard_map/ppermute | solution.py:37
  361.2 47.4 %collective-permute-start.49 = (bf16[2,256,1024]{2,1,0:T(8,128)(2,1)}, bf16[2,256,1024]{2,1,0:T(8,128)(2,1)}, u32[]{:S(2)}, u32[]{:S(2)}) collective-permute-start(bf16[2,256,1024]{2,1,0:T(8,128)(2,1)} %pad_maximum_fusion.10), channel_id=1, source_target_pairs={{0,2},{1,3},{2,0},{3,1},{4,6},{5,7},{6,4},{7,5},{8,10},{9,11},{10,... | collective-permute-start | bytes 3145736 | tf_op jit(solution)/shard_map/ppermute | solution.py:37
  375.3 33.3 %collective-permute-start.51 = (bf16[128,2048]{1,0:T(8,128)(2,1)}, bf16[128,2048]{1,0:T(8,128)(2,1)S(1)}, u32[]{:S(2)}, u32[]{:S(2)}) collective-permute-start(bf16[128,2048]{1,0:T(8,128)(2,1)} %bitcast.58), channel_id=1, source_target_pairs={{0,2},{1,3},{2,0},{3,1},{4,6},{5,7},{6,4},{7,5},{8,10},{9,11},{10,... | collective-permute-start | bytes 1572872 | tf_op jit(solution)/shard_map/ppermute | solution.py:37
  376.2 32.4 %collective-permute-start.52 = (bf16[128,2048]{1,0:T(8,128)(2,1)}, bf16[128,2048]{1,0:T(8,128)(2,1)}, u32[]{:S(2)}, u32[]{:S(2)}) collective-permute-start(bf16[128,2048]{1,0:T(8,128)(2,1)} %bitcast.59), channel_id=1, source_target_pairs={{0,3},{1,2},{2,1},{3,0},{4,7},{5,6},{6,5},{7,4},{8,11},{9,10},{10,... | collective-permute-start | bytes 1572872 | tf_op jit(solution)/shard_map/ppermute | solution.py:37
  378.7 29.9 %collective-permute-start.50 = (bf16[128,2048]{1,0:T(8,128)(2,1)}, bf16[128,2048]{1,0:T(8,128)(2,1)}, u32[]{:S(2)}, u32[]{:S(2)}) collective-permute-start(bf16[128,2048]{1,0:T(8,128)(2,1)} %bitcast.57), channel_id=1, source_target_pairs={{0,1},{1,0},{2,3},{3,2},{4,5},{5,4},{6,7},{7,6},{8,9},{9,8},{10,11... | collective-permute-start | bytes 1572872 | tf_op jit(solution)/shard_map/ppermute | solution.py:37
  (97 other events, 973.6 us)
Sparse Core Ops, SparseCore 0:
  22.5 47.1 all-gather.3
  72.0 107.2 all-gather.5
  180.9 58.7 all-gather.7
  252.2 62.9 reduce-scatter.3
  317.4 117.6 reduce-scatter.7
  440.3 57.7 reduce-scatter.5

commit v5 on v4

--- a/solution.py
+++ b/solution.py
@@ -363,7 +363,7 @@
             ],
         ),
         out_shape=jax.ShapeDtypeStruct((seq, width + LANES), LOW),
-        compiler_params=pltpu.CompilerParams(vmem_limit_bytes=60 << 20),
+        compiler_params=pltpu.CompilerParams(vmem_limit_bytes=48 << 20),
         cost_estimate=pl.CostEstimate(flops=5 * 2 * seq * seq * width, bytes_accessed=8 << 20, transcendentals=seq * seq * width // HEAD_DIM // 2),
         name="attend_back",
     )(order, rotated, grad, out, lse, cosine, sine, keys, values, cosine, sine)
@@ -408,7 +408,7 @@
         in_specs=[pl.BlockSpec(memory_space=pltpu.SMEM)] + [vmem] * (4 + len(parts)),
         out_specs=vmem,
         out_shape=jax.ShapeDtypeStruct((depth, full), LOW),
-        compiler_params=pltpu.CompilerParams(vmem_limit_bytes=60 << 20),
+        compiler_params=pltpu.CompilerParams(vmem_limit_bytes=48 << 20),
         cost_estimate=pl.CostEstimate(
             flops=2 * hidden.shape[0] * depth * width, bytes_accessed=16 << 20, transcendentals=0
         ),

time: 523 us -> 520 us (level)
    unnamed x108 -> x136, local copies, waits for them, and re-layouts: 18.5 us -> 20.1 us
  transfers between devices with their start and end apart: 71 -> 71, of which waited for: 34 -> 35; matrix products, arithmetic and copies ran while one was open for 21% -> 20% of each run, Pallas kernels for 27% -> 26%
where the time goes in v5:
time: 520 us; the launch traced here: 516 us
  waiting for transfers between devices  166 us (32%)
  Pallas kernels  138 us (27%)
  starting transfers between devices  70.1 us (13%)
  other arithmetic  45.4 us (9%)
  local copies, waits for them, and re-layouts  42.7 us (8%)
  matrix products  38.5 us (7%)
  between operations  15.5 us (3%)
    ppermute x65, waiting for transfers between devices, swapped(): return lax.ppermute(block, axis, route)  154 us
    ppermute x65, starting transfers between devices, swapped(): return lax.ppermute(block, axis, route)  69.5 us
    pallas_call x1, Pallas kernels, mlp_back(): pl.pallas_call(mlp_back_kernel, grid=(count // rows,), in_specs=[block(de...  29.1 us
    pallas_call x1, Pallas kernels, attend_back(): pl.pallas_call(functools.partial(attend_back_kernel, pairs, 2 * rows), gr...  27.4 us
    pallas_call x1, Pallas kernels, gate_up(): pl.pallas_call(gate_up_kernel, grid=(steps,), in_specs=[pl.BlockSpec((dep...  21.3 us
    unnamed x136, local copies, waits for them, and re-layouts  20.1 us
    pallas_call x1, Pallas kernels, attend(): pl.pallas_call(functools.partial(attend_kernel, pairs, 2 * rows), grid_sp...  19 us
    dot_general x1, matrix products, outer_sum(): lax.dot_general(left, right, (((0,), (0,)), ((), ())), preferred_element_...  17.4 us
  transfers between devices with their start and end apart: 71, of which 35 were waited for; matrix products, arithmetic and copies ran while one was open for 20% of the time, Pallas kernels for 26%

profile of v5, /device:TPU:0, one launch (start us, length us, event | category | flops | bytes accessed | tf_op | source)
XLA Modules:
  0.0 515.8 jit_solution(17440564694366652973)
XLA Ops:
  35.0 5.9 %collective-permute-done.6 = bf16[64,2816]{1,0:T(8,128)(2,1)S(1)} collective-permute-done((bf16[64,2816]{1,0:T(8,128)(2,1)S(1)}, bf16[64,2816]{1,0:T(8,128)(2,1)S(1)}, u32[]{:S(2)}, u32[]{:S(2)}) %collective-permute-start.6) | collective-permute-done | bytes 360480 | tf_op jit(solution)/shard_map/ppermute | solution.py:37
  44.1 8.0 %collective-permute-done.4 = bf16[128,2048]{1,0:T(8,128)(2,1)} collective-permute-done((bf16[128,2048]{1,0:T(8,128)(2,1)}, bf16[128,2048]{1,0:T(8,128)(2,1)}, u32[]{:S(2)}, u32[]{:S(2)}) %collective-permute-start.4) | collective-permute-done | bytes 524320 | tf_op jit(solution)/shard_map/ppermute | solution.py:37
  66.1 5.3 %collective-permute-done.8 = bf16[128,2048]{1,0:T(8,128)(2,1)} collective-permute-done((bf16[128,2048]{1,0:T(8,128)(2,1)}, bf16[128,2048]{1,0:T(8,128)(2,1)}, u32[]{:S(2)}, u32[]{:S(2)}) %collective-permute-start.8) | collective-permute-done | bytes 524320 | tf_op jit(solution)/shard_map/ppermute | solution.py:37
  74.2 8.3 %collective-permute-done.10 = bf16[128,2048]{1,0:T(8,128)(2,1)} collective-permute-done((bf16[128,2048]{1,0:T(8,128)(2,1)}, bf16[128,2048]{1,0:T(8,128)(2,1)}, u32[]{:S(2)}, u32[]{:S(2)}) %collective-permute-start.10) | collective-permute-done | bytes 524320 | tf_op jit(solution)/shard_map/ppermute | solution.py:37
  110.7 19.0 %attend.1 = (bf16[1024,512]{1,0:T(8,128)(2,1)}, bf16[1024,512]{1,0:T(8,128)(2,1)}, bf16[1024,128]{1,0:T(8,128)(2,1)}, bf16[1024,128]{1,0:T(8,128)(2,1)}, f32[1024,128]{1,0:T(8,128)}) custom-call(s32[8]{0:T(128)} %pad_add_fusion.order, f32[1024,640]{1,0:T(8,128)} %fusion.6.q_ref.kv_ref, f32[1024,640]{1,0:T(8,128)} %fusion.6.q_ref.kv_ref, ...), custom_call_target="tpu_custom_call" | custom-call | flops 2147483648 | bytes 8388608 | tf_op jit(solution)/shard_map/attend/pallas_call | solution.py:323
  139.5 22.0 %collective-permute-done.24 = bf16[2,256,1024]{2,1,0:T(8,128)(2,1)S(1)} collective-permute-done((bf16[2,256,1024]{2,1,0:T(8,128)(2,1)S(1)}, bf16[2,256,1024]{2,1,0:T(8,128)(2,1)S(1)}, u32[]{:S(2)}, u32[]{:S(2)}) %collective-permute-start.24) | collective-permute-done | bytes 1048608 | tf_op jit(solution)/shard_map/ppermute | solution.py:37
  165.7 10.0 %collective-permute-done.27 = bf16[256,1024]{1,0:T(8,128)(2,1)S(1)} collective-permute-done((bf16[256,1024]{1,0:T(8,128)(2,1)S(1)}, bf16[256,1024]{1,0:T(8,128)(2,1)S(1)}, u32[]{:S(2)}, u32[]{:S(2)}) %collective-permute-start.27) | collective-permute-done | bytes 524320 | tf_op jit(solution)/shard_map/ppermute | solution.py:37
  181.5 10.8 %collective-permute-done.30.refs_1_ = bf16[128,2048]{1,0:T(8,128)(2,1)S(1)} collective-permute-done((bf16[128,2048]{1,0:T(8,128)(2,1)S(1)}, bf16[128,2048]{1,0:T(8,128)(2,1)S(1)}, u32[]{:S(2)}, u32[]{:S(2)}) %collective-permute-start.30) | collective-permute-done | bytes 524320 | tf_op jit(solution)/shard_map/ppermute | solution.py:37
  195.9 9.3 %collective-permute-done.29.refs_3_ = bf16[128,2048]{1,0:T(8,128)(2,1)S(1)} collective-permute-done((bf16[128,2048]{1,0:T(8,128)(2,1)S(1)}, bf16[128,2048]{1,0:T(8,128)(2,1)S(1)}, u32[]{:S(2)}, u32[]{:S(2)}) %collective-permute-start.29) | collective-permute-done | bytes 524320 | tf_op jit(solution)/shard_map/ppermute | solution.py:37
  205.2 8.1 %collective-permute-done.32.refs_5_ = bf16[128,2048]{1,0:T(8,128)(2,1)S(1)} collective-permute-done((bf16[128,2048]{1,0:T(8,128)(2,1)S(1)}, bf16[128,2048]{1,0:T(8,128)(2,1)S(1)}, u32[]{:S(2)}, u32[]{:S(2)}) %collective-permute-start.32) | collective-permute-done | bytes 524320 | tf_op jit(solution)/shard_map/ppermute | solution.py:37
  217.7 21.3 %gate_up.1 = (f32[1024,1408]{1,0:T(8,128)}, f32[1024,1408]{1,0:T(8,128)}, bf16[1024,1408]{1,0:T(8,128)(2,1)}, bf16[1024,2048]{1,0:T(8,128)(2,1)}) custom-call(bf16[2048,2816]{1,0:T(8,128)(2,1)} %all-gather.6.cloned.1.call-done.gate_w_ref.up_w_ref.weight_ref, bf16[2048,2816]{1,0:T(8,128)(2,1)} %all-gather.6.cloned.1.call-done.gate_w_ref.up_w_ref.weight_ref, ...), custom_call_target="tpu_custom_call" | custom-call | flops 11811160064 | bytes 37748736 | tf_op jit(solution)/shard_map/gate_up/pallas_call | solution.py:573
  239.0 12.6 %down_sums.1 = (bf16[1408,2048]{1,0:T(8,128)(2,1)}, bf16[1024,2048]{1,0:T(8,128)(2,1)}) custom-call(bf16[1024,1408]{1,0:T(8,128)(2,1)} %get-tuple-element.179.active_ref, bf16[256,2048]{1,0:T(8,128)(2,1)} %bitcast.217, bf16[128,2048]{1,0:T(8,128)(2,1)} %collective-permute-done.15.refs_1_, bf16[128,2048]{1,0:T(8,128)(2,1)} %collective-permute-done.36.refs_2_, ...), custom_call_target="tpu_custom_call" | custom-call | flops 5905580032 | bytes 18874368 | tf_op jit(solution)/shard_map/down_sums/pallas_call | solution.py:620
  251.7 29.1 %mlp_back.1 = (bf16[1024,2816]{1,0:T(8,128)(2,1)}, bf16[1024,2048]{1,0:T(8,128)(2,1)}) custom-call(bf16[1024,2048]{1,0:T(8,128)(2,1)} %get-tuple-element.184.top_ref, f32[1024,1408]{1,0:T(8,128)} %get-tuple-element.185.gate_ref, f32[1024,1408]{1,0:T(8,128)} %get-tuple-element.186.up_ref, bf16[1408,2048]{1,0:T(8,128)(2,1)} %all-gather.8.cloned.1.call-done.down_ref, ...), custom_call_target="tpu_custom_call" | custom-call | flops 17716740096 | bytes 41943040 | tf_op jit(solution)/shard_map/mlp_back/pallas_call | solution.py:675
  286.6 17.4 %convolution_convert_fusion = bf16[2048,2816]{1,0:T(8,128)(2,1)} fusion(bf16[1024,2048]{1,0:T(8,128)(2,1)S(1)} %copy-done.60, bf16[1024,2816]{1,0:T(8,128)(2,1)} %get-tuple-element.192), kind=kOutput, calls=%fused_computation | convolution fusion | flops 11816927232 | bytes 21495808 | tf_op jit(solution)/shard_map/dot_general | solution.py:32
  309.3 7.5 %collective-permute-done.41 = bf16[256,1024]{1,0:T(8,128)(2,1)S(1)} collective-permute-done((bf16[256,1024]{1,0:T(8,128)(2,1)S(1)}, bf16[256,1024]{1,0:T(8,128)(2,1)S(1)}, u32[]{:S(2)}, u32[]{:S(2)}) %collective-permute-start.41) | collective-permute-done | bytes 524320 | tf_op jit(solution)/shard_map/ppermute | solution.py:37
  326.5 8.4 %convolution_convert_fusion.2 = bf16[1024,2048]{1,0:T(8,128)(2,1)} fusion(bf16[1024,1408]{1,0:T(8,128)(2,1)S(1)} %copy-done.61, bf16[1408,2048]{1,0:T(8,128)(2,1)S(1)} %bitcast.245), kind=kOutput, calls=%fused_computation.7 | convolution fusion | flops 5907677184 | bytes 12845056 | tf_op jit(solution)/shard_map/dot_general | solution.py:24
  341.3 7.4 %collective-permute-done.44.refs_2_ = bf16[128,2048]{1,0:T(8,128)(2,1)S(1)} collective-permute-done((bf16[128,2048]{1,0:T(8,128)(2,1)S(1)}, bf16[128,2048]{1,0:T(8,128)(2,1)S(1)}, u32[]{:S(2)}, u32[]{:S(2)}) %collective-permute-start.44) | collective-permute-done | bytes 524320 | tf_op jit(solution)/shard_map/ppermute | solution.py:37
  349.7 5.6 %collective-permute-done.46.refs_5_ = bf16[128,2048]{1,0:T(8,128)(2,1)S(1)} collective-permute-done((bf16[128,2048]{1,0:T(8,128)(2,1)S(1)}, bf16[128,2048]{1,0:T(8,128)(2,1)S(1)}, u32[]{:S(2)}, u32[]{:S(2)}) %collective-permute-start.46) | collective-permute-done | bytes 524320 | tf_op jit(solution)/shard_map/ppermute | solution.py:37
  361.5 10.0 %out_back.1 = (bf16[1024,512]{1,0:T(8,128)(2,1)}, bf16[512,2048]{1,0:T(8,128)(2,1)}) custom-call(bf16[512,2048]{1,0:T(8,128)(2,1)} %bitcast.210, bf16[1024,512]{1,0:T(8,128)(2,1)} %get-tuple-element.152.attn_ref.out_ref, bf16[256,2048]{1,0:T(8,128)(2,1)} %copy-done.38, bf16[128,2048]{1,0:T(8,128)(2,1)} %copy-done.50, bf16[128,2048]{1,0:T(8,128)(2,1)} %copy-done.53, ...), custom_call_target="tpu_custom_call" | custom-call | flops 4294967296 | bytes 16777216 | tf_op jit(solution)/shard_map/out_back/pallas_call | solution.py:719
  378.5 27.4 %attend_back.1.grad_ref = bf16[1024,640]{1,0:T(8,128)(2,1)} custom-call(s32[8]{0:T(128)S(1)} %copy-done.9, bf16[1024,512]{1,0:T(8,128)(2,1)S(1)} %copy-done.12, bf16[1024,512]{1,0:T(8,128)(2,1)S(1)} %copy-done.16, bf16[1024,512]{1,0:T(8,128)(2,1)S(1)} %copy-done.11, f32[1024,128]{1,0:T(8,128)S(1)} %copy-done.13, f32[1024,128]{1,0:T(8,128)S(1)} %copy-done.7, ...), custom_call_target="tpu_custom_call" | custom-call | flops 5368709120 | bytes 8388608 | tf_op jit(solution)/shard_map/attend_back/pallas_call | solution.py:351
  405.9 5.6 %convolution_convert_fusion.1 = bf16[1024,2048]{1,0:T(8,128)(2,1)S(1)} fusion(bf16[1024,640]{1,0:T(8,128)(2,1)} %attend_back.1.grad_ref, bf16[2048,768]{1,0:T(8,128)(2,1)S(1)} %copy-done.33), kind=kOutput, calls=%fused_computation.6 | convolution fusion | flops 2686451712 | bytes 8126464 | tf_op jit(solution)/shard_map/dot_general | solution.py:28
  420.7 9.3 %attn_sums.1 = bf16[2048,1280]{1,0:T(8,128)(2,1)} custom-call(s32[1]{0:T(128)} %bitcast.33.me_ref, bf16[1024,2048]{1,0:T(8,128)(2,1)} %copy-done.24, bf16[1024,640]{1,0:T(8,128)(2,1)S(1)} %copy-done.1, bf16[2048,768]{1,0:T(8,128)(2,1)} %all-gather.4.cloned.1.call-done.weight_ref, f32[2048,128]{1,0:T(8,128)S(1)} %pad.9.slopes_ref, ...), custom_call_target="tpu_custom_call" | custom-call | flops 2684354560 | bytes 16777216 | tf_op jit(solution)/shard_map/attn_sums/pallas_call | solution.py:406
  452.2 8.3 %collective-permute-done.58 = bf16[256,1024]{1,0:T(8,128)(2,1)} collective-permute-done((bf16[256,1024]{1,0:T(8,128)(2,1)S(1)}, bf16[256,1024]{1,0:T(8,128)(2,1)}, u32[]{:S(2)}, u32[]{:S(2)}) %collective-permute-start.58) | collective-permute-done | bytes 524320 | tf_op jit(solution)/shard_map/ppermute | solution.py:37
  483.5 11.6 %reduce-scatter.6.cloned.1.call-done.joined_ref = bf16[256,1280]{1,0:T(8,128)(2,1)} async-done(((bf16[2048,1280]{1,0:T(8,128)(2,1)}), bf16[256,1280]{1,0:T(8,128)(2,1)}) %reduce-scatter.6.cloned.1.call-update) | async-done | bytes 655376 | tf_op jit(solution)/shard_map/reduce_scatter | solution.py:144
  (372 shorter events, 212.0 us)
Async XLA Ops:
  7.2 88.3 %all-gather.4.cloned.1.call-start = ((), (), s32[]{:S(2)}) async-start(), calls=%async_computation.3 | async-start | bytes 3538944 | tf_op jit(solution)/shard_map/all_gather | solution.py:140
  22.4 195.2 %all-gather.6.cloned.1.call-start = ((), (), s32[]{:S(2)}) async-start(), calls=%async_computation.4 | async-start | bytes 12976128 | tf_op jit(solution)/shard_map/all_gather | solution.py:140
  27.2 24.9 %collective-permute-start.4 = (bf16[128,2048]{1,0:T(8,128)(2,1)}, bf16[128,2048]{1,0:T(8,128)(2,1)}, u32[]{:S(2)}, u32[]{:S(2)}) collective-permute-start(bf16[128,2048]{1,0:T(8,128)(2,1)} %get-tuple-element.325), channel_id=1, source_target_pairs={{0,2},{1,3},{2,0},{3,1},{4,6},{5,7},{6,4},{7,5},{8,10},{9,11},{10,... | collective-permute-start | bytes 1572872 | tf_op jit(solution)/shard_map/ppermute | solution.py:37
  28.6 24.0 %collective-permute-start.3 = (bf16[128,2048]{1,0:T(8,128)(2,1)}, bf16[128,2048]{1,0:T(8,128)(2,1)}, u32[]{:S(2)}, u32[]{:S(2)}) collective-permute-start(bf16[128,2048]{1,0:T(8,128)(2,1)} %get-tuple-element.326), channel_id=1, source_target_pairs={{0,1},{1,0},{2,3},{3,2},{4,5},{5,4},{6,7},{7,6},{8,9},{9,8},{10,11... | collective-permute-start | bytes 1572872 | tf_op jit(solution)/shard_map/ppermute | solution.py:37
  52.6 199.0 %all-gather.8.cloned.1.call-start = ((), (), s32[]{:S(2)}) async-start(), calls=%async_computation.5 | async-start | bytes 6488064 | tf_op jit(solution)/shard_map/all_gather | solution.py:140
  53.0 39.1 %collective-permute-start.13 = (bf16[64,2048]{1,0:T(8,128)(2,1)S(1)}, bf16[64,2048]{1,0:T(8,128)(2,1)S(1)}, u32[]{:S(2)}, u32[]{:S(2)}) collective-permute-start(bf16[64,2048]{1,0:T(8,128)(2,1)S(1)} %copy-done.8), channel_id=1, source_target_pairs={{0,16},{4,20},{8,24},{12,28},{16,0},{20,4},{24,8},{28,12},{1,17},{... | collective-permute-start | bytes 786440 | tf_op jit(solution)/shard_map/ppermute | solution.py:37
  101.3 28.4 %collective-permute-start.23 = (bf16[128,2048]{1,0:T(8,128)(2,1)}, bf16[128,2048]{1,0:T(8,128)(2,1)S(1)}, u32[]{:S(2)}, u32[]{:S(2)}) collective-permute-start(bf16[128,2048]{1,0:T(8,128)(2,1)} %get-tuple-element.295), channel_id=1, source_target_pairs={{0,3},{1,2},{2,1},{3,0},{4,7},{5,6},{6,5},{7,4},{8,11},{9,10},{10,... | collective-permute-start | bytes 1572872 | tf_op jit(solution)/shard_map/ppermute | solution.py:37
  102.6 27.1 %collective-permute-start.22 = (bf16[128,2048]{1,0:T(8,128)(2,1)}, bf16[128,2048]{1,0:T(8,128)(2,1)S(1)}, u32[]{:S(2)}, u32[]{:S(2)}) collective-permute-start(bf16[128,2048]{1,0:T(8,128)(2,1)} %get-tuple-element.296), channel_id=1, source_target_pairs={{0,2},{1,3},{2,0},{3,1},{4,6},{5,7},{6,4},{7,5},{8,10},{9,11},{10,... | collective-permute-start | bytes 1572872 | tf_op jit(solution)/shard_map/ppermute | solution.py:37
  104.1 26.4 %collective-permute-start.21 = (bf16[128,2048]{1,0:T(8,128)(2,1)S(1)}, bf16[128,2048]{1,0:T(8,128)(2,1)S(1)}, u32[]{:S(2)}, u32[]{:S(2)}) collective-permute-start(bf16[128,2048]{1,0:T(8,128)(2,1)S(1)} %get-tuple-element.297), channel_id=1, source_target_pairs={{0,1},{1,0},{2,3},{3,2},{4,5},{5,4},{6,7},{7,6},{8,9},{9,8},{10,11... | collective-permute-start | bytes 1572872 | tf_op jit(solution)/shard_map/ppermute | solution.py:37
  137.4 24.1 %collective-permute-start.24 = (bf16[2,256,1024]{2,1,0:T(8,128)(2,1)S(1)}, bf16[2,256,1024]{2,1,0:T(8,128)(2,1)S(1)}, u32[]{:S(2)}, u32[]{:S(2)}) collective-permute-start(bf16[2,256,1024]{2,1,0:T(8,128)(2,1)S(1)} %pad_maximum_fusion.5), channel_id=1, source_target_pairs={{0,1},{1,0},{2,3},{3,2},{4,5},{5,4},{6,7},{7,6},{8,9},{9,8},{10,11... | collective-permute-start | bytes 3145736 | tf_op jit(solution)/shard_map/ppermute | solution.py:37
  138.8 24.0 %collective-permute-start.25 = (bf16[2,256,1024]{2,1,0:T(8,128)(2,1)S(1)}, bf16[2,256,1024]{2,1,0:T(8,128)(2,1)S(1)}, u32[]{:S(2)}, u32[]{:S(2)}) collective-permute-start(bf16[2,256,1024]{2,1,0:T(8,128)(2,1)S(1)} %pad_maximum_fusion.6), channel_id=1, source_target_pairs={{0,2},{1,3},{2,0},{3,1},{4,6},{5,7},{6,4},{7,5},{8,10},{9,11},{10,... | collective-permute-start | bytes 3145736 | tf_op jit(solution)/shard_map/ppermute | solution.py:37
  176.8 178.6 %reduce-scatter.4.cloned.1.call-start = ((), (), s32[]{:S(2)}) async-start(), calls=%async_computation.6 | async-start | bytes 6488064 | tf_op jit(solution)/shard_map/reduce_scatter | solution.py:144
  179.5 25.7 %collective-permute-start.29 = (bf16[128,2048]{1,0:T(8,128)(2,1)S(1)}, bf16[128,2048]{1,0:T(8,128)(2,1)S(1)}, u32[]{:S(2)}, u32[]{:S(2)}) collective-permute-start(bf16[128,2048]{1,0:T(8,128)(2,1)S(1)} %get-tuple-element.321), channel_id=1, source_target_pairs={{0,2},{1,3},{2,0},{3,1},{4,6},{5,7},{6,4},{7,5},{8,10},{9,11},{10,... | collective-permute-start | bytes 1572872 | tf_op jit(solution)/shard_map/ppermute | solution.py:37
  181.1 24.1 %collective-permute-start.28 = (bf16[128,2048]{1,0:T(8,128)(2,1)S(1)}, bf16[128,2048]{1,0:T(8,128)(2,1)S(1)}, u32[]{:S(2)}, u32[]{:S(2)}) collective-permute-start(bf16[128,2048]{1,0:T(8,128)(2,1)S(1)} %get-tuple-element.322), channel_id=1, source_target_pairs={{0,1},{1,0},{2,3},{3,2},{4,5},{5,4},{6,7},{7,6},{8,9},{9,8},{10,11... | collective-permute-start | bytes 1572872 | tf_op jit(solution)/shard_map/ppermute | solution.py:37
  213.3 25.7 %collective-permute-start.34 = (bf16[128,2048]{1,0:T(8,128)(2,1)}, bf16[128,2048]{1,0:T(8,128)(2,1)}, u32[]{:S(2)}, u32[]{:S(2)}) collective-permute-start(bf16[128,2048]{1,0:T(8,128)(2,1)} %collective-permute-done.15.refs_1_), channel_id=1, source_target_pairs={{0,2},{1,3},{2,0},{3,1},{4,6},{5,7},{6,4},{7,5},{8,10},{9,11},{10,... | collective-permute-start | bytes 1572872 | tf_op jit(solution)/shard_map/ppermute | solution.py:37
  213.7 25.3 %collective-permute-start.35 = (bf16[128,2048]{1,0:T(8,128)(2,1)}, bf16[128,2048]{1,0:T(8,128)(2,1)}, u32[]{:S(2)}, u32[]{:S(2)}) collective-permute-start(bf16[128,2048]{1,0:T(8,128)(2,1)} %collective-permute-done.16.refs_4_), channel_id=1, source_target_pairs={{0,1},{1,0},{2,3},{3,2},{4,5},{5,4},{6,7},{7,6},{8,9},{9,8},{10,11... | collective-permute-start | bytes 1572872 | tf_op jit(solution)/shard_map/ppermute | solution.py:37
  215.4 23.6 %collective-permute-start.37 = (bf16[128,2048]{1,0:T(8,128)(2,1)S(1)}, bf16[128,2048]{1,0:T(8,128)(2,1)}, u32[]{:S(2)}, u32[]{:S(2)}) collective-permute-start(bf16[128,2048]{1,0:T(8,128)(2,1)S(1)} %get-tuple-element.319), channel_id=1, source_target_pairs={{0,2},{1,3},{2,0},{3,1},{4,6},{5,7},{6,4},{7,5},{8,10},{9,11},{10,... | collective-permute-start | bytes 1572872 | tf_op jit(solution)/shard_map/ppermute | solution.py:37
  251.7 213.1 %reduce-scatter.8.cloned.1.call-start = ((), (), s32[]{:S(2)}) async-start(), calls=%async_computation.8 | async-start | bytes 12976128 | tf_op jit(solution)/shard_map/reduce_scatter | solution.py:144
  304.6 190.5 %reduce-scatter.6.cloned.1.call-start = ((), (), s32[]{:S(2)}) async-start(), calls=%async_computation.7 | async-start | bytes 5898240 | tf_op jit(solution)/shard_map/reduce_scatter | solution.py:144
  358.5 47.4 %collective-permute-start.48 = (bf16[2,256,1024]{2,1,0:T(8,128)(2,1)}, bf16[2,256,1024]{2,1,0:T(8,128)(2,1)S(1)}, u32[]{:S(2)}, u32[]{:S(2)}) collective-permute-start(bf16[2,256,1024]{2,1,0:T(8,128)(2,1)} %pad_maximum_fusion.9), channel_id=1, source_target_pairs={{0,1},{1,0},{2,3},{3,2},{4,5},{5,4},{6,7},{7,6},{8,9},{9,8},{10,11... | collective-permute-start | bytes 3145736 | tf_op jit(solution)/shard_map/ppermute | solution.py:37
  360.3 45.6 %collective-permute-start.49 = (bf16[2,256,1024]{2,1,0:T(8,128)(2,1)}, bf16[2,256,1024]{2,1,0:T(8,128)(2,1)}, u32[]{:S(2)}, u32[]{:S(2)}) collective-permute-start(bf16[2,256,1024]{2,1,0:T(8,128)(2,1)} %pad_maximum_fusion.10), channel_id=1, source_target_pairs={{0,2},{1,3},{2,0},{3,1},{4,6},{5,7},{6,4},{7,5},{8,10},{9,11},{10,... | collective-permute-start | bytes 3145736 | tf_op jit(solution)/shard_map/ppermute | solution.py:37
  373.6 32.3 %collective-permute-start.51 = (bf16[128,2048]{1,0:T(8,128)(2,1)S(1)}, bf16[128,2048]{1,0:T(8,128)(2,1)S(1)}, u32[]{:S(2)}, u32[]{:S(2)}) collective-permute-start(bf16[128,2048]{1,0:T(8,128)(2,1)S(1)} %bitcast.226), channel_id=1, source_target_pairs={{0,2},{1,3},{2,0},{3,1},{4,6},{5,7},{6,4},{7,5},{8,10},{9,11},{10,... | collective-permute-start | bytes 1572872 | tf_op jit(solution)/shard_map/ppermute | solution.py:37
  374.4 31.5 %collective-permute-start.52 = (bf16[128,2048]{1,0:T(8,128)(2,1)S(1)}, bf16[128,2048]{1,0:T(8,128)(2,1)S(1)}, u32[]{:S(2)}, u32[]{:S(2)}) collective-permute-start(bf16[128,2048]{1,0:T(8,128)(2,1)S(1)} %bitcast.225), channel_id=1, source_target_pairs={{0,3},{1,2},{2,1},{3,0},{4,7},{5,6},{6,5},{7,4},{8,11},{9,10},{10,... | collective-permute-start | bytes 1572872 | tf_op jit(solution)/shard_map/ppermute | solution.py:37
  375.8 30.1 %collective-permute-start.50 = (bf16[128,2048]{1,0:T(8,128)(2,1)S(1)}, bf16[128,2048]{1,0:T(8,128)(2,1)S(1)}, u32[]{:S(2)}, u32[]{:S(2)}) collective-permute-start(bf16[128,2048]{1,0:T(8,128)(2,1)S(1)} %bitcast.224), channel_id=1, source_target_pairs={{0,1},{1,0},{2,3},{3,2},{4,5},{5,4},{6,7},{7,6},{8,9},{9,8},{10,11... | collective-permute-start | bytes 1572872 | tf_op jit(solution)/shard_map/ppermute | solution.py:37
  (111 other events, 1211.6 us)
Sparse Core Ops, SparseCore 0:
  22.5 47.1 all-gather.3
  71.9 107.4 all-gather.5
  181.1 58.7 all-gather.7
  251.8 62.9 reduce-scatter.3
  316.9 117.6 reduce-scatter.7
  436.8 58.2 reduce-scatter.5
